TPU v7x, 256 devices: a whole 4x4x8 slice. The times are simulated.
256 devices in a mesh: seq: 64 (over z, x, core), mp: 4 (over y).
Axes of the slice: x: 4, y: 4, z: 8, core: 2. Of those that a mesh axis runs over, the one named last changes fastest.
Arguments:
- queries: bfloat16 [65536, 1024], P('seq', 'mp'), may hold values from -8 to 8
- byte_keys: bfloat16 [65536, 1024], P('seq', 'mp'), may hold values from -8 to 8
- byte_values: bfloat16 [65536, 1024], P('seq', 'mp'), may hold values from -6 to 6
- w_query: bfloat16 [1024, 1024], P(None, 'mp'), may hold values from -0.1875 to 0.1875
- w_key: bfloat16 [1024, 1024], P(None, 'mp'), may hold values from -0.1875 to 0.1875
- w_value: bfloat16 [1024, 1024], P(None, 'mp'), may hold values from -0.1875 to 0.1875
- w_out: bfloat16 [1024, 1024], P('mp'), may hold values from -0.1875 to 0.1875
- d_output: bfloat16 [65536, 1024], P('seq'), may hold values from -96 to 96
- patch_index: int32 [65536], P('seq'), may hold values from 0 to 16383, as said below
- unpatch: bfloat16 [1024, 4096], P(None, 'mp'), may hold values from -0.09375 to 0.09375
Outputs:
- d_patch: bfloat16 [16384, 4096], P('seq', 'mp')
Inputs may be any that keep to these rules, and one draw needn't show every extreme that they name: patch_index never falls and every one of the 16384 patches covers one or more bytes; patch 0 starts at byte 0, and for every k from 1 to 64 - 1 the first byte of patch k * 256 lies 1 to 128 bytes after byte k * 1024, the latter distance reached.
All inputs are finite; a program needn't handle non-finite values.
Results may differ from a plain program's by a relative error of at most 0.025.
Values may be sent and summed in bfloat16 or wider, within the bound.
No kernel may reach another device: no remote copies, remote signals or barrier semaphores. Data moves between devices by JAX's collectives and lax.ppermute only.
A program may use at most 128 MiB of HBM per device.

v0:
```python
import jax
import jax.numpy as jnp
from jax import lax
from jax.sharding import PartitionSpec as P

HS = 64
WINDOW = 512
PATCH_DEV = 256


def passed_along(value, axis, steps):
    count = lax.axis_size(axis)
    leading, last = (max(0, -steps), min(count, count - steps))
    return lax.ppermute(value, axis, [(source, source + steps) for source in range(leading, last)])


def block_grads(query_block, grad_block, key_block, value_block, keep_first):
    block_rows = query_block.shape[0]
    head_count = query_block.shape[1] // HS
    factor = HS ** (-0.5)
    query_heads = query_block.reshape(block_rows, head_count, HS)
    grad_heads = grad_block.reshape(block_rows, head_count, HS)
    key_heads = key_block.reshape(2 * block_rows, head_count, HS)
    value_heads = value_block.reshape(2 * block_rows, head_count, HS)
    scores = (
        jnp.einsum("ihd,jhd->hij", query_heads, key_heads, preferred_element_type=jnp.float32)
        * factor
    )
    query_pos = jnp.arange(block_rows, dtype=jnp.int32)[:, None]
    key_pos = jnp.arange(2 * block_rows, dtype=jnp.int32)[None, :]
    allowed = (
        (key_pos > query_pos)
        & (key_pos <= query_pos + block_rows)
        & ((key_pos >= block_rows) | keep_first)
    )
    scores = jnp.where(allowed[None], scores, -1e30)
    peak = jnp.max(scores, axis=-1, keepdims=True)
    raised = jnp.exp(scores - peak)
    attend = raised / jnp.sum(raised, axis=-1, keepdims=True)
    d_attend = jnp.einsum(
        "ihd,jhd->hij", grad_heads, value_heads, preferred_element_type=jnp.float32
    )
    row_dot = jnp.sum(attend * d_attend, axis=-1, keepdims=True)
    d_scores = (attend * (d_attend - row_dot)).astype(jnp.bfloat16)
    attend_low = attend.astype(jnp.bfloat16)
    d_query = (
        jnp.einsum("hij,jhd->ihd", d_scores, key_heads, preferred_element_type=jnp.float32) * factor
    )
    d_key = (
        jnp.einsum("hij,ihd->jhd", d_scores, query_heads, preferred_element_type=jnp.float32)
        * factor
    )
    d_value = jnp.einsum("hij,ihd->jhd", attend_low, grad_heads, preferred_element_type=jnp.float32)
    return (
        d_query.reshape(block_rows, -1),
        d_key.reshape(2 * block_rows, -1),
        d_value.reshape(2 * block_rows, -1),
    )


def spread(parts, width):
    leading = parts[:, :WINDOW].reshape(-1, width)
    trailing = parts[:, WINDOW:].reshape(-1, width)
    blank_rows = jnp.zeros((WINDOW, width), jnp.float32)
    return jnp.concatenate([leading, blank_rows], 0) + jnp.concatenate([blank_rows, trailing], 0)


def on_device(
    queries, byte_keys, byte_values, w_query, w_key, w_value, w_out, d_output, patch_index, unpatch
):
    byte_count = queries.shape[0]
    width = queries.shape[1]
    shard = lax.axis_index("seq")
    grad_all = jnp.dot(d_output, w_out.T, preferred_element_type=jnp.float32).astype(jnp.bfloat16)
    tail_keys, tail_values = passed_along(
        (byte_keys[byte_count - WINDOW :], byte_values[byte_count - WINDOW :]), "seq", 1
    )
    ext_keys = jnp.concatenate([tail_keys, byte_keys], 0)
    ext_values = jnp.concatenate([tail_values, byte_values], 0)

    def one_block(block_id):
        offset = block_id * WINDOW
        return block_grads(
            lax.dynamic_slice_in_dim(queries, offset, WINDOW, 0),
            lax.dynamic_slice_in_dim(grad_all, offset, WINDOW, 0),
            lax.dynamic_slice_in_dim(ext_keys, offset, 2 * WINDOW, 0),
            lax.dynamic_slice_in_dim(ext_values, offset, 2 * WINDOW, 0),
            (block_id > 0) | (shard > 0),
        )

    d_query, key_parts, value_parts = lax.map(
        one_block, jnp.arange(byte_count // WINDOW, dtype=jnp.int32)
    )
    d_query_low = d_query.reshape(byte_count, width).astype(jnp.bfloat16)
    key_ext = spread(key_parts, width)
    value_ext = spread(value_parts, width)
    own_keys = key_ext[WINDOW:]
    own_values = value_ext[WINDOW:]
    head_rows = byte_count - WINDOW
    cross = PATCH_DEV
    local_slot = patch_index - shard * PATCH_DEV + cross
    slots = PATCH_DEV + cross
    next_keys, next_values = (
        passed_along(key_ext[:WINDOW].astype(jnp.bfloat16), "seq", -1).astype(jnp.float32),
        passed_along(value_ext[:WINDOW].astype(jnp.bfloat16), "seq", -1).astype(jnp.float32),
    )
    full_keys = jnp.concatenate([own_keys[:head_rows], own_keys[head_rows:] + next_keys], 0).astype(
        jnp.bfloat16
    )
    full_values = jnp.concatenate(
        [own_values[:head_rows], own_values[head_rows:] + next_values], 0
    ).astype(jnp.bfloat16)
    byte_grad = (
        jnp.dot(d_query_low, w_query.T, preferred_element_type=jnp.float32)
        + jnp.dot(full_keys, w_key.T, preferred_element_type=jnp.float32)
        + jnp.dot(full_values, w_value.T, preferred_element_type=jnp.float32)
    )
    frame = jax.ops.segment_sum(byte_grad, local_slot, num_segments=slots)
    from_next = passed_along(frame[:cross].astype(jnp.bfloat16), "seq", -1).astype(jnp.float32)
    owned = frame[cross:] + from_next
    patch_low = lax.psum(owned.astype(jnp.bfloat16), "mp")
    return jnp.dot(patch_low, unpatch, preferred_element_type=jnp.float32).astype(jnp.bfloat16)


def solution(mesh):
    in_specs = (
        P("seq", "mp"),
        P("seq", "mp"),
        P("seq", "mp"),
        P(None, "mp"),
        P(None, "mp"),
        P(None, "mp"),
        P("mp", None),
        P("seq", None),
        P("seq"),
        P(None, "mp"),
    )
    out_specs = P("seq", "mp")
    return jax.shard_map(
        on_device, mesh=mesh, in_specs=in_specs, out_specs=out_specs, check_vma=False
    )
```

profile of v0, /device:TPU:103, one launch (start us, length us, event | category | flops | bytes accessed | tf_op | source)
XLA Modules:
  0.0 191.6 jit_solution(15170219140943731336)
XLA Ops:
  6.5 1.4 copy.17
  8.8 5.2 %collective-permute-start = (bf16[512,256]{0,1:T(8,128)(2,1)}, bf16[512,256]{0,1:T(8,128)(2,1)}, u32[]{:S(2)}, u32[]{:S(2)}) collective-permute-start(bf16[512,256]{0,1:T(8,128)(2,1)} %slice.67), channel_id=1, source_target_pairs={{0,4},{4,8},{8,12},{12,16},{16,20},{20,24},{24,28},{28,32},{32,36}... | collective-permute-start | bytes 786440 | tf_op jit(solution)/shard_map/ppermute | solution.py:14
  14.1 1.2 copy.19
  15.3 1.9 %collective-permute-start.1 = (bf16[512,256]{0,1:T(8,128)(2,1)S(1)}, bf16[512,256]{0,1:T(8,128)(2,1)}, u32[]{:S(2)}, u32[]{:S(2)}) collective-permute-start(bf16[512,256]{0,1:T(8,128)(2,1)S(1)} %slice.68), channel_id=1, source_target_pairs={{0,4},{4,8},{8,12},{12,16},{16,20},{20,24},{24,28},{28,32},{32,36}... | collective-permute-start | bytes 786440 | tf_op jit(solution)/shard_map/ppermute | solution.py:14
  17.3 1.8 convolution_convert_fusion.1
  19.7 1.2 pad_maximum_fusion
  20.9 1.2 pad_maximum_fusion.1
  22.0 64.1 %while.16 = (s32[]{:T(128)}, bf16[2,512,256]{2,1,0:T(8,128)(2,1)}, f32[2,1024,256]{2,1,0:T(8,128)}, f32[2,1024,256]{2,1,0:T(8,128)}, s32[2]{0:T(128)S(1)}, /*ind...) while((s32[]{:T(128)}, bf16[2,512,256]{2,1,0:T(8,128)(2,1)}, ...), condition=%wide.region_4.5_spmd, body=%wide.region_0.4_spmd.sunk | while | flops 1372063232 | bytes 162323568 | solution.py:91
  23.5 1.0 constant_dynamic-slice_fusion.9
  25.8 5.4 %fusion.88 = (f32[4,512]{1,0:T(4,128)S(1)}, f32[4,512,1024]{2,1,0:T(8,128)}) fusion(pred[512,1024]{1,0:T(8,128)(4,1)S(1)} %fusion.87, bf16[512,4,64]{0,2,1:T(8,128)(2,1)S(1)} %bitcast.80, bf16[1024,4,64]{0,2,1:T(8,128)(2,1)S(1)} %bitcast.78), kind=kOutput, calls=%fused_computation.68.clone.1 | convolution fusion | flops 276825088 | bytes 9707520 | tf_op jit(solution)/shard_map/while/body/eval_jaxpr/sub | solution.py:38
  31.5 4.7 %multiply_reduce_fusion.2 = (f32[4,512]{1,0:T(4,128)S(1)}, f32[4,512,1024]{2,1,0:T(8,128)S(1)}) fusion(f32[4,512,1024]{2,1,0:T(8,128)} %get-tuple-element.249, f32[4,512]{1,0:T(4,128)S(1)} %get-tuple-element.250, bf16[512,4,64]{0,2,1:T(8,128)(2,1)S(1)} %bitcast.93, bf16[1024,4,64]{0,2,1:T(8,128)(2,1)S(1)} %bitcast.84), kind=kOutput, calls=%fused_computation.3.clone.1 | convolution fusion | flops 274724864 | bytes 17580032 | tf_op jit(solution)/shard_map/while/body/eval_jaxpr/ihd,jhd->hij/dot_general | solution.py:40
  36.2 1.2 slice-done.1
  37.4 1.3 multiply_convert_fusion.2
  38.7 2.0 %copy-done.2 = bf16[4,512,1024]{2,1,0:T(8,128)(2,1)} copy-done((bf16[4,512,1024]{2,1,0:T(8,128)(2,1)}, bf16[4,512,1024]{2,1,0:T(8,128)(2,1)S(1)}, u32[]{:S(2)}) %copy-start.2) | copy-done | bytes 4194328 | tf_op jit(solution)/shard_map/while
  40.7 0.9 convolution_multiply_fusion.5
  41.9 5.3 %fusion.89 = f32[4,64,1024]{2,1,0:T(8,128)} fusion(bf16[512,4,64]{0,2,1:T(8,128)(2,1)S(1)} %bitcast.94, f32[4,512,1024]{2,1,0:T(8,128)} %get-tuple-element.249, f32[4,512]{1,0:T(4,128)S(1)} %get-tuple-element.250), kind=kOutput, calls=%fused_computation.7.clone.1 | convolution fusion | flops 272629760 | bytes 9707520 | tf_op jit(solution)/shard_map/while/body/eval_jaxpr/hij,ihd->jhd/dot_general | solution.py:53
  47.2 1.6 copy.48
  48.8 1.5 constant_dynamic-update-slice_fusion.6
  50.3 1.4 copy-done.3
  51.7 1.4 convolution_multiply_fusion.4
  53.3 0.8 copy-done.16
  55.5 1.0 constant_dynamic-slice_fusion.9
  57.9 5.4 %fusion.88 = (f32[4,512]{1,0:T(4,128)S(1)}, f32[4,512,1024]{2,1,0:T(8,128)}) fusion(pred[512,1024]{1,0:T(8,128)(4,1)S(1)} %fusion.87, bf16[512,4,64]{0,2,1:T(8,128)(2,1)S(1)} %bitcast.80, bf16[1024,4,64]{0,2,1:T(8,128)(2,1)S(1)} %bitcast.78), kind=kOutput, calls=%fused_computation.68.clone.1 | convolution fusion | flops 276825088 | bytes 9707520 | tf_op jit(solution)/shard_map/while/body/eval_jaxpr/sub | solution.py:38
  63.5 4.7 %multiply_reduce_fusion.2 = (f32[4,512]{1,0:T(4,128)S(1)}, f32[4,512,1024]{2,1,0:T(8,128)S(1)}) fusion(f32[4,512,1024]{2,1,0:T(8,128)} %get-tuple-element.249, f32[4,512]{1,0:T(4,128)S(1)} %get-tuple-element.250, bf16[512,4,64]{0,2,1:T(8,128)(2,1)S(1)} %bitcast.93, bf16[1024,4,64]{0,2,1:T(8,128)(2,1)S(1)} %bitcast.84), kind=kOutput, calls=%fused_computation.3.clone.1 | convolution fusion | flops 274724864 | bytes 17580032 | tf_op jit(solution)/shard_map/while/body/eval_jaxpr/ihd,jhd->hij/dot_general | solution.py:40
  68.2 1.2 slice-done.1
  69.4 1.3 multiply_convert_fusion.2
  70.8 2.0 %copy-done.2 = bf16[4,512,1024]{2,1,0:T(8,128)(2,1)} copy-done((bf16[4,512,1024]{2,1,0:T(8,128)(2,1)}, bf16[4,512,1024]{2,1,0:T(8,128)(2,1)S(1)}, u32[]{:S(2)}) %copy-start.2) | copy-done | bytes 4194328 | tf_op jit(solution)/shard_map/while
  72.7 0.9 convolution_multiply_fusion.5
  73.9 5.3 %fusion.89 = f32[4,64,1024]{2,1,0:T(8,128)} fusion(bf16[512,4,64]{0,2,1:T(8,128)(2,1)S(1)} %bitcast.94, f32[4,512,1024]{2,1,0:T(8,128)} %get-tuple-element.249, f32[4,512]{1,0:T(4,128)S(1)} %get-tuple-element.250), kind=kOutput, calls=%fused_computation.7.clone.1 | convolution fusion | flops 272629760 | bytes 9707520 | tf_op jit(solution)/shard_map/while/body/eval_jaxpr/hij,ihd->jhd/dot_general | solution.py:53
  79.2 1.6 copy.48
  80.8 1.5 constant_dynamic-update-slice_fusion.6
  82.3 1.5 copy-done.3
  83.7 1.4 convolution_multiply_fusion.4
  85.3 0.8 copy-done.16
  86.1 2.6 %fusion.38 = (f32[2,512,256]{2,1,0:T(8,128)S(1)}, f32[2,512,256]{2,1,0:T(8,128)S(1)}, f32[2,512,256]{2,1,0:T(8,128)S(1)}, f32[2,512,256]{2,1,0:T(8,128)S(1)}) fusion(f32[2,1024,256]{2,1,0:T(8,128)} %get-tuple-element.124, f32[2,1024,256]{2,1,0:T(8,128)} %get-tuple-element.125), kind=kLoop, calls=%fused_computation.69 | loop fusion | bytes 8388608 | tf_op jit(solution)/shard_map/slice | solution.py:63
  88.9 2.5 %collective-permute-start.2 = (bf16[512,256]{1,0:T(8,128)(2,1)S(1)}, bf16[512,256]{1,0:T(8,128)(2,1)S(1)}, u32[]{:S(2)}, u32[]{:S(2)}) collective-permute-start(bf16[512,256]{1,0:T(8,128)(2,1)S(1)} %get-tuple-element.177), channel_id=1, source_target_pairs={{4,0},{8,4},{12,8},{16,12},{20,16},{24,20},{28,24},{32,28},{36,32}... | collective-permute-start | bytes 786440 | tf_op jit(solution)/shard_map/ppermute | solution.py:14
  91.7 2.2 %collective-permute-start.3 = (bf16[512,256]{1,0:T(8,128)(2,1)S(1)}, bf16[512,256]{1,0:T(8,128)(2,1)S(1)}, u32[]{:S(2)}, u32[]{:S(2)}) collective-permute-start(bf16[512,256]{1,0:T(8,128)(2,1)S(1)} %get-tuple-element.179), channel_id=1, source_target_pairs={{4,0},{8,4},{12,8},{16,12},{20,16},{24,20},{28,24},{32,28},{36,32}... | collective-permute-start | bytes 786440 | tf_op jit(solution)/shard_map/ppermute | solution.py:14
  93.9 2.7 %fusion.42 = f32[1024,1024]{1,0:T(8,128)} fusion(bf16[1024,256]{1,0:T(8,128)(2,1)S(1)} %bitcast.95, bf16[1024,256]{1,0:T(8,128)(2,1)S(1)} %copy-done.12), kind=kOutput, calls=%fused_computation.73 | convolution fusion | flops 536870912 | bytes 5242880 | tf_op jit(solution)/shard_map/dot_general | solution.py:114
  96.7 4.0 %collective-permute-done.2 = bf16[512,256]{1,0:T(8,128)(2,1)S(1)} collective-permute-done((bf16[512,256]{1,0:T(8,128)(2,1)S(1)}, bf16[512,256]{1,0:T(8,128)(2,1)S(1)}, u32[]{:S(2)}, u32[]{:S(2)}) %collective-permute-start.2) | collective-permute-done | bytes 262176 | tf_op jit(solution)/shard_map/ppermute | solution.py:14
  100.7 2.7 %fusion.27 = f32[1024,1024]{1,0:T(8,128)} fusion(bf16[1024,256]{1,0:T(8,128)(2,1)S(1)} %copy-done.13, bf16[512,256]{1,0:T(8,128)(2,1)S(1)} %fusion.23, bf16[512,256]{1,0:T(8,128)(2,1)S(1)} %get-tuple-element.176), kind=kOutput, calls=%fused_computation.57 | convolution fusion | flops 537919488 | bytes 5242880 | tf_op jit(solution)/shard_map/dot_general | solution.py:115
  103.5 2.7 %fusion.31 = f32[1024,1024]{1,0:T(8,128)} fusion(bf16[1024,256]{1,0:T(8,128)(2,1)S(1)} %copy-done.14, bf16[512,256]{1,0:T(8,128)(2,1)S(1)} %fusion.26, bf16[512,256]{1,0:T(8,128)(2,1)S(1)} %get-tuple-element.178), kind=kOutput, calls=%fused_computation.61 | convolution fusion | flops 537919488 | bytes 5242880 | tf_op jit(solution)/shard_map/dot_general | solution.py:116
  106.2 13.2 %scatter_custom_fusion = f32[512,1024]{1,0:T(8,128)} fusion(s32[1024]{0:T(1024)} %subtract_add_fusion, f32[1024,1024]{1,0:T(8,128)} %fusion.31, f32[1024,1024]{1,0:T(8,128)} %fusion.42, f32[1024,1024]{1,0:T(8,128)} %fusion.27, f32[]{:T(128)} %constant.66.clone.1), kind=kCustom, calls=%fused_computation.32 | custom fusion | flops 3145728 | bytes 14680576 | tf_op jit(solution)/shard_map/scatter-add | solution.py:118
  119.4 1.3 slice.103
  120.7 1.9 %collective-permute-start.4 = (bf16[256,1024]{1,0:T(8,128)(2,1)S(1)}, bf16[256,1024]{1,0:T(8,128)(2,1)S(1)}, u32[]{:S(2)}, u32[]{:S(2)}) collective-permute-start(bf16[256,1024]{1,0:T(8,128)(2,1)S(1)} %slice.103), channel_id=1, source_target_pairs={{4,0},{8,4},{12,8},{16,12},{20,16},{24,20},{28,24},{32,28},{36,32}... | collective-permute-start | bytes 1572872 | tf_op jit(solution)/shard_map/ppermute | solution.py:14
  122.6 11.9 %collective-permute-done.4 = bf16[256,1024]{1,0:T(8,128)(2,1)S(1)} collective-permute-done((bf16[256,1024]{1,0:T(8,128)(2,1)S(1)}, bf16[256,1024]{1,0:T(8,128)(2,1)S(1)}, u32[]{:S(2)}, u32[]{:S(2)}) %collective-permute-start.4) | collective-permute-done | bytes 524320 | tf_op jit(solution)/shard_map/ppermute | solution.py:14
  134.5 2.2 %fusion.19 = bf16[256,1024]{1,0:T(8,128)(2,1)} fusion(f32[512,1024]{1,0:T(8,128)} %scatter_custom_fusion, bf16[256,1024]{1,0:T(8,128)(2,1)S(1)} %collective-permute-done.4), kind=kLoop, calls=%fused_computation.47 | loop fusion | flops 786432 | bytes 2097152 | tf_op jit(solution)/shard_map/convert_element_type | solution.py:121
  136.7 44.7 %all-reduce.6.cloned.1.call-done = bf16[256,1024]{1,0:T(8,128)(2,1)} async-done(((bf16[256,1024]{1,0:T(8,128)(2,1)}), bf16[256,1024]{1,0:T(8,128)(2,1)}) %all-reduce.6.cloned.1.call-update) | async-done | bytes 524304 | tf_op jit(solution)/shard_map/psum | solution.py:121
  181.4 3.3 %convolution_convert_fusion = bf16[256,1024]{1,0:T(8,128)(2,1)} fusion(bf16[256,1024]{1,0:T(8,128)(2,1)} %all-reduce.6.cloned.1.call-done, bf16[1024,1024]{1,0:T(8,128)(2,1)} %param.21), kind=kOutput, calls=%fused_computation.43 | convolution fusion | flops 537133056 | bytes 3145728 | tf_op jit(solution)/shard_map/dot_general | solution.py:122
  (102 shorter events, 6.3 us)
Async XLA Ops:
  6.5 10.7 %copy-start = (bf16[1024,1024]{1,0:T(8,128)(2,1)S(1)}, bf16[1024,1024]{1,0:T(8,128)(2,1)}, u32[]{:S(2)}) copy-start(bf16[1024,1024]{1,0:T(8,128)(2,1)} %param.19) | copy-start | bytes 6291460
  6.5 174.9 %all-reduce.6.cloned.1.call-start = ((), (), s32[]{:S(2)}) async-start(), calls=%async_computation | async-start | bytes 1048576 | tf_op jit(solution)/shard_map/psum | solution.py:121
  7.9 0.9 copy-start.11
  7.9 11.1 %copy-start.18 = (s32[1024]{0:T(1024)S(1)}, s32[1024]{0:T(1024)}, u32[]{:S(2)}) copy-start(s32[1024]{0:T(1024)} %param.20) | copy-start | bytes 12292
  8.8 10.9 %collective-permute-start = (bf16[512,256]{0,1:T(8,128)(2,1)}, bf16[512,256]{0,1:T(8,128)(2,1)}, u32[]{:S(2)}, u32[]{:S(2)}) collective-permute-start(bf16[512,256]{0,1:T(8,128)(2,1)} %slice.67), channel_id=1, source_target_pairs={{0,4},{4,8},{8,12},{12,16},{16,20},{20,24},{24,28},{28,32},{32,36}... | collective-permute-start | bytes 786440 | tf_op jit(solution)/shard_map/ppermute | solution.py:14
  15.3 5.5 %copy-start.10 = (bf16[1024,256]{0,1:T(8,128)(2,1)}, bf16[1024,256]{0,1:T(8,128)(2,1)S(1)}, u32[]{:S(2)}) copy-start(bf16[1024,256]{0,1:T(8,128)(2,1)S(1)} %copy.19) | copy-start | bytes 1572868
  15.3 5.5 %collective-permute-start.1 = (bf16[512,256]{0,1:T(8,128)(2,1)S(1)}, bf16[512,256]{0,1:T(8,128)(2,1)}, u32[]{:S(2)}, u32[]{:S(2)}) collective-permute-start(bf16[512,256]{0,1:T(8,128)(2,1)S(1)} %slice.68), channel_id=1, source_target_pairs={{0,4},{4,8},{8,12},{12,16},{16,20},{20,24},{24,28},{28,32},{32,36}... | collective-permute-start | bytes 786440 | tf_op jit(solution)/shard_map/ppermute | solution.py:14
  22.1 9.1 %copy-start.4 = (bf16[1536,256]{0,1:T(8,128)(2,1)}, bf16[1536,256]{0,1:T(8,128)(2,1)S(1)}, u32[]{:S(2)}) copy-start(bf16[1536,256]{0,1:T(8,128)(2,1)S(1)} %get-tuple-element.292) | copy-start | bytes 2359300 | tf_op jit(solution)/shard_map/while
  22.1 9.1 %copy-start.8 = (bf16[1024,256]{1,0:T(8,128)(2,1)}, bf16[1024,256]{1,0:T(8,128)(2,1)S(1)}, u32[]{:S(2)}) copy-start(bf16[1024,256]{1,0:T(8,128)(2,1)S(1)} %get-tuple-element.295) | copy-start | bytes 1572868 | tf_op jit(solution)/shard_map/while
  22.1 9.3 %copy-start.6 = (bf16[1536,256]{0,1:T(8,128)(2,1)}, bf16[1536,256]{0,1:T(8,128)(2,1)S(1)}, u32[]{:S(2)}) copy-start(bf16[1536,256]{0,1:T(8,128)(2,1)S(1)} %get-tuple-element.296) | copy-start | bytes 2359300 | tf_op jit(solution)/shard_map/while
  31.4 4.8 %slice-start = ((s8[8388608]{0:T(1024)(128)(4,1)}), s8[4194304]{0:T(1024)(128)(4,1)S(1)}, s32[]{:S(2)}) async-start(s8[8388608]{0:T(1024)(128)(4,1)} %bitcast.75), calls=%async_computation.1 | async-start | bytes 8388608 | tf_op jit(solution)/shard_map/while
  31.4 5.9 %slice-start.1 = ((s8[8388608]{0:T(1024)(128)(4,1)}), s8[4194304]{0:T(1024)(128)(4,1)S(1)}, s32[]{:S(2)}) async-start(s8[8388608]{0:T(1024)(128)(4,1)} %bitcast.75), calls=%async_computation.2 | async-start | bytes 8388608 | tf_op jit(solution)/shard_map/while
  38.7 2.0 %copy-start.2 = (bf16[4,512,1024]{2,1,0:T(8,128)(2,1)}, bf16[4,512,1024]{2,1,0:T(8,128)(2,1)S(1)}, u32[]{:S(2)}) copy-start(bf16[4,512,1024]{2,1,0:T(8,128)(2,1)S(1)} %multiply_convert_fusion.2) | copy-start | bytes 12582916 | tf_op jit(solution)/shard_map/while
  48.8 2.9 %copy-start.3 = (bf16[4,512,1024]{2,1,0:T(8,128)(2,1)S(1)}, bf16[4,512,1024]{2,1,0:T(8,128)(2,1)}, u32[]{:S(2)}) copy-start(bf16[4,512,1024]{2,1,0:T(8,128)(2,1)} %copy-done.2) | copy-start | bytes 12582916 | tf_op jit(solution)/shard_map/while
  48.8 4.5 %copy-start.15 = (bf16[2,512,256]{2,1,0:T(8,128)(2,1)S(1)}, bf16[2,512,256]{2,1,0:T(8,128)(2,1)}, u32[]{:S(2)}) copy-start(bf16[2,512,256]{2,1,0:T(8,128)(2,1)} %get-tuple-element.272) | copy-start | bytes 1572868 | tf_op jit(solution)/shard_map/while
  50.3 3.8 %copy-start.5 = (bf16[1536,256]{0,1:T(8,128)(2,1)S(1)}, bf16[1536,256]{0,1:T(8,128)(2,1)}, u32[]{:S(2)}) copy-start(bf16[1536,256]{0,1:T(8,128)(2,1)} %copy-done.4) | copy-start | bytes 2359300 | tf_op jit(solution)/shard_map/while
  50.3 3.8 %copy-start.7 = (bf16[1536,256]{0,1:T(8,128)(2,1)S(1)}, bf16[1536,256]{0,1:T(8,128)(2,1)}, u32[]{:S(2)}) copy-start(bf16[1536,256]{0,1:T(8,128)(2,1)} %copy-done.6) | copy-start | bytes 2359300 | tf_op jit(solution)/shard_map/while
  50.3 3.8 %copy-start.9 = (bf16[1024,256]{1,0:T(8,128)(2,1)S(1)}, bf16[1024,256]{1,0:T(8,128)(2,1)}, u32[]{:S(2)}) copy-start(bf16[1024,256]{1,0:T(8,128)(2,1)} %copy-done.8) | copy-start | bytes 1572868 | tf_op jit(solution)/shard_map/while
  53.3 0.8 copy-start.16
  54.1 9.1 %copy-start.4 = (bf16[1536,256]{0,1:T(8,128)(2,1)}, bf16[1536,256]{0,1:T(8,128)(2,1)S(1)}, u32[]{:S(2)}) copy-start(bf16[1536,256]{0,1:T(8,128)(2,1)S(1)} %get-tuple-element.292) | copy-start | bytes 2359300 | tf_op jit(solution)/shard_map/while
  54.1 9.1 %copy-start.8 = (bf16[1024,256]{1,0:T(8,128)(2,1)}, bf16[1024,256]{1,0:T(8,128)(2,1)S(1)}, u32[]{:S(2)}) copy-start(bf16[1024,256]{1,0:T(8,128)(2,1)S(1)} %get-tuple-element.295) | copy-start | bytes 1572868 | tf_op jit(solution)/shard_map/while
  54.1 9.3 %copy-start.6 = (bf16[1536,256]{0,1:T(8,128)(2,1)}, bf16[1536,256]{0,1:T(8,128)(2,1)S(1)}, u32[]{:S(2)}) copy-start(bf16[1536,256]{0,1:T(8,128)(2,1)S(1)} %get-tuple-element.296) | copy-start | bytes 2359300 | tf_op jit(solution)/shard_map/while
  63.5 4.8 %slice-start = ((s8[8388608]{0:T(1024)(128)(4,1)}), s8[4194304]{0:T(1024)(128)(4,1)S(1)}, s32[]{:S(2)}) async-start(s8[8388608]{0:T(1024)(128)(4,1)} %bitcast.75), calls=%async_computation.1 | async-start | bytes 8388608 | tf_op jit(solution)/shard_map/while
  63.5 5.9 %slice-start.1 = ((s8[8388608]{0:T(1024)(128)(4,1)}), s8[4194304]{0:T(1024)(128)(4,1)S(1)}, s32[]{:S(2)}) async-start(s8[8388608]{0:T(1024)(128)(4,1)} %bitcast.75), calls=%async_computation.2 | async-start | bytes 8388608 | tf_op jit(solution)/shard_map/while
  70.8 2.0 %copy-start.2 = (bf16[4,512,1024]{2,1,0:T(8,128)(2,1)}, bf16[4,512,1024]{2,1,0:T(8,128)(2,1)S(1)}, u32[]{:S(2)}) copy-start(bf16[4,512,1024]{2,1,0:T(8,128)(2,1)S(1)} %multiply_convert_fusion.2) | copy-start | bytes 12582916 | tf_op jit(solution)/shard_map/while
  80.8 2.9 %copy-start.3 = (bf16[4,512,1024]{2,1,0:T(8,128)(2,1)S(1)}, bf16[4,512,1024]{2,1,0:T(8,128)(2,1)}, u32[]{:S(2)}) copy-start(bf16[4,512,1024]{2,1,0:T(8,128)(2,1)} %copy-done.2) | copy-start | bytes 12582916 | tf_op jit(solution)/shard_map/while
  80.8 4.5 %copy-start.15 = (bf16[2,512,256]{2,1,0:T(8,128)(2,1)S(1)}, bf16[2,512,256]{2,1,0:T(8,128)(2,1)}, u32[]{:S(2)}) copy-start(bf16[2,512,256]{2,1,0:T(8,128)(2,1)} %get-tuple-element.272) | copy-start | bytes 1572868 | tf_op jit(solution)/shard_map/while
  82.3 3.8 %copy-start.5 = (bf16[1536,256]{0,1:T(8,128)(2,1)S(1)}, bf16[1536,256]{0,1:T(8,128)(2,1)}, u32[]{:S(2)}) copy-start(bf16[1536,256]{0,1:T(8,128)(2,1)} %copy-done.4) | copy-start | bytes 2359300 | tf_op jit(solution)/shard_map/while
  82.3 3.8 %copy-start.7 = (bf16[1536,256]{0,1:T(8,128)(2,1)S(1)}, bf16[1536,256]{0,1:T(8,128)(2,1)}, u32[]{:S(2)}) copy-start(bf16[1536,256]{0,1:T(8,128)(2,1)} %copy-done.6) | copy-start | bytes 2359300 | tf_op jit(solution)/shard_map/while
  82.3 3.8 %copy-start.9 = (bf16[1024,256]{1,0:T(8,128)(2,1)S(1)}, bf16[1024,256]{1,0:T(8,128)(2,1)}, u32[]{:S(2)}) copy-start(bf16[1024,256]{1,0:T(8,128)(2,1)} %copy-done.8) | copy-start | bytes 1572868 | tf_op jit(solution)/shard_map/while
  85.3 0.8 copy-start.16
  88.7 5.2 %copy-start.12 = (bf16[1024,256]{1,0:T(8,128)(2,1)S(1)}, bf16[1024,256]{1,0:T(8,128)(2,1)}, u32[]{:S(2)}) copy-start(bf16[1024,256]{1,0:T(8,128)(2,1)} %param.15) | copy-start | bytes 1572868
  88.7 5.2 %copy-start.17 = (bf16[2,512,256]{2,1,0:T(8,128)(2,1)S(1)}, bf16[2,512,256]{2,1,0:T(8,128)(2,1)}, u32[]{:S(2)}) copy-start(bf16[2,512,256]{2,1,0:T(8,128)(2,1)} %get-tuple-element.123) | copy-start | bytes 1572868
  88.9 11.7 %collective-permute-start.2 = (bf16[512,256]{1,0:T(8,128)(2,1)S(1)}, bf16[512,256]{1,0:T(8,128)(2,1)S(1)}, u32[]{:S(2)}, u32[]{:S(2)}) collective-permute-start(bf16[512,256]{1,0:T(8,128)(2,1)S(1)} %get-tuple-element.177), channel_id=1, source_target_pairs={{4,0},{8,4},{12,8},{16,12},{20,16},{24,20},{28,24},{32,28},{36,32}... | collective-permute-start | bytes 786440 | tf_op jit(solution)/shard_map/ppermute | solution.py:14
  91.7 9.1 %copy-start.13 = (bf16[1024,256]{1,0:T(8,128)(2,1)S(1)}, bf16[1024,256]{1,0:T(8,128)(2,1)}, u32[]{:S(2)}) copy-start(bf16[1024,256]{1,0:T(8,128)(2,1)} %param.16) | copy-start | bytes 1572868
  91.7 11.8 %collective-permute-start.3 = (bf16[512,256]{1,0:T(8,128)(2,1)S(1)}, bf16[512,256]{1,0:T(8,128)(2,1)S(1)}, u32[]{:S(2)}, u32[]{:S(2)}) collective-permute-start(bf16[512,256]{1,0:T(8,128)(2,1)S(1)} %get-tuple-element.179), channel_id=1, source_target_pairs={{4,0},{8,4},{12,8},{16,12},{20,16},{24,20},{28,24},{32,28},{36,32}... | collective-permute-start | bytes 786440 | tf_op jit(solution)/shard_map/ppermute | solution.py:14
  100.7 2.8 %copy-start.14 = (bf16[1024,256]{1,0:T(8,128)(2,1)S(1)}, bf16[1024,256]{1,0:T(8,128)(2,1)}, u32[]{:S(2)}) copy-start(bf16[1024,256]{1,0:T(8,128)(2,1)} %param.17) | copy-start | bytes 1572868
  106.2 78.5 %copy-start.1 = (bf16[1024,1024]{1,0:T(8,128)(2,1)S(1)}, bf16[1024,1024]{1,0:T(8,128)(2,1)}, u32[]{:S(2)}) copy-start(bf16[1024,1024]{1,0:T(8,128)(2,1)} %param.19) | copy-start | bytes 6291460
  120.7 13.8 %collective-permute-start.4 = (bf16[256,1024]{1,0:T(8,128)(2,1)S(1)}, bf16[256,1024]{1,0:T(8,128)(2,1)S(1)}, u32[]{:S(2)}, u32[]{:S(2)}) collective-permute-start(bf16[256,1024]{1,0:T(8,128)(2,1)S(1)} %slice.103), channel_id=1, source_target_pairs={{4,0},{8,4},{12,8},{16,12},{20,16},{24,20},{28,24},{32,28},{36,32}... | collective-permute-start | bytes 1572872 | tf_op jit(solution)/shard_map/ppermute | solution.py:14
Sparse Core Ops, SparseCore 0:
  136.8 44.5 all-reduce.5
where the time goes:
time: 195 us; the launch traced here: 192 us
  waiting for transfers between devices  60.6 us (31%)
  matrix products  48.5 us (25%)
  local copies, waits for them, and re-layouts  29.7 us (15%)
  other arithmetic  22.2 us (11%)
  starting transfers between devices  13.8 us (7%)
  between operations  13.7 us (7%)
  loops' own time  3.07 us (2%)
    psum x1, waiting for transfers between devices, on_device(): patch_low = lax.psum(owned.astype(jnp.bfloat16), 'mp')  44.7 us
    ppermute x5, waiting for transfers between devices, passed_along(): lax.ppermute(value, axis, [(source, source + steps) for source in range(l...  15.9 us
    ppermute x5, starting transfers between devices, passed_along(): lax.ppermute(value, axis, [(source, source + steps) for source in range(l...  13.8 us
    scatter-add x1, other arithmetic, on_device(): frame = jax.ops.segment_sum(byte_grad, local_slot, num_segments=slots)  13.2 us
    while x48, local copies, waits for them, and re-layouts  10.7 us
    sub x2, matrix products, block_grads(): raised = jnp.exp(scores - peak)  10.7 us
    dot_general x2, matrix products, block_grads(): jnp.einsum('hij,ihd->jhd', attend_low, grad_heads, preferred_element_type...  10.6 us
    dot_general x2, matrix products, block_grads(): jnp.einsum('ihd,jhd->hij', grad_heads, value_heads, preferred_element_typ...  9.47 us
  transfers between devices with their start and end apart: 6, of which 3 were waited for; matrix products, arithmetic and copies ran while one was open for 5% of the time, Pallas kernels for 0%

commit v1 on v0

v1 whole, which is shorter than its diff:
```python
import functools

import jax
import jax.numpy as jnp
from jax import lax
from jax.experimental import pallas as pl
from jax.experimental.pallas import tpu as pltpu
from jax.sharding import PartitionSpec as P

HS = 64
WINDOW = 512
PATCH_DEV = 256
TILE = 256
REACH = 128
F32 = jnp.float32
BF16 = jnp.bfloat16


def mm(a, b):
    return lax.dot_general(a, b, (((1,), (0,)), ((), ())), preferred_element_type=F32)


def mm_t(a, b):
    return lax.dot_general(a, b, (((1,), (1,)), ((), ())), preferred_element_type=F32)


def head_parts(tile):
    head = lax.broadcasted_iota(jnp.int32, tile.shape, 1) // HS
    return [jnp.where(head == h, tile, jnp.zeros_like(tile)) for h in range(tile.shape[1] // HS)]


def one_hot(slots, first, count):
    places = lax.broadcasted_iota(jnp.int32, (count, slots.shape[1]), 0) + first
    return jnp.where(places == slots, 1.0, 0.0).astype(BF16)


def attend(query, grad, keys, values, keys_t, bias):
    key_row = lax.broadcasted_iota(jnp.int32, (TILE, TILE), 0)
    query_col = lax.broadcasted_iota(jnp.int32, (TILE, TILE), 1)
    late = key_row <= query_col
    nil = jnp.zeros((TILE, TILE), BF16)
    query = query * jnp.asarray(HS**-0.5, BF16)
    d_query, d_key, d_value = [], [None] * 3, [None] * 3

    def added(total, term):
        return term if total is None else total + term

    for h, (q, g) in enumerate(zip(head_parts(query), head_parts(grad))):
        s = [mm_t(k, q) for k in keys]
        s = [x if b is None else x + b for x, b in zip(s, bias)]
        dp = [mm_t(v, g) for v in values]
        s_edge, s_mid = jnp.where(late, s[2], s[0]), s[1]
        dp_edge, dp_mid = jnp.where(late, dp[2], dp[0]), dp[1]
        peak = jnp.maximum(
            jnp.max(s_edge, axis=0, keepdims=True), jnp.max(s_mid, axis=0, keepdims=True)
        )
        e_edge, e_mid = jnp.exp(s_edge - peak), jnp.exp(s_mid - peak)
        total = jnp.sum(e_edge, axis=0, keepdims=True) + jnp.sum(e_mid, axis=0, keepdims=True)
        inverse = 1.0 / total
        row_dot = inverse * (
            jnp.sum(e_edge * dp_edge, axis=0, keepdims=True)
            + jnp.sum(e_mid * dp_mid, axis=0, keepdims=True)
        )
        p_edge, p_mid = e_edge * inverse, e_mid * inverse
        ds_edge = (p_edge * (dp_edge - row_dot)).astype(BF16)
        ds_mid = (p_mid * (dp_mid - row_dot)).astype(BF16)
        p_edge, p_mid = p_edge.astype(BF16), p_mid.astype(BF16)
        ds = [jnp.where(late, nil, ds_edge), ds_mid, jnp.where(late, ds_edge, nil)]
        p = [jnp.where(late, nil, p_edge), p_mid, jnp.where(late, p_edge, nil)]
        for t in range(3):
            d_key[t] = added(d_key[t], mm(ds[t], q))
            d_value[t] = added(d_value[t], mm(p[t], g))
        rows = slice(h * HS, (h + 1) * HS)
        d_query.append(sum(mm(keys_t[t][rows], ds[t]) for t in range(3)))
    d_query_t = jnp.concatenate(d_query, 0) * HS**-0.5
    return d_query_t.astype(BF16), d_key, d_value


def tiles_of(ref, first, count=3):
    return [ref[t * TILE : (t + 1) * TILE, :] for t in range(first, first + count)]


def near_kernel(
    d_output, w_out, queries, keys, values, slots, heads_out, k_out, v_out, x_out, kt, dk, dv, dqt
):
    later = mm_t(d_output[WINDOW:, :], w_out[...]).astype(BF16)
    for t in range(4):
        kt[t] = keys[t * TILE : (t + 1) * TILE, :].T
    for n in range(2):
        rows = slice(WINDOW + n * TILE, WINDOW + (n + 1) * TILE)
        d_query_t, d_key, d_value = attend(
            queries[rows, :],
            later[n * TILE : (n + 1) * TILE],
            tiles_of(keys, n),
            tiles_of(values, n),
            [kt[n + t] for t in range(3)],
            (None, None, None),
        )
        dqt[:, n * TILE : (n + 1) * TILE] = d_query_t
        for t in range(3):
            at = slice((n + t) * TILE, (n + t + 1) * TILE)
            if n == 0 or t == 2:
                dk[at, :] = d_key[t]
                dv[at, :] = d_value[t]
            else:
                dk[at, :] += d_key[t]
                dv[at, :] += d_value[t]
    heads_out[...] = mm_t(d_output[:WINDOW, :], w_out[...]).astype(BF16)
    k_out[...] = dk[:WINDOW, :]
    v_out[...] = dv[:WINDOW, :]
    chosen = one_hot(slots[:, WINDOW:], 0, PATCH_DEV)
    x_out[:, :TILE] = mm_t(chosen, dqt[...])
    x_out[:, TILE : 2 * TILE] = mm(chosen, dk[WINDOW:, :].astype(BF16))
    x_out[:, 2 * TILE :] = mm(chosen, dv[WINDOW:, :].astype(BF16))


def far_kernel(
    bias_ref, grads, queries, keys, values, tail_keys, tail_values, slots, tail_slots, k_in, v_in, x_in,
    sent_out, x_out, kt, dk, dv, dqt,
):
    bias = bias_ref[0]
    for t in range(2):
        kt[t] = tail_keys[t * TILE : (t + 1) * TILE, :].T
        kt[2 + t] = keys[t * TILE : (t + 1) * TILE, :].T
    all_keys = tiles_of(tail_keys, 0, 2) + tiles_of(keys, 0, 2)
    all_values = tiles_of(tail_values, 0, 2) + tiles_of(values, 0, 2)
    dk[WINDOW:, :] = k_in[...]
    dv[WINDOW:, :] = v_in[...]
    for n in range(2):
        rows = slice(n * TILE, (n + 1) * TILE)
        d_query_t, d_key, d_value = attend(
            queries[rows, :],
            grads[rows, :],
            all_keys[n : n + 3],
            all_values[n : n + 3],
            [kt[n + t] for t in range(3)],
            (bias, bias if n == 0 else None, None),
        )
        dqt[:, n * TILE : (n + 1) * TILE] = d_query_t
        for t in range(3):
            at = slice((n + t) * TILE, (n + t + 1) * TILE)
            if n == 0 and t < 2:
                dk[at, :] = d_key[t]
                dv[at, :] = d_value[t]
            else:
                dk[at, :] += d_key[t]
                dv[at, :] += d_value[t]
    before = one_hot(tail_slots[...], 0, PATCH_DEV)
    near = one_hot(slots[:, :REACH], -PATCH_DEV, PATCH_DEV)
    edge = slice(WINDOW, WINDOW + REACH)
    for place, total in ((0, dk), (PATCH_DEV, dv)):
        sent_out[place : place + PATCH_DEV, :] = (
            mm(before, total[:WINDOW, :].astype(BF16)) + mm(near, total[edge, :].astype(BF16))
        ).astype(BF16)
    sent_out[2 * PATCH_DEV :, :] = mm_t(near[PATCH_DEV - REACH :], dqt[:, :REACH]).astype(BF16)
    chosen = one_hot(slots[:, :WINDOW], 0, PATCH_DEV)
    x_out[:, :TILE] = x_in[:, :TILE] + mm_t(chosen, dqt[...])
    x_out[:, TILE : 2 * TILE] = x_in[:, TILE : 2 * TILE] + mm(chosen, dk[WINDOW:, :].astype(BF16))
    x_out[:, 2 * TILE :] = x_in[:, 2 * TILE :] + mm(chosen, dv[WINDOW:, :].astype(BF16))


def project_kernel(x_in, arrived, w_query, w_key, w_value, first_out, second_out):
    low = PATCH_DEV - REACH
    x_query = jnp.concatenate(
        [x_in[:low, :TILE], x_in[low:, :TILE] + arrived[2 * PATCH_DEV :, :].astype(F32)], 0
    ).astype(BF16)
    x_key = (x_in[:, TILE : 2 * TILE] + arrived[:PATCH_DEV, :].astype(F32)).astype(BF16)
    x_value = (
        x_in[:, 2 * TILE :] + arrived[PATCH_DEV : 2 * PATCH_DEV, :].astype(F32)
    ).astype(BF16)
    d_up = mm_t(x_query, w_query[...]) + mm_t(x_key, w_key[...]) + mm_t(x_value, w_value[...])
    first_out[...] = d_up[: PATCH_DEV // 2].astype(BF16)
    second_out[...] = d_up[PATCH_DEV // 2 :].astype(BF16)


def final_kernel(a, a_in, b, b_in, unpatch, out):
    half = PATCH_DEV // 2
    for place, own, other in ((0, a, a_in), (half, b, b_in)):
        total = (own[...].astype(F32) + other[...].astype(F32)).astype(BF16)
        out[place : place + half, :] = mm(total, unpatch[...]).astype(BF16)


def call(kernel, shapes, args, scratch=(), smem=0, flops=0):
    specs = [pl.BlockSpec(memory_space=pltpu.SMEM)] * smem
    specs += [pl.BlockSpec(memory_space=pltpu.VMEM)] * (len(args) - smem)
    return pl.pallas_call(
        kernel,
        out_shape=[jax.ShapeDtypeStruct(*shape) for shape in shapes],
        in_specs=specs,
        out_specs=[pl.BlockSpec(memory_space=pltpu.VMEM)] * len(shapes),
        scratch_shapes=list(scratch),
        compiler_params=pltpu.CompilerParams(vmem_limit_bytes=40 * 1024 * 1024),
        cost_estimate=pl.CostEstimate(flops=flops, bytes_accessed=0, transcendentals=0),
    )(*args)


def on_device(
    queries, byte_keys, byte_values, w_query, w_key, w_value, w_out, d_output, patch_index, unpatch
):
    shard = lax.axis_index("seq")
    count = lax.axis_size("seq")
    onward = [(n, n + 1) for n in range(count - 1)]
    back = [(n + 1, n) for n in range(count - 1)]
    bytes_dev = queries.shape[0]
    tail = bytes_dev - WINDOW
    tail_keys = lax.ppermute(byte_keys[tail:], "seq", onward)
    tail_values = lax.ppermute(byte_values[tail:], "seq", onward)
    slots = (patch_index - shard * PATCH_DEV)[None, :]
    tail_slots = lax.ppermute(slots[:, tail:], "seq", onward)
    bias = jnp.where(shard > 0, 0.0, -1e30).astype(F32)[None]

    grads, k_part, v_part, x_part = call(
        near_kernel,
        [((WINDOW, 256), BF16), ((WINDOW, 256), F32), ((WINDOW, 256), F32), ((PATCH_DEV, 768), F32)],
        (d_output, w_out, queries, byte_keys, byte_values, slots),
        [
            pltpu.VMEM((4, 256, TILE), BF16),
            pltpu.VMEM((1024, 256), F32),
            pltpu.VMEM((1024, 256), F32),
            pltpu.VMEM((256, 512), BF16),
        ],
        flops=8 * 10**9,
    )
    sent, x_own = call(
        far_kernel,
        [((2 * PATCH_DEV + REACH, 256), BF16), ((PATCH_DEV, 768), F32)],
        (
            bias, grads, queries, byte_keys, byte_values, tail_keys, tail_values, slots, tail_slots,
            k_part, v_part, x_part,
        ),
        [
            pltpu.VMEM((4, 256, TILE), BF16),
            pltpu.VMEM((1024, 256), F32),
            pltpu.VMEM((1024, 256), F32),
            pltpu.VMEM((256, 512), BF16),
        ],
        smem=1,
        flops=8 * 10**9,
    )
    arrived = lax.ppermute(sent, "seq", back)
    a, b = call(
        project_kernel,
        [((PATCH_DEV // 2, 1024), BF16)] * 2,
        (x_own, arrived, w_query, w_key, w_value),
        flops=4 * 10**8,
    )
    across = [(0, 1), (1, 0), (2, 3), (3, 2)]
    around = [(0, 3), (3, 0), (1, 2), (2, 1)]

    def pair(mine, other):
        return (mine.astype(F32) + other.astype(F32)).astype(BF16)

    a_in, b_in = lax.ppermute(a, "mp", across), lax.ppermute(b, "mp", around)
    a, b = pair(a, a_in), pair(b, b_in)
    a_in, b_in = lax.ppermute(a, "mp", around), lax.ppermute(b, "mp", across)
    return call(
        final_kernel,
        [((PATCH_DEV, 1024), BF16)],
        (a, a_in, b, b_in, unpatch),
        flops=5 * 10**8,
    )[0]


def solution(mesh):
    in_specs = (
        P("seq", "mp"),
        P("seq", "mp"),
        P("seq", "mp"),
        P(None, "mp"),
        P(None, "mp"),
        P(None, "mp"),
        P("mp", None),
        P("seq", None),
        P("seq"),
        P(None, "mp"),
    )
    return jax.shard_map(
        on_device, mesh=mesh, in_specs=in_specs, out_specs=P("seq", "mp"), check_vma=False
    )
```

time: 195 us -> 67.5 us (0.35); the launches traced: 192 us -> 67 us
  matrix products: 48.5 us -> 0 us
  waiting for transfers between devices: 60.6 us -> 18.6 us
  other arithmetic: 22.2 us -> 0.82 us
  local copies, waits for them, and re-layouts: 29.7 us -> 12.6 us
  Pallas kernels: 0 us -> 16 us
  between operations: 13.7 us -> 0.15 us
  starting transfers between devices: 13.8 us -> 18.8 us
  loops' own time: 3.07 us -> 0 us
    psum x1 -> x0, waiting for transfers between devices: 44.7 us -> none  [on_device(): patch_low = lax.psum(owned.astype(jnp.bfloat16), 'mp')]
    dot_general x13 -> x0, matrix products: 37.8 us -> none  [the longest x2 10.6 us: block_grads(): jnp.einsum('hij,ihd->jhd', attend_low, grad_heads, preferred_element_type...]
    pallas_call x0 -> x4, Pallas kernels: none -> 16 us  [call(): pl.pallas_call(kernel, out_shape=[jax.ShapeDtypeStruct(*shape) for shape...]
    scatter-add x1 -> x0, other arithmetic: 13.2 us -> none  [on_device(): frame = jax.ops.segment_sum(byte_grad, local_slot, num_segments=slots)]
    while x48 -> x0, local copies, waits for them, and re-layouts: 10.7 us -> none
    sub x2 -> x0, matrix products: 10.7 us -> none  [block_grads(): raised = jnp.exp(scores - peak)]
    dynamic_update_slice x10 -> x0, local copies, waits for them, and re-layouts: 7.08 us -> none  [on_device(): lax.map(one_block, jnp.arange(byte_count // WINDOW, dtype=jnp.int32))]
    unnamed x20 -> x32, local copies, waits for them, and re-layouts: 2.84 us -> 9.25 us
  transfers between devices with their start and end apart: 6 -> 8, of which waited for: 3 -> 5; matrix products, arithmetic and copies ran while one was open for 5% -> 5% of each run, Pallas kernels for 0% -> 11%
where the time goes in v1:
time: 67.5 us; the launch traced here: 67 us
  starting transfers between devices  18.8 us (28%)
  waiting for transfers between devices  18.6 us (28%)
  Pallas kernels  16 us (24%)
  local copies, waits for them, and re-layouts  12.6 us (19%)
  other arithmetic  0.82 us (1%)
    pallas_call x4, Pallas kernels, call(): pl.pallas_call(kernel, out_shape=[jax.ShapeDtypeStruct(*shape) for shape...  16 us
    ppermute x1, waiting for transfers between devices, on_device(): arrived = lax.ppermute(sent, 'seq', back)  9.79 us
    unnamed x32, local copies, waits for them, and re-layouts  9.25 us
    ppermute x1, starting transfers between devices, on_device(): tail_slots = lax.ppermute(slots[:, tail:], 'seq', onward)  5.22 us
    ppermute x2, waiting for transfers between devices, on_device(): a_in, b_in = (lax.ppermute(a, 'mp', around), lax.ppermute(b, 'mp', across))  5.21 us
    ppermute x2, waiting for transfers between devices, on_device(): a_in, b_in = (lax.ppermute(a, 'mp', across), lax.ppermute(b, 'mp', around))  3.63 us
    ppermute x1, starting transfers between devices, on_device(): tail_keys = lax.ppermute(byte_keys[tail:], 'seq', onward)  3.49 us
    ppermute x2, starting transfers between devices, on_device(): a_in, b_in = (lax.ppermute(a, 'mp', across), lax.ppermute(b, 'mp', around))  3.29 us
  transfers between devices with their start and end apart: 8, of which 5 were waited for; matrix products, arithmetic and copies ran while one was open for 5% of the time, Pallas kernels for 11%

profile of v1, /device:TPU:103, one launch (start us, length us, event | category | flops | bytes accessed | tf_op | source)
XLA Modules:
  0.0 67.0 jit_solution(791775161255696728)
XLA Ops:
  0.0 0.7 %broadcast_subtract_fusion = s32[1024]{0:T(1024)S(1)} fusion(s32[1024]{0:T(1024)} %param.18, s32[]{:T(128)S(6)} %mul.3), kind=kLoop, calls=%fused_computation.2 | loop fusion | flops 1024 | bytes 8196 | tf_op jit(solution)/shard_map/sub | solution.py:208
  0.7 5.2 %collective-permute-start.2 = (s32[1,512]{1,0:T(1,128)S(1)}, s32[1,512]{1,0:T(1,128)S(1)}, u32[]{:S(2)}, u32[]{:S(2)}) collective-permute-start(s32[1,512]{1,0:T(1,128)S(1)} %slice.12), channel_id=1, source_target_pairs={{0,4},{4,8},{8,12},{12,16},{16,20},{20,24},{24,28},{28,32},{32,36}... | collective-permute-start | bytes 6152 | tf_op jit(solution)/shard_map/ppermute | solution.py:209
  5.9 1.7 %slice.10 = bf16[512,256]{1,0:T(8,128)(2,1)} slice(bf16[1024,256]{1,0:T(8,128)(2,1)} %values.3), slice={[512:1024], [0:256]} | slice | bytes 524288 | tf_op jit(solution)/shard_map/slice | solution.py:207
  7.6 1.9 %collective-permute-start.1 = (bf16[512,256]{1,0:T(8,128)(2,1)}, bf16[512,256]{1,0:T(8,128)(2,1)S(1)}, u32[]{:S(2)}, u32[]{:S(2)}) collective-permute-start(bf16[512,256]{1,0:T(8,128)(2,1)} %slice.10), channel_id=1, source_target_pairs={{0,4},{4,8},{8,12},{12,16},{16,20},{20,24},{24,28},{28,32},{32,36}... | collective-permute-start | bytes 786440 | tf_op jit(solution)/shard_map/ppermute | solution.py:207
  9.5 1.7 %slice.9 = bf16[512,256]{1,0:T(8,128)(2,1)} slice(bf16[1024,256]{1,0:T(8,128)(2,1)} %keys.3), slice={[512:1024], [0:256]} | slice | bytes 524288 | tf_op jit(solution)/shard_map/slice | solution.py:206
  11.2 3.5 %collective-permute-start = (bf16[512,256]{1,0:T(8,128)(2,1)}, bf16[512,256]{1,0:T(8,128)(2,1)S(1)}, u32[]{:S(2)}, u32[]{:S(2)}) collective-permute-start(bf16[512,256]{1,0:T(8,128)(2,1)} %slice.9), channel_id=1, source_target_pairs={{0,4},{4,8},{8,12},{12,16},{16,20},{20,24},{24,28},{28,32},{32,36}... | collective-permute-start | bytes 786440 | tf_op jit(solution)/shard_map/ppermute | solution.py:206
  14.7 0.0 copy-start.4
  14.7 1.0 %copy-done.4 = bf16[1024,256]{1,0:T(8,128)(2,1)S(1)} copy-done((bf16[1024,256]{1,0:T(8,128)(2,1)S(1)}, bf16[1024,256]{1,0:T(8,128)(2,1)}, u32[]{:S(2)}) %copy-start.4) | copy-done | bytes 524312
  15.7 0.0 copy-start.6
  15.7 1.0 %copy-done.6 = bf16[1024,256]{1,0:T(8,128)(2,1)S(1)} copy-done((bf16[1024,256]{1,0:T(8,128)(2,1)S(1)}, bf16[1024,256]{1,0:T(8,128)(2,1)}, u32[]{:S(2)}) %copy-start.6) | copy-done | bytes 524312
  16.8 0.0 copy-start.8
  16.8 1.6 %copy-done.8 = bf16[1024,1024]{1,0:T(8,128)(2,1)S(1)} copy-done((bf16[1024,1024]{1,0:T(8,128)(2,1)S(1)}, bf16[1024,1024]{1,0:T(8,128)(2,1)}, u32[]{:S(2)}) %copy-start.8) | copy-done | bytes 2097176
  18.3 1.0 %copy-done.9 = bf16[256,1024]{1,0:T(8,128)(2,1)S(1)} copy-done((bf16[256,1024]{1,0:T(8,128)(2,1)S(1)}, bf16[256,1024]{1,0:T(8,128)(2,1)}, u32[]{:S(2)}) %copy-start.9) | copy-done | bytes 524312
  19.4 0.0 copy-start.10
  19.4 1.0 %copy-done.10 = bf16[1024,256]{1,0:T(8,128)(2,1)S(1)} copy-done((bf16[1024,256]{1,0:T(8,128)(2,1)S(1)}, bf16[1024,256]{1,0:T(8,128)(2,1)}, u32[]{:S(2)}) %copy-start.10) | copy-done | bytes 524312
  20.4 7.1 %shard_map.100 = (bf16[512,256]{1,0:T(8,128)(2,1)S(1)}, f32[512,256]{1,0:T(8,128)S(1)}, f32[512,256]{1,0:T(8,128)S(1)}, f32[256,768]{1,0:T(8,128)S(1)}) custom-call(bf16[1024,1024]{1,0:T(8,128)(2,1)S(1)} %copy-done.8, bf16[256,1024]{1,0:T(8,128)(2,1)S(1)} %copy-done.9, bf16[1024,256]{1,0:T(8,128)(2,1)S(1)} %copy-done.10, bf16[1024,256]{1,0:T(8,128)(2,1)S(1)} %copy-done.4, ...), custom_call_target="tpu_custom_call" | custom-call | flops 8000000000 | tf_op jit(solution)/shard_map/pallas_call | solution.py:186
  27.5 0.0 copy-start.12
  27.5 0.8 %copy-done.12 = f32[512,256]{1,0:T(8,128)} copy-done((f32[512,256]{1,0:T(8,128)}, f32[512,256]{1,0:T(8,128)S(1)}, u32[]{:S(2)}) %copy-start.12) | copy-done | bytes 524312
  28.3 0.7 %copy-done.14 = bf16[512,256]{1,0:T(8,128)(2,1)} copy-done((bf16[512,256]{1,0:T(8,128)(2,1)}, bf16[512,256]{1,0:T(8,128)(2,1)S(1)}, u32[]{:S(2)}) %copy-start.14) | copy-done | bytes 262168
  29.0 0.0 collective-permute-done.2.tail_slots
  29.0 0.0 collective-permute-done.1.tail_values
  29.0 0.0 collective-permute-done.tail_keys
  29.0 0.0 copy-done.5
  29.0 0.0 copy-done.7
  29.0 0.0 copy-done.11
  29.0 0.0 copy-start.13
  29.1 1.0 %copy-done.13 = f32[512,256]{1,0:T(8,128)S(1)} copy-done((f32[512,256]{1,0:T(8,128)S(1)}, f32[512,256]{1,0:T(8,128)}, u32[]{:S(2)}) %copy-start.13) | copy-done | bytes 524312
  30.1 0.9 %copy-done.15 = bf16[512,256]{1,0:T(8,128)(2,1)S(1)} copy-done((bf16[512,256]{1,0:T(8,128)(2,1)S(1)}, bf16[512,256]{1,0:T(8,128)(2,1)}, u32[]{:S(2)}) %copy-start.15) | copy-done | bytes 262168
  31.0 6.8 %shard_map.101 = (bf16[640,256]{1,0:T(8,128)(2,1)S(1)}, f32[256,768]{1,0:T(8,128)S(1)}) custom-call(f32[1]{0:T(128)} %bitcast.bias_ref, bf16[512,256]{1,0:T(8,128)(2,1)S(1)} %copy-done.15, bf16[1024,256]{1,0:T(8,128)(2,1)S(1)} %copy-done.11, bf16[1024,256]{1,0:T(8,128)(2,1)S(1)} %copy-done.5, bf16[1024,256]{1,0:T(8,128)(2,1)S(1)} %copy-done.7, ...), custom_call_target="tpu_custom_call" | custom-call | flops 8000000000 | tf_op jit(solution)/shard_map/pallas_call | solution.py:186
  37.9 1.9 %collective-permute-start.3 = (bf16[640,256]{1,0:T(8,128)(2,1)S(1)}, bf16[640,256]{1,0:T(8,128)(2,1)S(1)}, u32[]{:S(2)}, u32[]{:S(2)}) collective-permute-start(bf16[640,256]{1,0:T(8,128)(2,1)S(1)} %get-tuple-element.18), channel_id=1, source_target_pairs={{4,0},{8,4},{12,8},{16,12},{20,16},{24,20},{28,24},{32,28},{36,32}... | collective-permute-start | bytes 983048 | tf_op jit(solution)/shard_map/ppermute | solution.py:240
  39.8 9.8 %collective-permute-done.3.arrived = bf16[640,256]{1,0:T(8,128)(2,1)S(1)} collective-permute-done((bf16[640,256]{1,0:T(8,128)(2,1)S(1)}, bf16[640,256]{1,0:T(8,128)(2,1)S(1)}, u32[]{:S(2)}, u32[]{:S(2)}) %collective-permute-start.3) | collective-permute-done | bytes 327712 | tf_op jit(solution)/shard_map/ppermute | solution.py:240
  49.6 0.0 copy-done.1
  49.6 0.0 copy-done.2
  49.6 0.0 copy-done.3
  49.6 0.0 copy-start
  49.6 0.6 shard_map.102
  50.3 1.4 %collective-permute-start.4 = (bf16[128,1024]{1,0:T(8,128)(2,1)S(1)}, bf16[128,1024]{1,0:T(8,128)(2,1)S(1)}, u32[]{:S(2)}, u32[]{:S(2)}) collective-permute-start(bf16[128,1024]{1,0:T(8,128)(2,1)S(1)} %get-tuple-element.19), channel_id=1, source_target_pairs={{0,1},{1,0},{2,3},{3,2},{4,5},{5,4},{6,7},{7,6},{8,9},{9,8},{10,11... | collective-permute-start | bytes 786440 | tf_op jit(solution)/shard_map/ppermute | solution.py:253
  51.7 1.9 %collective-permute-start.6 = (bf16[128,1024]{1,0:T(8,128)(2,1)S(1)}, bf16[128,1024]{1,0:T(8,128)(2,1)S(1)}, u32[]{:S(2)}, u32[]{:S(2)}) collective-permute-start(bf16[128,1024]{1,0:T(8,128)(2,1)S(1)} %get-tuple-element.20), channel_id=1, source_target_pairs={{0,3},{3,0},{1,2},{2,1},{4,7},{7,4},{5,6},{6,5},{8,11},{11,8},{9,1... | collective-permute-start | bytes 786440 | tf_op jit(solution)/shard_map/ppermute | solution.py:253
  53.5 2.0 %collective-permute-done.4 = bf16[128,1024]{1,0:T(8,128)(2,1)S(1)} collective-permute-done((bf16[128,1024]{1,0:T(8,128)(2,1)S(1)}, bf16[128,1024]{1,0:T(8,128)(2,1)S(1)}, u32[]{:S(2)}, u32[]{:S(2)}) %collective-permute-start.4) | collective-permute-done | bytes 262176 | tf_op jit(solution)/shard_map/ppermute | solution.py:253
  55.6 0.1 add_convert_fusion.1.a
  55.6 2.8 %collective-permute-start.5 = (bf16[128,1024]{1,0:T(8,128)(2,1)S(1)}, bf16[128,1024]{1,0:T(8,128)(2,1)S(1)}, u32[]{:S(2)}, u32[]{:S(2)}) collective-permute-start(bf16[128,1024]{1,0:T(8,128)(2,1)S(1)} %add_convert_fusion.1.a), channel_id=1, source_target_pairs={{0,3},{3,0},{1,2},{2,1},{4,7},{7,4},{5,6},{6,5},{8,11},{11,8},{9,1... | collective-permute-start | bytes 786440 | tf_op jit(solution)/shard_map/ppermute | solution.py:255
  58.5 1.6 %collective-permute-done.6 = bf16[128,1024]{1,0:T(8,128)(2,1)S(1)} collective-permute-done((bf16[128,1024]{1,0:T(8,128)(2,1)S(1)}, bf16[128,1024]{1,0:T(8,128)(2,1)S(1)}, u32[]{:S(2)}, u32[]{:S(2)}) %collective-permute-start.6) | collective-permute-done | bytes 262176 | tf_op jit(solution)/shard_map/ppermute | solution.py:253
  60.1 0.1 add_convert_fusion.b
  60.1 0.1 collective-permute-start.7
  60.2 3.5 %collective-permute-done.5.a_in = bf16[128,1024]{1,0:T(8,128)(2,1)S(1)} collective-permute-done((bf16[128,1024]{1,0:T(8,128)(2,1)S(1)}, bf16[128,1024]{1,0:T(8,128)(2,1)S(1)}, u32[]{:S(2)}, u32[]{:S(2)}) %collective-permute-start.5) | collective-permute-done | bytes 262176 | tf_op jit(solution)/shard_map/ppermute | solution.py:255
  63.7 1.8 %collective-permute-done.7.b_in = bf16[128,1024]{1,0:T(8,128)(2,1)S(1)} collective-permute-done((bf16[128,1024]{1,0:T(8,128)(2,1)S(1)}, bf16[128,1024]{1,0:T(8,128)(2,1)S(1)}, u32[]{:S(2)}, u32[]{:S(2)}) %collective-permute-start.7) | collective-permute-done | bytes 262176 | tf_op jit(solution)/shard_map/ppermute | solution.py:255
  65.5 0.0 copy-done
  65.5 1.5 %shard_map.103 = bf16[256,1024]{1,0:T(8,128)(2,1)} custom-call(bf16[128,1024]{1,0:T(8,128)(2,1)S(1)} %add_convert_fusion.1.a, bf16[128,1024]{1,0:T(8,128)(2,1)S(1)} %collective-permute-done.5.a_in, bf16[128,1024]{1,0:T(8,128)(2,1)S(1)} %add_convert_fusion.b, bf16[128,1024]{1,0:T(8,128)(2,1)S(1)} %collective-permute-done.7.b_in, bf16[1024,1024]{1,0:T(8,128)(2,1)S(1)} %copy-done), custom_call_target="tpu_custom_call" | custom-call | flops 500000000 | tf_op jit(solution)/shard_map/pallas_call | solution.py:186
  (10 shorter events, 0.0 us)
Async XLA Ops:
  0.7 28.3 %collective-permute-start.2 = (s32[1,512]{1,0:T(1,128)S(1)}, s32[1,512]{1,0:T(1,128)S(1)}, u32[]{:S(2)}, u32[]{:S(2)}) collective-permute-start(s32[1,512]{1,0:T(1,128)S(1)} %slice.12), channel_id=1, source_target_pairs={{0,4},{4,8},{8,12},{12,16},{16,20},{20,24},{24,28},{28,32},{32,36}... | collective-permute-start | bytes 6152 | tf_op jit(solution)/shard_map/ppermute | solution.py:209
  7.6 21.4 %collective-permute-start.1 = (bf16[512,256]{1,0:T(8,128)(2,1)}, bf16[512,256]{1,0:T(8,128)(2,1)S(1)}, u32[]{:S(2)}, u32[]{:S(2)}) collective-permute-start(bf16[512,256]{1,0:T(8,128)(2,1)} %slice.10), channel_id=1, source_target_pairs={{0,4},{4,8},{8,12},{12,16},{16,20},{20,24},{24,28},{28,32},{32,36}... | collective-permute-start | bytes 786440 | tf_op jit(solution)/shard_map/ppermute | solution.py:207
  11.2 17.8 %collective-permute-start = (bf16[512,256]{1,0:T(8,128)(2,1)}, bf16[512,256]{1,0:T(8,128)(2,1)S(1)}, u32[]{:S(2)}, u32[]{:S(2)}) collective-permute-start(bf16[512,256]{1,0:T(8,128)(2,1)} %slice.9), channel_id=1, source_target_pairs={{0,4},{4,8},{8,12},{12,16},{16,20},{20,24},{24,28},{28,32},{32,36}... | collective-permute-start | bytes 786440 | tf_op jit(solution)/shard_map/ppermute | solution.py:206
  14.7 1.0 %copy-start.4 = (bf16[1024,256]{1,0:T(8,128)(2,1)S(1)}, bf16[1024,256]{1,0:T(8,128)(2,1)}, u32[]{:S(2)}) copy-start(bf16[1024,256]{1,0:T(8,128)(2,1)} %keys.3) | copy-start | bytes 1572868
  15.7 1.0 %copy-start.6 = (bf16[1024,256]{1,0:T(8,128)(2,1)S(1)}, bf16[1024,256]{1,0:T(8,128)(2,1)}, u32[]{:S(2)}) copy-start(bf16[1024,256]{1,0:T(8,128)(2,1)} %values.3) | copy-start | bytes 1572868
  16.8 1.6 %copy-start.8 = (bf16[1024,1024]{1,0:T(8,128)(2,1)S(1)}, bf16[1024,1024]{1,0:T(8,128)(2,1)}, u32[]{:S(2)}) copy-start(bf16[1024,1024]{1,0:T(8,128)(2,1)} %d_output.1) | copy-start | bytes 6291460
  18.3 1.0 %copy-start.9 = (bf16[256,1024]{1,0:T(8,128)(2,1)S(1)}, bf16[256,1024]{1,0:T(8,128)(2,1)}, u32[]{:S(2)}) copy-start(bf16[256,1024]{1,0:T(8,128)(2,1)} %w_out.1) | copy-start | bytes 1572868
  19.4 1.0 %copy-start.10 = (bf16[1024,256]{1,0:T(8,128)(2,1)S(1)}, bf16[1024,256]{1,0:T(8,128)(2,1)}, u32[]{:S(2)}) copy-start(bf16[1024,256]{1,0:T(8,128)(2,1)} %queries.3) | copy-start | bytes 1572868
  20.4 8.6 %copy-start.5 = (bf16[1024,256]{1,0:T(8,128)(2,1)S(1)}, bf16[1024,256]{1,0:T(8,128)(2,1)}, u32[]{:S(2)}) copy-start(bf16[1024,256]{1,0:T(8,128)(2,1)} %keys.3) | copy-start | bytes 1572868
  20.4 8.6 %copy-start.7 = (bf16[1024,256]{1,0:T(8,128)(2,1)S(1)}, bf16[1024,256]{1,0:T(8,128)(2,1)}, u32[]{:S(2)}) copy-start(bf16[1024,256]{1,0:T(8,128)(2,1)} %values.3) | copy-start | bytes 1572868
  20.4 8.6 %copy-start.11 = (bf16[1024,256]{1,0:T(8,128)(2,1)S(1)}, bf16[1024,256]{1,0:T(8,128)(2,1)}, u32[]{:S(2)}) copy-start(bf16[1024,256]{1,0:T(8,128)(2,1)} %queries.3) | copy-start | bytes 1572868
  27.5 0.8 %copy-start.12 = (f32[512,256]{1,0:T(8,128)}, f32[512,256]{1,0:T(8,128)S(1)}, u32[]{:S(2)}) copy-start(f32[512,256]{1,0:T(8,128)S(1)} %get-tuple-element.15.v_in) | copy-start | bytes 1572868
  28.3 0.7 %copy-start.14 = (bf16[512,256]{1,0:T(8,128)(2,1)}, bf16[512,256]{1,0:T(8,128)(2,1)S(1)}, u32[]{:S(2)}) copy-start(bf16[512,256]{1,0:T(8,128)(2,1)S(1)} %get-tuple-element.13.grads) | copy-start | bytes 786436
  29.0 1.0 %copy-start.13 = (f32[512,256]{1,0:T(8,128)S(1)}, f32[512,256]{1,0:T(8,128)}, u32[]{:S(2)}) copy-start(f32[512,256]{1,0:T(8,128)} %copy-done.12) | copy-start | bytes 1572868
  30.1 0.9 %copy-start.15 = (bf16[512,256]{1,0:T(8,128)(2,1)S(1)}, bf16[512,256]{1,0:T(8,128)(2,1)}, u32[]{:S(2)}) copy-start(bf16[512,256]{1,0:T(8,128)(2,1)} %copy-done.14) | copy-start | bytes 786436
  31.0 18.6 %copy-start.1 = (bf16[1024,256]{1,0:T(8,128)(2,1)S(1)}, bf16[1024,256]{1,0:T(8,128)(2,1)}, u32[]{:S(2)}) copy-start(bf16[1024,256]{1,0:T(8,128)(2,1)} %w_query.1) | copy-start | bytes 1572868
  31.0 18.6 %copy-start.2 = (bf16[1024,256]{1,0:T(8,128)(2,1)S(1)}, bf16[1024,256]{1,0:T(8,128)(2,1)}, u32[]{:S(2)}) copy-start(bf16[1024,256]{1,0:T(8,128)(2,1)} %w_key.1) | copy-start | bytes 1572868
  31.0 18.6 %copy-start.3 = (bf16[1024,256]{1,0:T(8,128)(2,1)S(1)}, bf16[1024,256]{1,0:T(8,128)(2,1)}, u32[]{:S(2)}) copy-start(bf16[1024,256]{1,0:T(8,128)(2,1)} %w_value.1) | copy-start | bytes 1572868
  37.9 11.7 %collective-permute-start.3 = (bf16[640,256]{1,0:T(8,128)(2,1)S(1)}, bf16[640,256]{1,0:T(8,128)(2,1)S(1)}, u32[]{:S(2)}, u32[]{:S(2)}) collective-permute-start(bf16[640,256]{1,0:T(8,128)(2,1)S(1)} %get-tuple-element.18), channel_id=1, source_target_pairs={{4,0},{8,4},{12,8},{16,12},{20,16},{24,20},{28,24},{32,28},{36,32}... | collective-permute-start | bytes 983048 | tf_op jit(solution)/shard_map/ppermute | solution.py:240
  49.6 15.8 %copy-start = (bf16[1024,1024]{1,0:T(8,128)(2,1)S(1)}, bf16[1024,1024]{1,0:T(8,128)(2,1)}, u32[]{:S(2)}) copy-start(bf16[1024,1024]{1,0:T(8,128)(2,1)} %unpatch.1) | copy-start | bytes 6291460
  50.3 5.3 %collective-permute-start.4 = (bf16[128,1024]{1,0:T(8,128)(2,1)S(1)}, bf16[128,1024]{1,0:T(8,128)(2,1)S(1)}, u32[]{:S(2)}, u32[]{:S(2)}) collective-permute-start(bf16[128,1024]{1,0:T(8,128)(2,1)S(1)} %get-tuple-element.19), channel_id=1, source_target_pairs={{0,1},{1,0},{2,3},{3,2},{4,5},{5,4},{6,7},{7,6},{8,9},{9,8},{10,11... | collective-permute-start | bytes 786440 | tf_op jit(solution)/shard_map/ppermute | solution.py:253
  51.7 8.4 %collective-permute-start.6 = (bf16[128,1024]{1,0:T(8,128)(2,1)S(1)}, bf16[128,1024]{1,0:T(8,128)(2,1)S(1)}, u32[]{:S(2)}, u32[]{:S(2)}) collective-permute-start(bf16[128,1024]{1,0:T(8,128)(2,1)S(1)} %get-tuple-element.20), channel_id=1, source_target_pairs={{0,3},{3,0},{1,2},{2,1},{4,7},{7,4},{5,6},{6,5},{8,11},{11,8},{9,1... | collective-permute-start | bytes 786440 | tf_op jit(solution)/shard_map/ppermute | solution.py:253
  55.6 8.1 %collective-permute-start.5 = (bf16[128,1024]{1,0:T(8,128)(2,1)S(1)}, bf16[128,1024]{1,0:T(8,128)(2,1)S(1)}, u32[]{:S(2)}, u32[]{:S(2)}) collective-permute-start(bf16[128,1024]{1,0:T(8,128)(2,1)S(1)} %add_convert_fusion.1.a), channel_id=1, source_target_pairs={{0,3},{3,0},{1,2},{2,1},{4,7},{7,4},{5,6},{6,5},{8,11},{11,8},{9,1... | collective-permute-start | bytes 786440 | tf_op jit(solution)/shard_map/ppermute | solution.py:255
  60.1 5.3 %collective-permute-start.7 = (bf16[128,1024]{1,0:T(8,128)(2,1)S(1)}, bf16[128,1024]{1,0:T(8,128)(2,1)S(1)}, u32[]{:S(2)}, u32[]{:S(2)}) collective-permute-start(bf16[128,1024]{1,0:T(8,128)(2,1)S(1)} %add_convert_fusion.b), channel_id=1, source_target_pairs={{0,1},{1,0},{2,3},{3,2},{4,5},{5,4},{6,7},{7,6},{8,9},{9,8},{10,11... | collective-permute-start | bytes 786440 | tf_op jit(solution)/shard_map/ppermute | solution.py:255

commit v2 on v1

--- a/solution.py
+++ b/solution.py
@@ -80,52 +80,80 @@
     return [ref[t * TILE : (t + 1) * TILE, :] for t in range(first, first + count)]
 
 
-def near_kernel(
-    d_output, w_out, queries, keys, values, slots, heads_out, k_out, v_out, x_out, kt, dk, dv, dqt
+def pack_kernel(shard_ref, keys, values, index, packed, sems):
+    copies = [
+        pltpu.make_async_copy(source.at[WINDOW:, :], packed.at[n * WINDOW : (n + 1) * WINDOW, :], sems.at[n])
+        for n, source in enumerate((keys, values))
+    ]
+    for copy in copies:
+        copy.start()
+    slots = (index[:, WINDOW:] - shard_ref[0] * PATCH_DEV).astype(F32)
+    row = lax.broadcasted_iota(jnp.int32, (16, TILE), 0)
+    both = jnp.where(row == 0, slots[:, :TILE], slots[:, TILE:])
+    packed[2 * WINDOW :, :] = both.astype(BF16)
+    for copy in copies:
+        copy.wait()
+
+
+def heads_kernel(d_output_hbm, w_out_hbm, grads, d_output, w_out, sems):
+    half = d_output.shape[0] // 2
+    pairs = [(w_out_hbm, w_out)]
+    pairs += [(d_output_hbm.at[n : n + half, :], d_output.at[n : n + half, :]) for n in (0, half)]
+    copies = [pltpu.make_async_copy(*pair, sems.at[n]) for n, pair in enumerate(pairs)]
+    for copy in copies:
+        copy.start()
+    copies[0].wait()
+    for n in range(2):
+        copies[1 + n].wait()
+        rows = slice(n * half, (n + 1) * half)
+        grads[rows, :] = mm_t(d_output[rows, :], w_out[...]).astype(BF16)
+
+
+def place_sums(first, d_key, d_value, dk, dv, fresh=(True, True, True)):
+    for t in range(3):
+        at = slice((first + t) * TILE, (first + t + 1) * TILE)
+        if fresh[t]:
+            dk[at, :] = d_key[t]
+            dv[at, :] = d_value[t]
+        else:
+            dk[at, :] += d_key[t]
+            dv[at, :] += d_value[t]
+
+
+def near_kernel(shard_ref, grads, queries, keys, values, index, near_out, x_out):
+    rows = slice(2 * TILE, 3 * TILE)
+    d_query_t, d_key, d_value = attend(
+        queries[rows, :],
+        grads[rows, :],
+        tiles_of(keys, 0),
+        tiles_of(values, 0),
+        [keys[t * TILE : (t + 1) * TILE, :].T for t in range(3)],
+        (None, None, None),
+    )
+    slots = index[...] - shard_ref[0] * PATCH_DEV
+    d_key = jnp.concatenate([d.astype(BF16) for d in d_key], 0)
+    d_value = jnp.concatenate([d.astype(BF16) for d in d_value], 0)
+    before = one_hot(slots[:, :REACH], -REACH, REACH)
+    near_out[:, :TILE] = mm(before, d_key[:REACH])
+    near_out[:, TILE:] = mm(before, d_value[:REACH])
+    chosen = one_hot(slots[:, : 3 * TILE], 0, PATCH_DEV)
+    x_out[:, :TILE] = mm_t(chosen[:, 2 * TILE :], d_query_t)
+    x_out[:, TILE : 2 * TILE] = mm(chosen, d_key)
+    x_out[:, 2 * TILE :] = mm(chosen, d_value)
+
+
+def far_kernel(
+    shard_ref, grads, queries, keys, values, packed, index, near,
+    sent_out, k_out, v_out, q_out, kt, dk, dv,
 ):
-    later = mm_t(d_output[WINDOW:, :], w_out[...]).astype(BF16)
-    for t in range(4):
-        kt[t] = keys[t * TILE : (t + 1) * TILE, :].T
-    for n in range(2):
-        rows = slice(WINDOW + n * TILE, WINDOW + (n + 1) * TILE)
-        d_query_t, d_key, d_value = attend(
-            queries[rows, :],
-            later[n * TILE : (n + 1) * TILE],
-            tiles_of(keys, n),
-            tiles_of(values, n),
-            [kt[n + t] for t in range(3)],
-            (None, None, None),
-        )
-        dqt[:, n * TILE : (n + 1) * TILE] = d_query_t
-        for t in range(3):
-            at = slice((n + t) * TILE, (n + t + 1) * TILE)
-            if n == 0 or t == 2:
-                dk[at, :] = d_key[t]
-                dv[at, :] = d_value[t]
-            else:
-                dk[at, :] += d_key[t]
-                dv[at, :] += d_value[t]
-    heads_out[...] = mm_t(d_output[:WINDOW, :], w_out[...]).astype(BF16)
-    k_out[...] = dk[:WINDOW, :]
-    v_out[...] = dv[:WINDOW, :]
-    chosen = one_hot(slots[:, WINDOW:], 0, PATCH_DEV)
-    x_out[:, :TILE] = mm_t(chosen, dqt[...])
-    x_out[:, TILE : 2 * TILE] = mm(chosen, dk[WINDOW:, :].astype(BF16))
-    x_out[:, 2 * TILE :] = mm(chosen, dv[WINDOW:, :].astype(BF16))
-
-
-def far_kernel(
-    bias_ref, grads, queries, keys, values, tail_keys, tail_values, slots, tail_slots, k_in, v_in, x_in,
-    sent_out, x_out, kt, dk, dv, dqt,
-):
-    bias = bias_ref[0]
+    shard = shard_ref[0]
+    bias = jnp.where(shard > 0, 0.0, -1e30).astype(F32)
+    slots = index[:, :REACH] - shard * PATCH_DEV
     for t in range(2):
-        kt[t] = tail_keys[t * TILE : (t + 1) * TILE, :].T
+        kt[t] = packed[t * TILE : (t + 1) * TILE, :].T
         kt[2 + t] = keys[t * TILE : (t + 1) * TILE, :].T
-    all_keys = tiles_of(tail_keys, 0, 2) + tiles_of(keys, 0, 2)
-    all_values = tiles_of(tail_values, 0, 2) + tiles_of(values, 0, 2)
-    dk[WINDOW:, :] = k_in[...]
-    dv[WINDOW:, :] = v_in[...]
+    all_keys = tiles_of(packed, 0, 2) + tiles_of(keys, 0, 2)
+    all_values = tiles_of(packed, 2, 2) + tiles_of(values, 0, 2)
     for n in range(2):
         rows = slice(n * TILE, (n + 1) * TILE)
         d_query_t, d_key, d_value = attend(
@@ -136,27 +164,43 @@
             [kt[n + t] for t in range(3)],
             (bias, bias if n == 0 else None, None),
         )
-        dqt[:, n * TILE : (n + 1) * TILE] = d_query_t
-        for t in range(3):
-            at = slice((n + t) * TILE, (n + t + 1) * TILE)
-            if n == 0 and t < 2:
-                dk[at, :] = d_key[t]
-                dv[at, :] = d_value[t]
-            else:
-                dk[at, :] += d_key[t]
-                dv[at, :] += d_value[t]
-    before = one_hot(tail_slots[...], 0, PATCH_DEV)
-    near = one_hot(slots[:, :REACH], -PATCH_DEV, PATCH_DEV)
-    edge = slice(WINDOW, WINDOW + REACH)
-    for place, total in ((0, dk), (PATCH_DEV, dv)):
-        sent_out[place : place + PATCH_DEV, :] = (
-            mm(before, total[:WINDOW, :].astype(BF16)) + mm(near, total[edge, :].astype(BF16))
+        q_out[:, rows] = d_query_t
+        place_sums(n, d_key, d_value, dk, dv, (n == 0, n == 0, True))
+    k_out[...] = dk[WINDOW:, :].astype(BF16)
+    v_out[...] = dv[WINDOW:, :].astype(BF16)
+    tail = packed[2 * WINDOW :, :].astype(F32).astype(jnp.int32)
+    before = jnp.concatenate([one_hot(tail[n : n + 1], 0, PATCH_DEV) for n in range(2)], 1)
+    own = one_hot(slots, -REACH, REACH)
+    low = PATCH_DEV - REACH
+    for n, (total, out) in enumerate(((dk, k_out), (dv, v_out))):
+        place = n * PATCH_DEV
+        part = mm(before, total[:WINDOW, :].astype(BF16))
+        sent_out[place : place + low, :] = part[:low].astype(BF16)
+        sent_out[place + low : place + PATCH_DEV, :] = (
+            part[low:] + mm(own, out[:REACH, :]) + near[:, n * TILE : (n + 1) * TILE]
         ).astype(BF16)
-    sent_out[2 * PATCH_DEV :, :] = mm_t(near[PATCH_DEV - REACH :], dqt[:, :REACH]).astype(BF16)
-    chosen = one_hot(slots[:, :WINDOW], 0, PATCH_DEV)
-    x_out[:, :TILE] = x_in[:, :TILE] + mm_t(chosen, dqt[...])
-    x_out[:, TILE : 2 * TILE] = x_in[:, TILE : 2 * TILE] + mm(chosen, dk[WINDOW:, :].astype(BF16))
-    x_out[:, 2 * TILE :] = x_in[:, 2 * TILE :] + mm(chosen, dv[WINDOW:, :].astype(BF16))
+    sent_out[2 * PATCH_DEV :, :] = mm_t(own, q_out[:, :REACH]).astype(BF16)
+
+
+def last_kernel(shard_ref, grads, queries, keys, values, index, k_in, v_in, q_in, x_in, x_out):
+    rows = slice(3 * TILE, 4 * TILE)
+    d_query_t, d_key, d_value = attend(
+        queries[rows, :],
+        grads[rows, :],
+        tiles_of(keys, 1),
+        tiles_of(values, 1),
+        [keys[t * TILE : (t + 1) * TILE, :].T for t in range(1, 4)],
+        (None, None, None),
+    )
+    chosen = one_hot(index[...] - shard_ref[0] * PATCH_DEV, 0, PATCH_DEV)
+    first, later = chosen[:, :WINDOW], chosen[:, TILE:]
+    x_out[:, :TILE] = (
+        x_in[:, :TILE] + mm_t(first, q_in[...]) + mm_t(chosen[:, 3 * TILE :], d_query_t)
+    )
+    for n, (early, parts) in enumerate(((k_in, d_key), (v_in, d_value))):
+        at = slice((n + 1) * TILE, (n + 2) * TILE)
+        late = jnp.concatenate([d.astype(BF16) for d in parts], 0)
+        x_out[:, at] = x_in[:, at] + mm(first, early[...]) + mm(later, late)
 
 
 def project_kernel(x_in, arrived, w_query, w_key, w_value, first_out, second_out):
@@ -180,16 +224,18 @@
         out[place : place + half, :] = mm(total, unpatch[...]).astype(BF16)
 
 
-def call(kernel, shapes, args, scratch=(), smem=0, flops=0):
-    specs = [pl.BlockSpec(memory_space=pltpu.SMEM)] * smem
-    specs += [pl.BlockSpec(memory_space=pltpu.VMEM)] * (len(args) - smem)
+def call(kernel, shapes, args, scratch=(), flops=0, vmem=32, whole=()):
+    specs = []
+    for n, arg in enumerate(args):
+        space = pltpu.SMEM if arg.shape == (1,) else pl.ANY if n in whole else pltpu.VMEM
+        specs.append(pl.BlockSpec(memory_space=space))
     return pl.pallas_call(
         kernel,
         out_shape=[jax.ShapeDtypeStruct(*shape) for shape in shapes],
         in_specs=specs,
         out_specs=[pl.BlockSpec(memory_space=pltpu.VMEM)] * len(shapes),
         scratch_shapes=list(scratch),
-        compiler_params=pltpu.CompilerParams(vmem_limit_bytes=40 * 1024 * 1024),
+        compiler_params=pltpu.CompilerParams(vmem_limit_bytes=vmem * 1024 * 1024),
         cost_estimate=pl.CostEstimate(flops=flops, bytes_accessed=0, transcendentals=0),
     )(*args)
 
@@ -201,43 +247,48 @@
     count = lax.axis_size("seq")
     onward = [(n, n + 1) for n in range(count - 1)]
     back = [(n + 1, n) for n in range(count - 1)]
-    bytes_dev = queries.shape[0]
-    tail = bytes_dev - WINDOW
-    tail_keys = lax.ppermute(byte_keys[tail:], "seq", onward)
-    tail_values = lax.ppermute(byte_values[tail:], "seq", onward)
-    slots = (patch_index - shard * PATCH_DEV)[None, :]
-    tail_slots = lax.ppermute(slots[:, tail:], "seq", onward)
-    bias = jnp.where(shard > 0, 0.0, -1e30).astype(F32)[None]
-
-    grads, k_part, v_part, x_part = call(
+    place = shard.astype(jnp.int32)[None]
+    index = patch_index[None, :]
+    packed = call(
+        pack_kernel,
+        [((2 * WINDOW + 16, 256), BF16)],
+        (place, byte_keys, byte_values, index),
+        [pltpu.SemaphoreType.DMA((2,))],
+        flops=10**6,
+        vmem=60,
+        whole=(1, 2),
+    )[0]
+    packed = lax.ppermute(packed, "seq", onward)
+    grads = call(
+        heads_kernel,
+        [((1024, 256), BF16)],
+        (d_output, w_out),
+        [pltpu.VMEM((1024, 1024), BF16), pltpu.VMEM((256, 1024), BF16), pltpu.SemaphoreType.DMA((3,))],
+        flops=8 * 10**9,
+        vmem=58,
+        whole=(0, 1),
+    )[0]
+    own = (place, grads, queries, byte_keys, byte_values)
+    near, x_near = call(
         near_kernel,
-        [((WINDOW, 256), BF16), ((WINDOW, 256), F32), ((WINDOW, 256), F32), ((PATCH_DEV, 768), F32)],
-        (d_output, w_out, queries, byte_keys, byte_values, slots),
-        [
-            pltpu.VMEM((4, 256, TILE), BF16),
-            pltpu.VMEM((1024, 256), F32),
-            pltpu.VMEM((1024, 256), F32),
-            pltpu.VMEM((256, 512), BF16),
-        ],
+        [((REACH, 512), F32), ((PATCH_DEV, 768), F32)],
+        (*own, index),
         flops=8 * 10**9,
     )
-    sent, x_own = call(
+    sent, k_part, v_part, q_part = call(
         far_kernel,
-        [((2 * PATCH_DEV + REACH, 256), BF16), ((PATCH_DEV, 768), F32)],
-        (
-            bias, grads, queries, byte_keys, byte_values, tail_keys, tail_values, slots, tail_slots,
-            k_part, v_part, x_part,
-        ),
-        [
-            pltpu.VMEM((4, 256, TILE), BF16),
-            pltpu.VMEM((1024, 256), F32),
-            pltpu.VMEM((1024, 256), F32),
-            pltpu.VMEM((256, 512), BF16),
-        ],
-        smem=1,
+        [((2 * PATCH_DEV + REACH, 256), BF16), ((WINDOW, 256), BF16), ((WINDOW, 256), BF16), ((256, WINDOW), BF16)],
+        (*own, packed, index, near),
+        [pltpu.VMEM((4, 256, TILE), BF16), pltpu.VMEM((1024, 256), F32), pltpu.VMEM((1024, 256), F32)],
         flops=8 * 10**9,
     )
     arrived = lax.ppermute(sent, "seq", back)
+    x_own = call(
+        last_kernel,
+        [((PATCH_DEV, 768), F32)],
+        (*own, index, k_part, v_part, q_part, x_near),
+        flops=8 * 10**9,
+    )[0]
     a, b = call(
         project_kernel,
         [((PATCH_DEV // 2, 1024), BF16)] * 2,

time: 67.5 us -> 52.3 us (0.77)
  local copies, waits for them, and re-layouts: 12.6 us -> 1.09 us
  Pallas kernels: 16 us -> 21.9 us
  starting transfers between devices: 18.8 us -> 14 us
  waiting for transfers between devices: 18.6 us -> 14.8 us
  other arithmetic: 0.82 us -> 0.13 us
    unnamed x32 -> x18, local copies, waits for them, and re-layouts: 9.25 us -> 1.09 us
    pallas_call x4 -> x7, Pallas kernels: 16 us -> 21.9 us  [call(): pl.pallas_call(kernel, out_shape=[jax.ShapeDtypeStruct(*shape) for shape...]
    ppermute x3 -> x1, starting transfers between devices: 10.6 us -> 5.36 us  [on_device(): packed = lax.ppermute(packed, 'seq', onward)]
    ppermute x1, waiting for transfers between devices: 9.79 us -> 5.9 us  [on_device(): arrived = lax.ppermute(sent, 'seq', back)]
    slice x3 -> x0, local copies, waits for them, and re-layouts: 3.33 us -> none  [the longest x1 1.66 us: on_device(): tail_values = lax.ppermute(byte_values[tail:], 'seq', onward)]
    sub x1 -> x0, other arithmetic: 0.69 us -> none  [on_device(): slots = (patch_index - shard * PATCH_DEV)[None, :]]
  transfers between devices with their start and end apart: 8 -> 6, of which waited for: 5 -> 5; matrix products, arithmetic and copies ran while one was open for 5% -> 0% of each run, Pallas kernels for 11% -> 21%
where the time goes in v2:
time: 52.3 us; the launch traced here: 52.1 us
  Pallas kernels  21.9 us (42%)
  waiting for transfers between devices  14.8 us (28%)
  starting transfers between devices  14 us (27%)
  local copies, waits for them, and re-layouts  1.09 us (2%)
    pallas_call x7, Pallas kernels, call(): pl.pallas_call(kernel, out_shape=[jax.ShapeDtypeStruct(*shape) for shape...  21.9 us
    ppermute x1, waiting for transfers between devices, on_device(): arrived = lax.ppermute(sent, 'seq', back)  5.9 us
    ppermute x1, starting transfers between devices, on_device(): packed = lax.ppermute(packed, 'seq', onward)  5.36 us
    ppermute x2, waiting for transfers between devices, on_device(): a_in, b_in = (lax.ppermute(a, 'mp', around), lax.ppermute(b, 'mp', across))  4.9 us
    ppermute x2, waiting for transfers between devices, on_device(): a_in, b_in = (lax.ppermute(a, 'mp', across), lax.ppermute(b, 'mp', around))  4.01 us
    ppermute x2, starting transfers between devices, on_device(): a_in, b_in = (lax.ppermute(a, 'mp', across), lax.ppermute(b, 'mp', around))  3.29 us
    ppermute x2, starting transfers between devices, on_device(): a_in, b_in = (lax.ppermute(a, 'mp', around), lax.ppermute(b, 'mp', across))  3.23 us
    ppermute x1, starting transfers between devices, on_device(): arrived = lax.ppermute(sent, 'seq', back)  2.1 us
  transfers between devices with their start and end apart: 6, of which 5 were waited for; matrix products, arithmetic and copies ran while one was open for 0% of the time, Pallas kernels for 21%

profile of v2, /device:TPU:103, one launch (start us, length us, event | category | flops | bytes accessed | tf_op | source)
XLA Modules:
  0.0 52.1 jit_solution(10727169628299707867)
XLA Ops:
  0.0 2.5 %shard_map.101 = bf16[1040,256]{1,0:T(8,128)(2,1)} custom-call(s32[1]{0:T(128)} %bitcast.shard_ref, bf16[1024,256]{1,0:T(8,128)(2,1)} %keys.7, bf16[1024,256]{1,0:T(8,128)(2,1)} %values.7, s32[1,1024]{1,0:T(1,128)} %bitcast.2), custom_call_target="tpu_custom_call" | custom-call | flops 1000000 | tf_op jit(solution)/shard_map/pallas_call | solution.py:232
  2.5 0.0 copy-start.1
  2.6 0.0 copy-start.2
  2.6 0.0 copy-start.6
  2.6 0.0 copy-start.7
  2.6 5.4 %collective-permute-start = (bf16[1040,256]{1,0:T(8,128)(2,1)}, bf16[1040,256]{1,0:T(8,128)(2,1)S(1)}, u32[]{:S(2)}, u32[]{:S(2)}) collective-permute-start(bf16[1040,256]{1,0:T(8,128)(2,1)} %shard_map.101), channel_id=1, source_target_pairs={{0,4},{4,8},{8,12},{12,16},{16,20},{20,24},{24,28},{28,32},{32,36}... | collective-permute-start | bytes 1597448 | tf_op jit(solution)/shard_map/ppermute | solution.py:261
  8.0 3.7 %shard_map.100.grads = bf16[1024,256]{1,0:T(8,128)(2,1)} custom-call(bf16[1024,1024]{1,0:T(8,128)(2,1)} %d_output_hbm.1, bf16[256,1024]{1,0:T(8,128)(2,1)} %w_out_hbm.1), custom_call_target="tpu_custom_call" | custom-call | flops 8000000000 | tf_op jit(solution)/shard_map/pallas_call | solution.py:232
  11.6 0.0 copy-done.1
  11.6 0.0 copy-done.2
  11.7 0.0 copy-done.6
  11.7 0.0 copy-done.7
  11.7 0.0 copy-start.8
  11.7 1.0 %copy-done.8 = bf16[1024,256]{1,0:T(8,128)(2,1)S(1)} copy-done((bf16[1024,256]{1,0:T(8,128)(2,1)S(1)}, bf16[1024,256]{1,0:T(8,128)(2,1)}, u32[]{:S(2)}) %copy-start.8) | copy-done | bytes 524312
  12.7 3.6 %shard_map.102 = (f32[128,512]{1,0:T(8,128)S(1)}, f32[256,768]{1,0:T(8,128)S(1)}) custom-call(s32[1]{0:T(128)} %bitcast.shard_ref, bf16[1024,256]{1,0:T(8,128)(2,1)S(1)} %copy-done.8, bf16[1024,256]{1,0:T(8,128)(2,1)S(1)} %copy-done.7, bf16[1024,256]{1,0:T(8,128)(2,1)S(1)} %copy-done.1, bf16[1024,256]{1,0:T(8,128)(2,1)S(1)} %copy-done.2, s32[1,1024]{1,0:T(1,128)S(1)} %bitcast.3), custom_call_target="tpu_custom_call" | custom-call | flops 8000000000 | tf_op jit(solution)/shard_map/pallas_call | solution.py:232
  16.3 0.0 collective-permute-done.packed
  16.3 6.3 %shard_map.103 = (bf16[640,256]{1,0:T(8,128)(2,1)S(1)}, bf16[512,256]{1,0:T(8,128)(2,1)S(1)}, bf16[512,256]{1,0:T(8,128)(2,1)S(1)}, bf16[256,512]{1,0:T(8,128)(2,1)S(1)}) custom-call(s32[1]{0:T(128)} %bitcast.shard_ref, bf16[1024,256]{1,0:T(8,128)(2,1)S(1)} %copy-done.8, bf16[1024,256]{1,0:T(8,128)(2,1)S(1)} %copy-done.7, bf16[1024,256]{1,0:T(8,128)(2,1)S(1)} %copy-done.1, ...), custom_call_target="tpu_custom_call" | custom-call | flops 8000000000 | tf_op jit(solution)/shard_map/pallas_call | solution.py:232
  22.6 2.1 %collective-permute-start.1 = (bf16[640,256]{1,0:T(8,128)(2,1)S(1)}, bf16[640,256]{1,0:T(8,128)(2,1)S(1)}, u32[]{:S(2)}, u32[]{:S(2)}) collective-permute-start(bf16[640,256]{1,0:T(8,128)(2,1)S(1)} %get-tuple-element.18), channel_id=1, source_target_pairs={{4,0},{8,4},{12,8},{16,12},{20,16},{24,20},{28,24},{32,28},{36,32}... | collective-permute-start | bytes 983048 | tf_op jit(solution)/shard_map/ppermute | solution.py:285
  24.7 0.0 copy-start.3
  24.8 0.0 copy-start.4
  24.8 0.0 copy-start.5
  24.8 3.6 %shard_map.104.x_in = f32[256,768]{1,0:T(8,128)S(1)} custom-call(s32[1]{0:T(128)} %bitcast.shard_ref, bf16[1024,256]{1,0:T(8,128)(2,1)S(1)} %copy-done.8, bf16[1024,256]{1,0:T(8,128)(2,1)S(1)} %copy-done.7, bf16[1024,256]{1,0:T(8,128)(2,1)S(1)} %copy-done.1, bf16[1024,256]{1,0:T(8,128)(2,1)S(1)} %copy-done.2, s32[1,1024]{1,0:T(1,128)S(1)} %bitcast.5, ...), custom_call_target="tpu_custom_call" | custom-call | flops 8000000000 | tf_op jit(solution)/shard_map/pallas_call | solution.py:232
  28.4 0.0 copy-start
  28.4 5.9 %collective-permute-done.1.arrived = bf16[640,256]{1,0:T(8,128)(2,1)S(1)} collective-permute-done((bf16[640,256]{1,0:T(8,128)(2,1)S(1)}, bf16[640,256]{1,0:T(8,128)(2,1)S(1)}, u32[]{:S(2)}, u32[]{:S(2)}) %collective-permute-start.1) | collective-permute-done | bytes 327712 | tf_op jit(solution)/shard_map/ppermute | solution.py:285
  34.4 0.0 copy-done.3
  34.4 0.0 copy-done.4
  34.4 0.0 copy-done.5
  34.4 0.6 %shard_map.105 = (bf16[128,1024]{1,0:T(8,128)(2,1)S(1)}, bf16[128,1024]{1,0:T(8,128)(2,1)S(1)}) custom-call(f32[256,768]{1,0:T(8,128)S(1)} %shard_map.104.x_in, bf16[640,256]{1,0:T(8,128)(2,1)S(1)} %collective-permute-done.1.arrived, bf16[1024,256]{1,0:T(8,128)(2,1)S(1)} %copy-done.3, bf16[1024,256]{1,0:T(8,128)(2,1)S(1)} %copy-done.4, ...), custom_call_target="tpu_custom_call" | custom-call | flops 400000000 | tf_op jit(solution)/shard_map/pallas_call | solution.py:232
  35.0 1.4 %collective-permute-start.2 = (bf16[128,1024]{1,0:T(8,128)(2,1)S(1)}, bf16[128,1024]{1,0:T(8,128)(2,1)S(1)}, u32[]{:S(2)}, u32[]{:S(2)}) collective-permute-start(bf16[128,1024]{1,0:T(8,128)(2,1)S(1)} %get-tuple-element.19), channel_id=1, source_target_pairs={{0,1},{1,0},{2,3},{3,2},{4,5},{5,4},{6,7},{7,6},{8,9},{9,8},{10,11... | collective-permute-start | bytes 786440 | tf_op jit(solution)/shard_map/ppermute | solution.py:304
  36.4 1.9 %collective-permute-start.4 = (bf16[128,1024]{1,0:T(8,128)(2,1)S(1)}, bf16[128,1024]{1,0:T(8,128)(2,1)S(1)}, u32[]{:S(2)}, u32[]{:S(2)}) collective-permute-start(bf16[128,1024]{1,0:T(8,128)(2,1)S(1)} %get-tuple-element.20), channel_id=1, source_target_pairs={{0,3},{3,0},{1,2},{2,1},{4,7},{7,4},{5,6},{6,5},{8,11},{11,8},{9,1... | collective-permute-start | bytes 786440 | tf_op jit(solution)/shard_map/ppermute | solution.py:304
  38.3 2.3 %collective-permute-done.2 = bf16[128,1024]{1,0:T(8,128)(2,1)S(1)} collective-permute-done((bf16[128,1024]{1,0:T(8,128)(2,1)S(1)}, bf16[128,1024]{1,0:T(8,128)(2,1)S(1)}, u32[]{:S(2)}, u32[]{:S(2)}) %collective-permute-start.2) | collective-permute-done | bytes 262176 | tf_op jit(solution)/shard_map/ppermute | solution.py:304
  40.6 0.1 add_convert_fusion.1.a
  40.7 2.8 %collective-permute-start.3 = (bf16[128,1024]{1,0:T(8,128)(2,1)S(1)}, bf16[128,1024]{1,0:T(8,128)(2,1)S(1)}, u32[]{:S(2)}, u32[]{:S(2)}) collective-permute-start(bf16[128,1024]{1,0:T(8,128)(2,1)S(1)} %add_convert_fusion.1.a), channel_id=1, source_target_pairs={{0,3},{3,0},{1,2},{2,1},{4,7},{7,4},{5,6},{6,5},{8,11},{11,8},{9,1... | collective-permute-start | bytes 786440 | tf_op jit(solution)/shard_map/ppermute | solution.py:306
  43.5 1.7 %collective-permute-done.4 = bf16[128,1024]{1,0:T(8,128)(2,1)S(1)} collective-permute-done((bf16[128,1024]{1,0:T(8,128)(2,1)S(1)}, bf16[128,1024]{1,0:T(8,128)(2,1)S(1)}, u32[]{:S(2)}, u32[]{:S(2)}) %collective-permute-start.4) | collective-permute-done | bytes 262176 | tf_op jit(solution)/shard_map/ppermute | solution.py:304
  45.2 0.1 add_convert_fusion.b
  45.3 0.4 collective-permute-start.5
  45.7 2.3 %collective-permute-done.3.a_in = bf16[128,1024]{1,0:T(8,128)(2,1)S(1)} collective-permute-done((bf16[128,1024]{1,0:T(8,128)(2,1)S(1)}, bf16[128,1024]{1,0:T(8,128)(2,1)S(1)}, u32[]{:S(2)}, u32[]{:S(2)}) %collective-permute-start.3) | collective-permute-done | bytes 262176 | tf_op jit(solution)/shard_map/ppermute | solution.py:306
  48.0 2.6 %collective-permute-done.5.b_in = bf16[128,1024]{1,0:T(8,128)(2,1)S(1)} collective-permute-done((bf16[128,1024]{1,0:T(8,128)(2,1)S(1)}, bf16[128,1024]{1,0:T(8,128)(2,1)S(1)}, u32[]{:S(2)}, u32[]{:S(2)}) %collective-permute-start.5) | collective-permute-done | bytes 262176 | tf_op jit(solution)/shard_map/ppermute | solution.py:306
  50.6 0.0 copy-done
  50.6 1.5 %shard_map.106 = bf16[256,1024]{1,0:T(8,128)(2,1)} custom-call(bf16[128,1024]{1,0:T(8,128)(2,1)S(1)} %add_convert_fusion.1.a, bf16[128,1024]{1,0:T(8,128)(2,1)S(1)} %collective-permute-done.3.a_in, bf16[128,1024]{1,0:T(8,128)(2,1)S(1)} %add_convert_fusion.b, bf16[128,1024]{1,0:T(8,128)(2,1)S(1)} %collective-permute-done.5.b_in, bf16[1024,1024]{1,0:T(8,128)(2,1)S(1)} %copy-done), custom_call_target="tpu_custom_call" | custom-call | flops 500000000 | tf_op jit(solution)/shard_map/pallas_call | solution.py:232
Async XLA Ops:
  2.5 9.1 %copy-start.1 = (bf16[1024,256]{1,0:T(8,128)(2,1)S(1)}, bf16[1024,256]{1,0:T(8,128)(2,1)}, u32[]{:S(2)}) copy-start(bf16[1024,256]{1,0:T(8,128)(2,1)} %keys.7) | copy-start | bytes 1572868
  2.6 9.1 %copy-start.2 = (bf16[1024,256]{1,0:T(8,128)(2,1)S(1)}, bf16[1024,256]{1,0:T(8,128)(2,1)}, u32[]{:S(2)}) copy-start(bf16[1024,256]{1,0:T(8,128)(2,1)} %values.7) | copy-start | bytes 1572868
  2.6 9.1 %copy-start.6 = (s32[1024]{0:T(1024)S(1)}, s32[1024]{0:T(1024)}, u32[]{:S(2)}) copy-start(s32[1024]{0:T(1024)} %param.18) | copy-start | bytes 12292
  2.6 9.1 %copy-start.7 = (bf16[1024,256]{1,0:T(8,128)(2,1)S(1)}, bf16[1024,256]{1,0:T(8,128)(2,1)}, u32[]{:S(2)}) copy-start(bf16[1024,256]{1,0:T(8,128)(2,1)} %queries.5) | copy-start | bytes 1572868
  2.6 13.7 %collective-permute-start = (bf16[1040,256]{1,0:T(8,128)(2,1)}, bf16[1040,256]{1,0:T(8,128)(2,1)S(1)}, u32[]{:S(2)}, u32[]{:S(2)}) collective-permute-start(bf16[1040,256]{1,0:T(8,128)(2,1)} %shard_map.101), channel_id=1, source_target_pairs={{0,4},{4,8},{8,12},{12,16},{16,20},{20,24},{24,28},{28,32},{32,36}... | collective-permute-start | bytes 1597448 | tf_op jit(solution)/shard_map/ppermute | solution.py:261
  11.7 1.0 %copy-start.8 = (bf16[1024,256]{1,0:T(8,128)(2,1)S(1)}, bf16[1024,256]{1,0:T(8,128)(2,1)}, u32[]{:S(2)}) copy-start(bf16[1024,256]{1,0:T(8,128)(2,1)} %shard_map.100.grads) | copy-start | bytes 1572868
  22.6 11.7 %collective-permute-start.1 = (bf16[640,256]{1,0:T(8,128)(2,1)S(1)}, bf16[640,256]{1,0:T(8,128)(2,1)S(1)}, u32[]{:S(2)}, u32[]{:S(2)}) collective-permute-start(bf16[640,256]{1,0:T(8,128)(2,1)S(1)} %get-tuple-element.18), channel_id=1, source_target_pairs={{4,0},{8,4},{12,8},{16,12},{20,16},{24,20},{28,24},{32,28},{36,32}... | collective-permute-start | bytes 983048 | tf_op jit(solution)/shard_map/ppermute | solution.py:285
  24.7 9.6 %copy-start.3 = (bf16[1024,256]{1,0:T(8,128)(2,1)S(1)}, bf16[1024,256]{1,0:T(8,128)(2,1)}, u32[]{:S(2)}) copy-start(bf16[1024,256]{1,0:T(8,128)(2,1)} %w_query.1) | copy-start | bytes 1572868
  24.8 9.6 %copy-start.4 = (bf16[1024,256]{1,0:T(8,128)(2,1)S(1)}, bf16[1024,256]{1,0:T(8,128)(2,1)}, u32[]{:S(2)}) copy-start(bf16[1024,256]{1,0:T(8,128)(2,1)} %w_key.1) | copy-start | bytes 1572868
  24.8 9.6 %copy-start.5 = (bf16[1024,256]{1,0:T(8,128)(2,1)S(1)}, bf16[1024,256]{1,0:T(8,128)(2,1)}, u32[]{:S(2)}) copy-start(bf16[1024,256]{1,0:T(8,128)(2,1)} %w_value.1) | copy-start | bytes 1572868
  28.4 22.1 %copy-start = (bf16[1024,1024]{1,0:T(8,128)(2,1)S(1)}, bf16[1024,1024]{1,0:T(8,128)(2,1)}, u32[]{:S(2)}) copy-start(bf16[1024,1024]{1,0:T(8,128)(2,1)} %unpatch.1) | copy-start | bytes 6291460
  35.0 5.6 %collective-permute-start.2 = (bf16[128,1024]{1,0:T(8,128)(2,1)S(1)}, bf16[128,1024]{1,0:T(8,128)(2,1)S(1)}, u32[]{:S(2)}, u32[]{:S(2)}) collective-permute-start(bf16[128,1024]{1,0:T(8,128)(2,1)S(1)} %get-tuple-element.19), channel_id=1, source_target_pairs={{0,1},{1,0},{2,3},{3,2},{4,5},{5,4},{6,7},{7,6},{8,9},{9,8},{10,11... | collective-permute-start | bytes 786440 | tf_op jit(solution)/shard_map/ppermute | solution.py:304
  36.4 8.8 %collective-permute-start.4 = (bf16[128,1024]{1,0:T(8,128)(2,1)S(1)}, bf16[128,1024]{1,0:T(8,128)(2,1)S(1)}, u32[]{:S(2)}, u32[]{:S(2)}) collective-permute-start(bf16[128,1024]{1,0:T(8,128)(2,1)S(1)} %get-tuple-element.20), channel_id=1, source_target_pairs={{0,3},{3,0},{1,2},{2,1},{4,7},{7,4},{5,6},{6,5},{8,11},{11,8},{9,1... | collective-permute-start | bytes 786440 | tf_op jit(solution)/shard_map/ppermute | solution.py:304
  40.7 7.3 %collective-permute-start.3 = (bf16[128,1024]{1,0:T(8,128)(2,1)S(1)}, bf16[128,1024]{1,0:T(8,128)(2,1)S(1)}, u32[]{:S(2)}, u32[]{:S(2)}) collective-permute-start(bf16[128,1024]{1,0:T(8,128)(2,1)S(1)} %add_convert_fusion.1.a), channel_id=1, source_target_pairs={{0,3},{3,0},{1,2},{2,1},{4,7},{7,4},{5,6},{6,5},{8,11},{11,8},{9,1... | collective-permute-start | bytes 786440 | tf_op jit(solution)/shard_map/ppermute | solution.py:306
  45.3 5.3 %collective-permute-start.5 = (bf16[128,1024]{1,0:T(8,128)(2,1)S(1)}, bf16[128,1024]{1,0:T(8,128)(2,1)S(1)}, u32[]{:S(2)}, u32[]{:S(2)}) collective-permute-start(bf16[128,1024]{1,0:T(8,128)(2,1)S(1)} %add_convert_fusion.b), channel_id=1, source_target_pairs={{0,1},{1,0},{2,3},{3,2},{4,5},{5,4},{6,7},{7,6},{8,9},{9,8},{10,11... | collective-permute-start | bytes 786440 | tf_op jit(solution)/shard_map/ppermute | solution.py:306

commit v3 on v2

--- a/solution.py
+++ b/solution.py
@@ -12,6 +12,7 @@
 PATCH_DEV = 256
 TILE = 256
 REACH = 128
+STRIP = 32
 F32 = jnp.float32
 BF16 = jnp.bfloat16
 
@@ -34,50 +35,160 @@
     return jnp.where(places == slots, 1.0, 0.0).astype(BF16)
 
 
-def attend(query, grad, keys, values, keys_t, bias):
-    key_row = lax.broadcasted_iota(jnp.int32, (TILE, TILE), 0)
-    query_col = lax.broadcasted_iota(jnp.int32, (TILE, TILE), 1)
-    late = key_row <= query_col
-    nil = jnp.zeros((TILE, TILE), BF16)
-    query = query * jnp.asarray(HS**-0.5, BF16)
-    d_query, d_key, d_value = [], [None] * 3, [None] * 3
-
-    def added(total, term):
-        return term if total is None else total + term
-
-    for h, (q, g) in enumerate(zip(head_parts(query), head_parts(grad))):
-        s = [mm_t(k, q) for k in keys]
-        s = [x if b is None else x + b for x, b in zip(s, bias)]
-        dp = [mm_t(v, g) for v in values]
-        s_edge, s_mid = jnp.where(late, s[2], s[0]), s[1]
-        dp_edge, dp_mid = jnp.where(late, dp[2], dp[0]), dp[1]
-        peak = jnp.maximum(
-            jnp.max(s_edge, axis=0, keepdims=True), jnp.max(s_mid, axis=0, keepdims=True)
-        )
-        e_edge, e_mid = jnp.exp(s_edge - peak), jnp.exp(s_mid - peak)
-        total = jnp.sum(e_edge, axis=0, keepdims=True) + jnp.sum(e_mid, axis=0, keepdims=True)
-        inverse = 1.0 / total
-        row_dot = inverse * (
-            jnp.sum(e_edge * dp_edge, axis=0, keepdims=True)
-            + jnp.sum(e_mid * dp_mid, axis=0, keepdims=True)
-        )
-        p_edge, p_mid = e_edge * inverse, e_mid * inverse
-        ds_edge = (p_edge * (dp_edge - row_dot)).astype(BF16)
-        ds_mid = (p_mid * (dp_mid - row_dot)).astype(BF16)
-        p_edge, p_mid = p_edge.astype(BF16), p_mid.astype(BF16)
-        ds = [jnp.where(late, nil, ds_edge), ds_mid, jnp.where(late, ds_edge, nil)]
-        p = [jnp.where(late, nil, p_edge), p_mid, jnp.where(late, p_edge, nil)]
+def rows_of_8(x, reduce):
+    return reduce(x.reshape(x.shape[0] // 8, 8, x.shape[1]), 0)
+
+
+def joined(total, term, op=jnp.add):
+    return term if total is None else op(total, term)
+
+
+class Unit:
+    def __init__(self, keys, values, keys_t, query, grad, far_bias, mid_bias):
+        self.keys, self.values, self.keys_t = keys, values, keys_t
+        self.query, self.grad = query, grad
+        self.far_bias, self.mid_bias = far_bias, mid_bias
+        self.s, self.dp = [None] * 3, [None] * 3
+        self.d_key, self.d_value = [None] * 3, [None] * 3
+        self.strips, self.low = {}, {}
+        self.peak = self.total = self.dot = None
+
+    def score_steps(self):
+        def step(into, t, a, b):
+            into[t] = mm_t(a, b)
+
+        steps = [functools.partial(step, self.s, t, self.keys[t], self.query) for t in (0, 2, 1)]
+        return steps + [functools.partial(step, self.dp, t, self.values[t], self.grad) for t in (0, 2, 1)]
+
+    def back_steps(self):
+        def step(into, t, a, b):
+            into[t] = mm(a[t], b)
+
+        def query_step():
+            self.d_query_t = mm(self.keys_t, jnp.concatenate(self.ds, 0))
+
+        steps = []
         for t in range(3):
-            d_key[t] = added(d_key[t], mm(ds[t], q))
-            d_value[t] = added(d_value[t], mm(p[t], g))
-        rows = slice(h * HS, (h + 1) * HS)
-        d_query.append(sum(mm(keys_t[t][rows], ds[t]) for t in range(3)))
-    d_query_t = jnp.concatenate(d_query, 0) * HS**-0.5
-    return d_query_t.astype(BF16), d_key, d_value
+            steps.append(functools.partial(step, self.d_key, t, self.ds, self.query))
+            steps.append(functools.partial(step, self.d_value, t, self.p, self.grad))
+        return steps[:3] + [query_step] + steps[3:]
+
+    def inside(self, row):
+        shape = (STRIP, TILE // 2)
+        ahead = lax.broadcasted_iota(jnp.int32, shape, 1) - lax.broadcasted_iota(jnp.int32, shape, 0)
+        return ahead >= row % (TILE // 2)
+
+    def edge(self, parts, row, bias=None):
+        half = TILE // 2
+        far, near = parts[0][row : row + STRIP], parts[2][row : row + STRIP]
+        if bias is not None:
+            far = far + bias
+        if row < half:
+            left, right = jnp.where(self.inside(row), near[:, :half], far[:, :half]), near[:, half:]
+        else:
+            left, right = far[:, :half], jnp.where(self.inside(row), near[:, half:], far[:, half:])
+        return jnp.concatenate([left, right], 1)
+
+    def parted(self, x, row):
+        half = TILE // 2
+        left, right = x[:, :half], x[:, half:]
+        nil = jnp.zeros_like(left)
+        ok = self.inside(row)
+        if row < half:
+            near, far = [jnp.where(ok, left, nil), right], [jnp.where(ok, nil, left), nil]
+        else:
+            near, far = [nil, jnp.where(ok, right, nil)], [left, jnp.where(ok, nil, right)]
+        return jnp.concatenate(far, 1), jnp.concatenate(near, 1)
+
+    def strip_of(self, parts, mid, row):
+        return parts[1][row : row + STRIP] if mid else self.edge(parts, row)
+
+    def soft_steps(self):
+        places = [(mid, row) for mid in (False, True) for row in range(0, TILE, STRIP)]
+
+        def peak_step(mid, row):
+            if mid:
+                x = self.s[1][row : row + STRIP]
+                x = x if self.mid_bias is None else x + self.mid_bias
+            else:
+                x = self.edge(self.s, row, self.far_bias)
+            self.strips[mid, row] = x
+            self.peak = joined(self.peak, rows_of_8(x, jnp.max), jnp.maximum)
+
+        def peak_end():
+            self.peak = jnp.max(self.peak, axis=0, keepdims=True)
+
+        def exp_step(mid, row):
+            e = jnp.exp(self.strips[mid, row] - self.peak)
+            self.strips[mid, row] = e
+            self.total = joined(self.total, rows_of_8(e, jnp.sum))
+            self.dot = joined(self.dot, rows_of_8(e * self.strip_of(self.dp, mid, row), jnp.sum))
+
+        def exp_end():
+            self.inverse = 1.0 / jnp.sum(self.total, axis=0, keepdims=True)
+            self.row_dot = self.inverse * jnp.sum(self.dot, axis=0, keepdims=True)
+
+        def low_step(mid, row):
+            p = self.strips[mid, row] * self.inverse
+            ds = p * (self.strip_of(self.dp, mid, row) - self.row_dot)
+            for name, x in (("p", p), ("ds", ds)):
+                if mid:
+                    self.low[name, 1, row] = x.astype(BF16)
+                else:
+                    far, near = self.parted(x, row)
+                    self.low[name, 0, row], self.low[name, 2, row] = far.astype(BF16), near.astype(BF16)
+
+        def low_end():
+            self.p, self.ds = (
+                [
+                    jnp.concatenate([self.low[name, t, row] for row in range(0, TILE, STRIP)], 0)
+                    for t in range(3)
+                ]
+                for name in ("p", "ds")
+            )
+
+        steps = []
+        for step, end in ((peak_step, peak_end), (exp_step, exp_end), (low_step, low_end)):
+            steps += [functools.partial(step, *place) for place in places] + [end]
+        return steps
+
+
+def attend(tiles):
+    units = []
+    for query, grad, keys, values, far_bias, mid_bias in tiles:
+        keys_t = jnp.concatenate([k.T for k in keys], 1)
+        q_heads = head_parts(query * jnp.asarray(HS**-0.5, BF16))
+        for h, (q, g) in enumerate(zip(q_heads, head_parts(grad))):
+            units.append(Unit(keys, values, keys_t[h * HS : (h + 1) * HS], q, g, far_bias, mid_bias))
+    for n in range(len(units) + 2):
+        matmuls = units[n - 2].back_steps() if n >= 2 else []
+        matmuls += units[n].score_steps() if n < len(units) else []
+        strips = units[n - 1].soft_steps() if 1 <= n <= len(units) else []
+        done = 0
+        for place, step in enumerate(strips):
+            step()
+            while done < (place + 1) * len(matmuls) // len(strips):
+                matmuls[done]()
+                done += 1
+        for step in matmuls[done:]:
+            step()
+    out = []
+    heads = len(units) // len(tiles)
+    for first in range(0, len(units), heads):
+        own = units[first : first + heads]
+        d_query_t = jnp.concatenate([unit.d_query_t for unit in own], 0) * HS**-0.5
+        d_key = [sum(unit.d_key[t] for unit in own) for t in range(3)]
+        d_value = [sum(unit.d_value[t] for unit in own) for t in range(3)]
+        out.append((d_query_t.astype(BF16), d_key, d_value))
+    return out
 
 
 def tiles_of(ref, first, count=3):
     return [ref[t * TILE : (t + 1) * TILE, :] for t in range(first, first + count)]
+
+
+def whole_low(parts):
+    return jnp.concatenate([part.astype(BF16) for part in parts], 0)
 
 
 def pack_kernel(shard_ref, keys, values, index, packed, sems):
@@ -109,30 +220,13 @@
         grads[rows, :] = mm_t(d_output[rows, :], w_out[...]).astype(BF16)
 
 
-def place_sums(first, d_key, d_value, dk, dv, fresh=(True, True, True)):
-    for t in range(3):
-        at = slice((first + t) * TILE, (first + t + 1) * TILE)
-        if fresh[t]:
-            dk[at, :] = d_key[t]
-            dv[at, :] = d_value[t]
-        else:
-            dk[at, :] += d_key[t]
-            dv[at, :] += d_value[t]
-
-
 def near_kernel(shard_ref, grads, queries, keys, values, index, near_out, x_out):
     rows = slice(2 * TILE, 3 * TILE)
     d_query_t, d_key, d_value = attend(
-        queries[rows, :],
-        grads[rows, :],
-        tiles_of(keys, 0),
-        tiles_of(values, 0),
-        [keys[t * TILE : (t + 1) * TILE, :].T for t in range(3)],
-        (None, None, None),
-    )
+        [(queries[rows, :], grads[rows, :], tiles_of(keys, 0), tiles_of(values, 0), None, None)]
+    )[0]
     slots = index[...] - shard_ref[0] * PATCH_DEV
-    d_key = jnp.concatenate([d.astype(BF16) for d in d_key], 0)
-    d_value = jnp.concatenate([d.astype(BF16) for d in d_value], 0)
+    d_key, d_value = whole_low(d_key), whole_low(d_value)
     before = one_hot(slots[:, :REACH], -REACH, REACH)
     near_out[:, :TILE] = mm(before, d_key[:REACH])
     near_out[:, TILE:] = mm(before, d_value[:REACH])
@@ -144,37 +238,30 @@
 
 def far_kernel(
     shard_ref, grads, queries, keys, values, packed, index, near,
-    sent_out, k_out, v_out, q_out, kt, dk, dv,
+    sent_out, k_out, v_out, q_out,
 ):
     shard = shard_ref[0]
     bias = jnp.where(shard > 0, 0.0, -1e30).astype(F32)
     slots = index[:, :REACH] - shard * PATCH_DEV
-    for t in range(2):
-        kt[t] = packed[t * TILE : (t + 1) * TILE, :].T
-        kt[2 + t] = keys[t * TILE : (t + 1) * TILE, :].T
     all_keys = tiles_of(packed, 0, 2) + tiles_of(keys, 0, 2)
     all_values = tiles_of(packed, 2, 2) + tiles_of(values, 0, 2)
+    tiles = []
     for n in range(2):
         rows = slice(n * TILE, (n + 1) * TILE)
-        d_query_t, d_key, d_value = attend(
-            queries[rows, :],
-            grads[rows, :],
-            all_keys[n : n + 3],
-            all_values[n : n + 3],
-            [kt[n + t] for t in range(3)],
-            (bias, bias if n == 0 else None, None),
+        tiles.append(
+            (queries[rows, :], grads[rows, :], all_keys[n : n + 3], all_values[n : n + 3], bias, None if n else bias)
         )
-        q_out[:, rows] = d_query_t
-        place_sums(n, d_key, d_value, dk, dv, (n == 0, n == 0, True))
-    k_out[...] = dk[WINDOW:, :].astype(BF16)
-    v_out[...] = dv[WINDOW:, :].astype(BF16)
+    (q_first, *first), (q_second, *second) = attend(tiles)
+    q_out[:, :TILE], q_out[:, TILE:] = q_first, q_second
     tail = packed[2 * WINDOW :, :].astype(F32).astype(jnp.int32)
     before = jnp.concatenate([one_hot(tail[n : n + 1], 0, PATCH_DEV) for n in range(2)], 1)
     own = one_hot(slots, -REACH, REACH)
     low = PATCH_DEV - REACH
-    for n, (total, out) in enumerate(((dk, k_out), (dv, v_out))):
+    for n, (a, b, out) in enumerate(zip(first, second, (k_out, v_out))):
         place = n * PATCH_DEV
-        part = mm(before, total[:WINDOW, :].astype(BF16))
+        gone = whole_low([a[0], a[1] + b[0]])
+        out[...] = whole_low([a[2] + b[1], b[2]])
+        part = mm(before, gone)
         sent_out[place : place + low, :] = part[:low].astype(BF16)
         sent_out[place + low : place + PATCH_DEV, :] = (
             part[low:] + mm(own, out[:REACH, :]) + near[:, n * TILE : (n + 1) * TILE]
@@ -185,13 +272,8 @@
 def last_kernel(shard_ref, grads, queries, keys, values, index, k_in, v_in, q_in, x_in, x_out):
     rows = slice(3 * TILE, 4 * TILE)
     d_query_t, d_key, d_value = attend(
-        queries[rows, :],
-        grads[rows, :],
-        tiles_of(keys, 1),
-        tiles_of(values, 1),
-        [keys[t * TILE : (t + 1) * TILE, :].T for t in range(1, 4)],
-        (None, None, None),
-    )
+        [(queries[rows, :], grads[rows, :], tiles_of(keys, 1), tiles_of(values, 1), None, None)]
+    )[0]
     chosen = one_hot(index[...] - shard_ref[0] * PATCH_DEV, 0, PATCH_DEV)
     first, later = chosen[:, :WINDOW], chosen[:, TILE:]
     x_out[:, :TILE] = (
@@ -199,8 +281,7 @@
     )
     for n, (early, parts) in enumerate(((k_in, d_key), (v_in, d_value))):
         at = slice((n + 1) * TILE, (n + 2) * TILE)
-        late = jnp.concatenate([d.astype(BF16) for d in parts], 0)
-        x_out[:, at] = x_in[:, at] + mm(first, early[...]) + mm(later, late)
+        x_out[:, at] = x_in[:, at] + mm(first, early[...]) + mm(later, whole_low(parts))
 
 
 def project_kernel(x_in, arrived, w_query, w_key, w_value, first_out, second_out):
@@ -279,7 +360,6 @@
         far_kernel,
         [((2 * PATCH_DEV + REACH, 256), BF16), ((WINDOW, 256), BF16), ((WINDOW, 256), BF16), ((256, WINDOW), BF16)],
         (*own, packed, index, near),
-        [pltpu.VMEM((4, 256, TILE), BF16), pltpu.VMEM((1024, 256), F32), pltpu.VMEM((1024, 256), F32)],
         flops=8 * 10**9,
     )
     arrived = lax.ppermute(sent, "seq", back)

time: 52.3 us -> 50.5 us (0.966)
  Pallas kernels: 21.9 us -> 19.1 us
  waiting for transfers between devices: 14.8 us -> 15.7 us
    pallas_call x7, Pallas kernels: 21.9 us -> 19.1 us  [call(): pl.pallas_call(kernel, out_shape=[jax.ShapeDtypeStruct(*shape) for shape...]
    ppermute x1, waiting for transfers between devices: 5.9 us -> 6.83 us  [on_device(): arrived = lax.ppermute(sent, 'seq', back)]
  transfers between devices with their start and end apart: 6 -> 6, of which waited for: 5 -> 5; matrix products, arithmetic and copies ran while one was open for 0% -> 0% of each run, Pallas kernels for 21% -> 19%
where the time goes in v3:
time: 50.5 us; the launch traced here: 50.2 us
  Pallas kernels  19.1 us (38%)
  waiting for transfers between devices  15.7 us (31%)
  starting transfers between devices  14 us (28%)
  local copies, waits for them, and re-layouts  1.09 us (2%)
    pallas_call x7, Pallas kernels, call(): pl.pallas_call(kernel, out_shape=[jax.ShapeDtypeStruct(*shape) for shape...  19.1 us
    ppermute x1, waiting for transfers between devices, on_device(): arrived = lax.ppermute(sent, 'seq', back)  6.83 us
    ppermute x1, starting transfers between devices, on_device(): packed = lax.ppermute(packed, 'seq', onward)  5.36 us
    ppermute x2, waiting for transfers between devices, on_device(): a_in, b_in = (lax.ppermute(a, 'mp', around), lax.ppermute(b, 'mp', across))  4.87 us
    ppermute x2, waiting for transfers between devices, on_device(): a_in, b_in = (lax.ppermute(a, 'mp', across), lax.ppermute(b, 'mp', around))  4 us
    ppermute x2, starting transfers between devices, on_device(): a_in, b_in = (lax.ppermute(a, 'mp', across), lax.ppermute(b, 'mp', around))  3.47 us
    ppermute x2, starting transfers between devices, on_device(): a_in, b_in = (lax.ppermute(a, 'mp', around), lax.ppermute(b, 'mp', across))  3.26 us
    ppermute x1, starting transfers between devices, on_device(): arrived = lax.ppermute(sent, 'seq', back)  1.92 us
  transfers between devices with their start and end apart: 6, of which 5 were waited for; matrix products, arithmetic and copies ran while one was open for 0% of the time, Pallas kernels for 19%

profile of v3, /device:TPU:103, one launch (start us, length us, event | category | flops | bytes accessed | tf_op | source)
XLA Modules:
  0.0 50.2 jit_solution(3759301573074943685)
XLA Ops:
  0.0 2.5 %shard_map.101 = bf16[1040,256]{1,0:T(8,128)(2,1)} custom-call(s32[1]{0:T(128)} %bitcast.shard_ref, bf16[1024,256]{1,0:T(8,128)(2,1)} %keys.7, bf16[1024,256]{1,0:T(8,128)(2,1)} %values.7, s32[1,1024]{1,0:T(1,128)} %bitcast.2), custom_call_target="tpu_custom_call" | custom-call | flops 1000000 | tf_op jit(solution)/shard_map/pallas_call | solution.py:313
  2.5 0.0 copy-start.1
  2.6 0.0 copy-start.2
  2.6 0.0 copy-start.6
  2.6 0.0 copy-start.7
  2.6 5.4 %collective-permute-start = (bf16[1040,256]{1,0:T(8,128)(2,1)}, bf16[1040,256]{1,0:T(8,128)(2,1)S(1)}, u32[]{:S(2)}, u32[]{:S(2)}) collective-permute-start(bf16[1040,256]{1,0:T(8,128)(2,1)} %shard_map.101), channel_id=1, source_target_pairs={{0,4},{4,8},{8,12},{12,16},{16,20},{20,24},{24,28},{28,32},{32,36}... | collective-permute-start | bytes 1597448 | tf_op jit(solution)/shard_map/ppermute | solution.py:342
  8.0 3.7 %shard_map.100.grads = bf16[1024,256]{1,0:T(8,128)(2,1)} custom-call(bf16[1024,1024]{1,0:T(8,128)(2,1)} %d_output_hbm.1, bf16[256,1024]{1,0:T(8,128)(2,1)} %w_out_hbm.1), custom_call_target="tpu_custom_call" | custom-call | flops 8000000000 | tf_op jit(solution)/shard_map/pallas_call | solution.py:313
  11.6 0.0 copy-done.1
  11.6 0.0 copy-done.2
  11.7 0.0 copy-done.6
  11.7 0.0 copy-done.7
  11.7 0.0 copy-start.8
  11.7 1.0 %copy-done.8 = bf16[1024,256]{1,0:T(8,128)(2,1)S(1)} copy-done((bf16[1024,256]{1,0:T(8,128)(2,1)S(1)}, bf16[1024,256]{1,0:T(8,128)(2,1)}, u32[]{:S(2)}) %copy-start.8) | copy-done | bytes 524312
  12.7 2.8 %shard_map.102 = (f32[128,512]{1,0:T(8,128)S(1)}, f32[256,768]{1,0:T(8,128)S(1)}) custom-call(s32[1]{0:T(128)} %bitcast.shard_ref, bf16[1024,256]{1,0:T(8,128)(2,1)S(1)} %copy-done.8, bf16[1024,256]{1,0:T(8,128)(2,1)S(1)} %copy-done.7, bf16[1024,256]{1,0:T(8,128)(2,1)S(1)} %copy-done.1, bf16[1024,256]{1,0:T(8,128)(2,1)S(1)} %copy-done.2, s32[1,1024]{1,0:T(1,128)S(1)} %bitcast.3), custom_call_target="tpu_custom_call" | custom-call | flops 8000000000 | tf_op jit(solution)/shard_map/pallas_call | solution.py:313
  15.5 0.0 collective-permute-done.packed
  15.5 5.1 %shard_map.103 = (bf16[640,256]{1,0:T(8,128)(2,1)S(1)}, bf16[512,256]{1,0:T(8,128)(2,1)S(1)}, bf16[512,256]{1,0:T(8,128)(2,1)S(1)}, bf16[256,512]{1,0:T(8,128)(2,1)S(1)}) custom-call(s32[1]{0:T(128)} %bitcast.shard_ref, bf16[1024,256]{1,0:T(8,128)(2,1)S(1)} %copy-done.8, bf16[1024,256]{1,0:T(8,128)(2,1)S(1)} %copy-done.7, bf16[1024,256]{1,0:T(8,128)(2,1)S(1)} %copy-done.1, ...), custom_call_target="tpu_custom_call" | custom-call | flops 8000000000 | tf_op jit(solution)/shard_map/pallas_call | solution.py:313
  20.6 1.9 %collective-permute-start.1 = (bf16[640,256]{1,0:T(8,128)(2,1)S(1)}, bf16[640,256]{1,0:T(8,128)(2,1)S(1)}, u32[]{:S(2)}, u32[]{:S(2)}) collective-permute-start(bf16[640,256]{1,0:T(8,128)(2,1)S(1)} %get-tuple-element.18), channel_id=1, source_target_pairs={{4,0},{8,4},{12,8},{16,12},{20,16},{24,20},{28,24},{32,28},{36,32}... | collective-permute-start | bytes 983048 | tf_op jit(solution)/shard_map/ppermute | solution.py:365
  22.6 0.0 copy-start.3
  22.6 0.0 copy-start.4
  22.6 0.0 copy-start.5
  22.6 2.9 %shard_map.104.x_in = f32[256,768]{1,0:T(8,128)S(1)} custom-call(s32[1]{0:T(128)} %bitcast.shard_ref, bf16[1024,256]{1,0:T(8,128)(2,1)S(1)} %copy-done.8, bf16[1024,256]{1,0:T(8,128)(2,1)S(1)} %copy-done.7, bf16[1024,256]{1,0:T(8,128)(2,1)S(1)} %copy-done.1, bf16[1024,256]{1,0:T(8,128)(2,1)S(1)} %copy-done.2, s32[1,1024]{1,0:T(1,128)S(1)} %bitcast.5, ...), custom_call_target="tpu_custom_call" | custom-call | flops 8000000000 | tf_op jit(solution)/shard_map/pallas_call | solution.py:313
  25.5 0.0 copy-start
  25.5 6.8 %collective-permute-done.1.arrived = bf16[640,256]{1,0:T(8,128)(2,1)S(1)} collective-permute-done((bf16[640,256]{1,0:T(8,128)(2,1)S(1)}, bf16[640,256]{1,0:T(8,128)(2,1)S(1)}, u32[]{:S(2)}, u32[]{:S(2)}) %collective-permute-start.1) | collective-permute-done | bytes 327712 | tf_op jit(solution)/shard_map/ppermute | solution.py:365
  32.3 0.0 copy-done.3
  32.4 0.0 copy-done.4
  32.4 0.0 copy-done.5
  32.4 0.6 %shard_map.105 = (bf16[128,1024]{1,0:T(8,128)(2,1)S(1)}, bf16[128,1024]{1,0:T(8,128)(2,1)S(1)}) custom-call(f32[256,768]{1,0:T(8,128)S(1)} %shard_map.104.x_in, bf16[640,256]{1,0:T(8,128)(2,1)S(1)} %collective-permute-done.1.arrived, bf16[1024,256]{1,0:T(8,128)(2,1)S(1)} %copy-done.3, bf16[1024,256]{1,0:T(8,128)(2,1)S(1)} %copy-done.4, ...), custom_call_target="tpu_custom_call" | custom-call | flops 400000000 | tf_op jit(solution)/shard_map/pallas_call | solution.py:313
  33.0 1.6 %collective-permute-start.2 = (bf16[128,1024]{1,0:T(8,128)(2,1)S(1)}, bf16[128,1024]{1,0:T(8,128)(2,1)S(1)}, u32[]{:S(2)}, u32[]{:S(2)}) collective-permute-start(bf16[128,1024]{1,0:T(8,128)(2,1)S(1)} %get-tuple-element.19), channel_id=1, source_target_pairs={{0,1},{1,0},{2,3},{3,2},{4,5},{5,4},{6,7},{7,6},{8,9},{9,8},{10,11... | collective-permute-start | bytes 786440 | tf_op jit(solution)/shard_map/ppermute | solution.py:384
  34.5 1.9 %collective-permute-start.4 = (bf16[128,1024]{1,0:T(8,128)(2,1)S(1)}, bf16[128,1024]{1,0:T(8,128)(2,1)S(1)}, u32[]{:S(2)}, u32[]{:S(2)}) collective-permute-start(bf16[128,1024]{1,0:T(8,128)(2,1)S(1)} %get-tuple-element.20), channel_id=1, source_target_pairs={{0,3},{3,0},{1,2},{2,1},{4,7},{7,4},{5,6},{6,5},{8,11},{11,8},{9,1... | collective-permute-start | bytes 786440 | tf_op jit(solution)/shard_map/ppermute | solution.py:384
  36.4 2.3 %collective-permute-done.2 = bf16[128,1024]{1,0:T(8,128)(2,1)S(1)} collective-permute-done((bf16[128,1024]{1,0:T(8,128)(2,1)S(1)}, bf16[128,1024]{1,0:T(8,128)(2,1)S(1)}, u32[]{:S(2)}, u32[]{:S(2)}) %collective-permute-start.2) | collective-permute-done | bytes 262176 | tf_op jit(solution)/shard_map/ppermute | solution.py:384
  38.8 0.1 add_convert_fusion.1.a
  38.8 2.8 %collective-permute-start.3 = (bf16[128,1024]{1,0:T(8,128)(2,1)S(1)}, bf16[128,1024]{1,0:T(8,128)(2,1)S(1)}, u32[]{:S(2)}, u32[]{:S(2)}) collective-permute-start(bf16[128,1024]{1,0:T(8,128)(2,1)S(1)} %add_convert_fusion.1.a), channel_id=1, source_target_pairs={{0,3},{3,0},{1,2},{2,1},{4,7},{7,4},{5,6},{6,5},{8,11},{11,8},{9,1... | collective-permute-start | bytes 786440 | tf_op jit(solution)/shard_map/ppermute | solution.py:386
  41.7 1.7 %collective-permute-done.4 = bf16[128,1024]{1,0:T(8,128)(2,1)S(1)} collective-permute-done((bf16[128,1024]{1,0:T(8,128)(2,1)S(1)}, bf16[128,1024]{1,0:T(8,128)(2,1)S(1)}, u32[]{:S(2)}, u32[]{:S(2)}) %collective-permute-start.4) | collective-permute-done | bytes 262176 | tf_op jit(solution)/shard_map/ppermute | solution.py:384
  43.3 0.1 add_convert_fusion.b
  43.4 0.4 collective-permute-start.5
  43.8 2.3 %collective-permute-done.3.a_in = bf16[128,1024]{1,0:T(8,128)(2,1)S(1)} collective-permute-done((bf16[128,1024]{1,0:T(8,128)(2,1)S(1)}, bf16[128,1024]{1,0:T(8,128)(2,1)S(1)}, u32[]{:S(2)}, u32[]{:S(2)}) %collective-permute-start.3) | collective-permute-done | bytes 262176 | tf_op jit(solution)/shard_map/ppermute | solution.py:386
  46.1 2.6 %collective-permute-done.5.b_in = bf16[128,1024]{1,0:T(8,128)(2,1)S(1)} collective-permute-done((bf16[128,1024]{1,0:T(8,128)(2,1)S(1)}, bf16[128,1024]{1,0:T(8,128)(2,1)S(1)}, u32[]{:S(2)}, u32[]{:S(2)}) %collective-permute-start.5) | collective-permute-done | bytes 262176 | tf_op jit(solution)/shard_map/ppermute | solution.py:386
  48.7 0.0 copy-done
  48.7 1.5 %shard_map.106 = bf16[256,1024]{1,0:T(8,128)(2,1)} custom-call(bf16[128,1024]{1,0:T(8,128)(2,1)S(1)} %add_convert_fusion.1.a, bf16[128,1024]{1,0:T(8,128)(2,1)S(1)} %collective-permute-done.3.a_in, bf16[128,1024]{1,0:T(8,128)(2,1)S(1)} %add_convert_fusion.b, bf16[128,1024]{1,0:T(8,128)(2,1)S(1)} %collective-permute-done.5.b_in, bf16[1024,1024]{1,0:T(8,128)(2,1)S(1)} %copy-done), custom_call_target="tpu_custom_call" | custom-call | flops 500000000 | tf_op jit(solution)/shard_map/pallas_call | solution.py:313
Async XLA Ops:
  2.5 9.1 %copy-start.1 = (bf16[1024,256]{1,0:T(8,128)(2,1)S(1)}, bf16[1024,256]{1,0:T(8,128)(2,1)}, u32[]{:S(2)}) copy-start(bf16[1024,256]{1,0:T(8,128)(2,1)} %keys.7) | copy-start | bytes 1572868
  2.6 9.1 %copy-start.2 = (bf16[1024,256]{1,0:T(8,128)(2,1)S(1)}, bf16[1024,256]{1,0:T(8,128)(2,1)}, u32[]{:S(2)}) copy-start(bf16[1024,256]{1,0:T(8,128)(2,1)} %values.7) | copy-start | bytes 1572868
  2.6 9.1 %copy-start.6 = (s32[1024]{0:T(1024)S(1)}, s32[1024]{0:T(1024)}, u32[]{:S(2)}) copy-start(s32[1024]{0:T(1024)} %param.18) | copy-start | bytes 12292
  2.6 9.1 %copy-start.7 = (bf16[1024,256]{1,0:T(8,128)(2,1)S(1)}, bf16[1024,256]{1,0:T(8,128)(2,1)}, u32[]{:S(2)}) copy-start(bf16[1024,256]{1,0:T(8,128)(2,1)} %queries.5) | copy-start | bytes 1572868
  2.6 12.9 %collective-permute-start = (bf16[1040,256]{1,0:T(8,128)(2,1)}, bf16[1040,256]{1,0:T(8,128)(2,1)S(1)}, u32[]{:S(2)}, u32[]{:S(2)}) collective-permute-start(bf16[1040,256]{1,0:T(8,128)(2,1)} %shard_map.101), channel_id=1, source_target_pairs={{0,4},{4,8},{8,12},{12,16},{16,20},{20,24},{24,28},{28,32},{32,36}... | collective-permute-start | bytes 1597448 | tf_op jit(solution)/shard_map/ppermute | solution.py:342
  11.7 1.0 %copy-start.8 = (bf16[1024,256]{1,0:T(8,128)(2,1)S(1)}, bf16[1024,256]{1,0:T(8,128)(2,1)}, u32[]{:S(2)}) copy-start(bf16[1024,256]{1,0:T(8,128)(2,1)} %shard_map.100.grads) | copy-start | bytes 1572868
  20.6 11.7 %collective-permute-start.1 = (bf16[640,256]{1,0:T(8,128)(2,1)S(1)}, bf16[640,256]{1,0:T(8,128)(2,1)S(1)}, u32[]{:S(2)}, u32[]{:S(2)}) collective-permute-start(bf16[640,256]{1,0:T(8,128)(2,1)S(1)} %get-tuple-element.18), channel_id=1, source_target_pairs={{4,0},{8,4},{12,8},{16,12},{20,16},{24,20},{28,24},{32,28},{36,32}... | collective-permute-start | bytes 983048 | tf_op jit(solution)/shard_map/ppermute | solution.py:365
  22.6 9.8 %copy-start.3 = (bf16[1024,256]{1,0:T(8,128)(2,1)S(1)}, bf16[1024,256]{1,0:T(8,128)(2,1)}, u32[]{:S(2)}) copy-start(bf16[1024,256]{1,0:T(8,128)(2,1)} %w_query.1) | copy-start | bytes 1572868
  22.6 9.8 %copy-start.4 = (bf16[1024,256]{1,0:T(8,128)(2,1)S(1)}, bf16[1024,256]{1,0:T(8,128)(2,1)}, u32[]{:S(2)}) copy-start(bf16[1024,256]{1,0:T(8,128)(2,1)} %w_key.1) | copy-start | bytes 1572868
  22.6 9.8 %copy-start.5 = (bf16[1024,256]{1,0:T(8,128)(2,1)S(1)}, bf16[1024,256]{1,0:T(8,128)(2,1)}, u32[]{:S(2)}) copy-start(bf16[1024,256]{1,0:T(8,128)(2,1)} %w_value.1) | copy-start | bytes 1572868
  25.5 23.2 %copy-start = (bf16[1024,1024]{1,0:T(8,128)(2,1)S(1)}, bf16[1024,1024]{1,0:T(8,128)(2,1)}, u32[]{:S(2)}) copy-start(bf16[1024,1024]{1,0:T(8,128)(2,1)} %unpatch.1) | copy-start | bytes 6291460
  33.0 5.8 %collective-permute-start.2 = (bf16[128,1024]{1,0:T(8,128)(2,1)S(1)}, bf16[128,1024]{1,0:T(8,128)(2,1)S(1)}, u32[]{:S(2)}, u32[]{:S(2)}) collective-permute-start(bf16[128,1024]{1,0:T(8,128)(2,1)S(1)} %get-tuple-element.19), channel_id=1, source_target_pairs={{0,1},{1,0},{2,3},{3,2},{4,5},{5,4},{6,7},{7,6},{8,9},{9,8},{10,11... | collective-permute-start | bytes 786440 | tf_op jit(solution)/shard_map/ppermute | solution.py:384
  34.5 8.8 %collective-permute-start.4 = (bf16[128,1024]{1,0:T(8,128)(2,1)S(1)}, bf16[128,1024]{1,0:T(8,128)(2,1)S(1)}, u32[]{:S(2)}, u32[]{:S(2)}) collective-permute-start(bf16[128,1024]{1,0:T(8,128)(2,1)S(1)} %get-tuple-element.20), channel_id=1, source_target_pairs={{0,3},{3,0},{1,2},{2,1},{4,7},{7,4},{5,6},{6,5},{8,11},{11,8},{9,1... | collective-permute-start | bytes 786440 | tf_op jit(solution)/shard_map/ppermute | solution.py:384
  38.8 7.3 %collective-permute-start.3 = (bf16[128,1024]{1,0:T(8,128)(2,1)S(1)}, bf16[128,1024]{1,0:T(8,128)(2,1)S(1)}, u32[]{:S(2)}, u32[]{:S(2)}) collective-permute-start(bf16[128,1024]{1,0:T(8,128)(2,1)S(1)} %add_convert_fusion.1.a), channel_id=1, source_target_pairs={{0,3},{3,0},{1,2},{2,1},{4,7},{7,4},{5,6},{6,5},{8,11},{11,8},{9,1... | collective-permute-start | bytes 786440 | tf_op jit(solution)/shard_map/ppermute | solution.py:386
  43.4 5.3 %collective-permute-start.5 = (bf16[128,1024]{1,0:T(8,128)(2,1)S(1)}, bf16[128,1024]{1,0:T(8,128)(2,1)S(1)}, u32[]{:S(2)}, u32[]{:S(2)}) collective-permute-start(bf16[128,1024]{1,0:T(8,128)(2,1)S(1)} %add_convert_fusion.b), channel_id=1, source_target_pairs={{0,1},{1,0},{2,3},{3,2},{4,5},{5,4},{6,7},{7,6},{8,9},{9,8},{10,11... | collective-permute-start | bytes 786440 | tf_op jit(solution)/shard_map/ppermute | solution.py:386

commit v4 on v3

--- a/solution.py
+++ b/solution.py
@@ -191,19 +191,32 @@
     return jnp.concatenate([part.astype(BF16) for part in parts], 0)
 
 
-def pack_kernel(shard_ref, keys, values, index, packed, sems):
-    copies = [
-        pltpu.make_async_copy(source.at[WINDOW:, :], packed.at[n * WINDOW : (n + 1) * WINDOW, :], sems.at[n])
-        for n, source in enumerate((keys, values))
-    ]
-    for copy in copies:
+def pack_kernel(keys, values, index_hbm, packed, index, held, sems, out_sems):
+    arriving, leaving = [], []
+    for n in range(4):
+        source = (keys, values)[n // 2]
+        first = WINDOW + n % 2 * TILE
+        rows = slice(n * TILE, (n + 1) * TILE)
+        arriving.append(pltpu.make_async_copy(source.at[first : first + TILE, :], held.at[rows, :], sems.at[n]))
+        leaving.append(pltpu.make_async_copy(held.at[rows, :], packed.at[rows, :], out_sems.at[n]))
+    places = pltpu.make_async_copy(index_hbm, index, sems.at[4])
+    for copy in (places, *arriving):
         copy.start()
-    slots = (index[:, WINDOW:] - shard_ref[0] * PATCH_DEV).astype(F32)
+    places.wait()
+    slots = (index[:, WINDOW:] & (PATCH_DEV - 1)).astype(F32)
     row = lax.broadcasted_iota(jnp.int32, (16, TILE), 0)
     both = jnp.where(row == 0, slots[:, :TILE], slots[:, TILE:])
-    packed[2 * WINDOW :, :] = both.astype(BF16)
-    for copy in copies:
+    held[2 * WINDOW :, :] = both.astype(BF16)
+    slots_leaving = pltpu.make_async_copy(
+        held.at[2 * WINDOW :, :], packed.at[2 * WINDOW :, :], out_sems.at[4]
+    )
+    slots_leaving.start()
+    for copy, onward in zip(arriving, leaving):
         copy.wait()
+        onward.start()
+    for onward in leaving:
+        onward.wait()
+    slots_leaving.wait()
 
 
 def heads_kernel(d_output_hbm, w_out_hbm, grads, d_output, w_out, sems):
@@ -220,12 +233,12 @@
         grads[rows, :] = mm_t(d_output[rows, :], w_out[...]).astype(BF16)
 
 
-def near_kernel(shard_ref, grads, queries, keys, values, index, near_out, x_out):
+def near_kernel(grads, queries, keys, values, index, near_out, x_out):
     rows = slice(2 * TILE, 3 * TILE)
     d_query_t, d_key, d_value = attend(
         [(queries[rows, :], grads[rows, :], tiles_of(keys, 0), tiles_of(values, 0), None, None)]
     )[0]
-    slots = index[...] - shard_ref[0] * PATCH_DEV
+    slots = index[...] - lax.axis_index("seq") * PATCH_DEV
     d_key, d_value = whole_low(d_key), whole_low(d_value)
     before = one_hot(slots[:, :REACH], -REACH, REACH)
     near_out[:, :TILE] = mm(before, d_key[:REACH])
@@ -237,10 +250,10 @@
 
 
 def far_kernel(
-    shard_ref, grads, queries, keys, values, packed, index, near,
+    grads, queries, keys, values, packed, index, near,
     sent_out, k_out, v_out, q_out,
 ):
-    shard = shard_ref[0]
+    shard = lax.axis_index("seq")
     bias = jnp.where(shard > 0, 0.0, -1e30).astype(F32)
     slots = index[:, :REACH] - shard * PATCH_DEV
     all_keys = tiles_of(packed, 0, 2) + tiles_of(keys, 0, 2)
@@ -269,12 +282,12 @@
     sent_out[2 * PATCH_DEV :, :] = mm_t(own, q_out[:, :REACH]).astype(BF16)
 
 
-def last_kernel(shard_ref, grads, queries, keys, values, index, k_in, v_in, q_in, x_in, x_out):
+def last_kernel(grads, queries, keys, values, index, k_in, v_in, q_in, x_in, x_out):
     rows = slice(3 * TILE, 4 * TILE)
     d_query_t, d_key, d_value = attend(
         [(queries[rows, :], grads[rows, :], tiles_of(keys, 1), tiles_of(values, 1), None, None)]
     )[0]
-    chosen = one_hot(index[...] - shard_ref[0] * PATCH_DEV, 0, PATCH_DEV)
+    chosen = one_hot(index[...] - lax.axis_index("seq") * PATCH_DEV, 0, PATCH_DEV)
     first, later = chosen[:, :WINDOW], chosen[:, TILE:]
     x_out[:, :TILE] = (
         x_in[:, :TILE] + mm_t(first, q_in[...]) + mm_t(chosen[:, 3 * TILE :], d_query_t)
@@ -298,23 +311,32 @@
     second_out[...] = d_up[PATCH_DEV // 2 :].astype(BF16)
 
 
-def final_kernel(a, a_in, b, b_in, unpatch, out):
+def final_kernel(first, mine, other, unpatch, *refs):
+    out, low, sems = refs[-3:]
+    total = (mine[...].astype(F32) + other[...].astype(F32)).astype(BF16)
     half = PATCH_DEV // 2
-    for place, own, other in ((0, a, a_in), (half, b, b_in)):
-        total = (own[...].astype(F32) + other[...].astype(F32)).astype(BF16)
-        out[place : place + half, :] = mm(total, unpatch[...]).astype(BF16)
-
-
-def call(kernel, shapes, args, scratch=(), flops=0, vmem=32, whole=()):
+    width = low.shape[1] // sems.shape[0]
+    copies = []
+    for n in range(sems.shape[0]):
+        at = slice(n * width, (n + 1) * width)
+        low[:, at] = mm(total, unpatch[:, at]).astype(BF16)
+        copies.append(pltpu.make_async_copy(low.at[:, at], out.at[first : first + half, at], sems.at[n]))
+        copies[n].start()
+    for copy in copies:
+        copy.wait()
+
+
+def call(kernel, shapes, args, scratch=(), flops=0, vmem=32, whole=(), out_space=pltpu.VMEM, aliases={}):
     specs = []
-    for n, arg in enumerate(args):
-        space = pltpu.SMEM if arg.shape == (1,) else pl.ANY if n in whole else pltpu.VMEM
+    for n in range(len(args)):
+        space = pl.ANY if n in whole else pltpu.VMEM
         specs.append(pl.BlockSpec(memory_space=space))
     return pl.pallas_call(
         kernel,
         out_shape=[jax.ShapeDtypeStruct(*shape) for shape in shapes],
         in_specs=specs,
-        out_specs=[pl.BlockSpec(memory_space=pltpu.VMEM)] * len(shapes),
+        out_specs=[pl.BlockSpec(memory_space=out_space)] * len(shapes),
+        input_output_aliases=aliases,
         scratch_shapes=list(scratch),
         compiler_params=pltpu.CompilerParams(vmem_limit_bytes=vmem * 1024 * 1024),
         cost_estimate=pl.CostEstimate(flops=flops, bytes_accessed=0, transcendentals=0),
@@ -324,20 +346,24 @@
 def on_device(
     queries, byte_keys, byte_values, w_query, w_key, w_value, w_out, d_output, patch_index, unpatch
 ):
-    shard = lax.axis_index("seq")
     count = lax.axis_size("seq")
     onward = [(n, n + 1) for n in range(count - 1)]
     back = [(n + 1, n) for n in range(count - 1)]
-    place = shard.astype(jnp.int32)[None]
     index = patch_index[None, :]
     packed = call(
         pack_kernel,
         [((2 * WINDOW + 16, 256), BF16)],
-        (place, byte_keys, byte_values, index),
-        [pltpu.SemaphoreType.DMA((2,))],
+        (byte_keys, byte_values, index),
+        [
+            pltpu.VMEM((1, 1024), jnp.int32),
+            pltpu.VMEM((2 * WINDOW + 16, 256), BF16),
+            pltpu.SemaphoreType.DMA((5,)),
+            pltpu.SemaphoreType.DMA((5,)),
+        ],
         flops=10**6,
         vmem=60,
-        whole=(1, 2),
+        whole=(0, 1, 2),
+        out_space=pl.ANY,
     )[0]
     packed = lax.ppermute(packed, "seq", onward)
     grads = call(
@@ -349,7 +375,7 @@
         vmem=58,
         whole=(0, 1),
     )[0]
-    own = (place, grads, queries, byte_keys, byte_values)
+    own = (grads, queries, byte_keys, byte_values)
     near, x_near = call(
         near_kernel,
         [((REACH, 512), F32), ((PATCH_DEV, 768), F32)],
@@ -384,12 +410,20 @@
     a_in, b_in = lax.ppermute(a, "mp", across), lax.ppermute(b, "mp", around)
     a, b = pair(a, a_in), pair(b, b_in)
     a_in, b_in = lax.ppermute(a, "mp", around), lax.ppermute(b, "mp", across)
-    return call(
-        final_kernel,
-        [((PATCH_DEV, 1024), BF16)],
-        (a, a_in, b, b_in, unpatch),
-        flops=5 * 10**8,
-    )[0]
+    half = PATCH_DEV // 2
+    done = ()
+    for first, mine, other in ((0, a, a_in), (half, b, b_in)):
+        done = call(
+            functools.partial(final_kernel, first),
+            [((PATCH_DEV, 1024), BF16)],
+            (mine, other, unpatch, *done),
+            [pltpu.VMEM((half, 1024), BF16), pltpu.SemaphoreType.DMA((4,))],
+            flops=3 * 10**8,
+            whole=(3,),
+            out_space=pl.ANY,
+            aliases={3: 0} if done else {},
+        )
+    return done[0]
 
 
 def solution(mesh):

time: 50.5 us -> 49.6 us (0.982)
  waiting for transfers between devices: 15.7 us -> 14.5 us
    ppermute x2, waiting for transfers between devices: 4.87 us -> 3.7 us  [on_device(): a_in, b_in = (lax.ppermute(a, 'mp', around), lax.ppermute(b, 'mp', across))]
    pallas_call x7 -> x8, Pallas kernels: 19.1 us -> 19.3 us  [call(): pl.pallas_call(kernel, out_shape=[jax.ShapeDtypeStruct(*shape) for shape...]
  transfers between devices with their start and end apart: 6 -> 6, of which waited for: 5 -> 5; matrix products, arithmetic and copies ran while one was open for 0% -> 0% of each run, Pallas kernels for 19% -> 21%
where the time goes in v4:
time: 49.6 us; the launch traced here: 49.4 us
  Pallas kernels  19.3 us (39%)
  waiting for transfers between devices  14.5 us (29%)
  starting transfers between devices  14 us (28%)
  local copies, waits for them, and re-layouts  1.09 us (2%)
    pallas_call x8, Pallas kernels, call(): pl.pallas_call(kernel, out_shape=[jax.ShapeDtypeStruct(*shape) for shape...  19.3 us
    ppermute x1, waiting for transfers between devices, on_device(): arrived = lax.ppermute(sent, 'seq', back)  6.82 us
    ppermute x1, starting transfers between devices, on_device(): packed = lax.ppermute(packed, 'seq', onward)  5.36 us
    ppermute x2, waiting for transfers between devices, on_device(): a_in, b_in = (lax.ppermute(a, 'mp', across), lax.ppermute(b, 'mp', around))  3.99 us
    ppermute x2, waiting for transfers between devices, on_device(): a_in, b_in = (lax.ppermute(a, 'mp', around), lax.ppermute(b, 'mp', across))  3.7 us
    ppermute x2, starting transfers between devices, on_device(): a_in, b_in = (lax.ppermute(a, 'mp', across), lax.ppermute(b, 'mp', around))  3.47 us
    ppermute x2, starting transfers between devices, on_device(): a_in, b_in = (lax.ppermute(a, 'mp', around), lax.ppermute(b, 'mp', across))  3.27 us
    ppermute x1, starting transfers between devices, on_device(): arrived = lax.ppermute(sent, 'seq', back)  1.92 us
  transfers between devices with their start and end apart: 6, of which 5 were waited for; matrix products, arithmetic and copies ran while one was open for 0% of the time, Pallas kernels for 21%

profile of v4, /device:TPU:103, one launch (start us, length us, event | category | flops | bytes accessed | tf_op | source)
XLA Modules:
  0.0 49.4 jit_solution(14157128309983292116)
XLA Ops:
  0.0 1.8 %shard_map.101 = bf16[1040,256]{1,0:T(8,128)(2,1)} custom-call(bf16[1024,256]{1,0:T(8,128)(2,1)} %keys.7, bf16[1024,256]{1,0:T(8,128)(2,1)} %values.7, s32[1,1024]{1,0:T(1,128)} %bitcast.1), custom_call_target="tpu_custom_call" | custom-call | flops 1000000 | tf_op jit(solution)/shard_map/pallas_call | solution.py:334
  1.8 0.0 copy-start.1
  1.9 0.0 copy-start.2
  1.9 0.0 copy-start.6
  1.9 0.0 copy-start.7
  1.9 5.4 %collective-permute-start = (bf16[1040,256]{1,0:T(8,128)(2,1)}, bf16[1040,256]{1,0:T(8,128)(2,1)S(1)}, u32[]{:S(2)}, u32[]{:S(2)}) collective-permute-start(bf16[1040,256]{1,0:T(8,128)(2,1)} %shard_map.101), channel_id=1, source_target_pairs={{0,4},{4,8},{8,12},{12,16},{16,20},{20,24},{24,28},{28,32},{32,36}... | collective-permute-start | bytes 1597448 | tf_op jit(solution)/shard_map/ppermute | solution.py:368
  7.3 3.7 %shard_map.100.grads = bf16[1024,256]{1,0:T(8,128)(2,1)} custom-call(bf16[1024,1024]{1,0:T(8,128)(2,1)} %d_output_hbm.1, bf16[256,1024]{1,0:T(8,128)(2,1)} %w_out_hbm.1), custom_call_target="tpu_custom_call" | custom-call | flops 8000000000 | tf_op jit(solution)/shard_map/pallas_call | solution.py:334
  10.9 0.0 copy-done.1
  10.9 0.0 copy-done.2
  11.0 0.0 copy-done.6
  11.0 0.0 copy-done.7
  11.0 0.0 copy-start.8
  11.0 1.0 %copy-done.8 = bf16[1024,256]{1,0:T(8,128)(2,1)S(1)} copy-done((bf16[1024,256]{1,0:T(8,128)(2,1)S(1)}, bf16[1024,256]{1,0:T(8,128)(2,1)}, u32[]{:S(2)}) %copy-start.8) | copy-done | bytes 524312
  12.0 2.8 %shard_map.102 = (f32[128,512]{1,0:T(8,128)S(1)}, f32[256,768]{1,0:T(8,128)S(1)}) custom-call(bf16[1024,256]{1,0:T(8,128)(2,1)S(1)} %copy-done.8, bf16[1024,256]{1,0:T(8,128)(2,1)S(1)} %copy-done.7, bf16[1024,256]{1,0:T(8,128)(2,1)S(1)} %copy-done.1, bf16[1024,256]{1,0:T(8,128)(2,1)S(1)} %copy-done.2, s32[1,1024]{1,0:T(1,128)S(1)} %bitcast.2), custom_call_target="tpu_custom_call" | custom-call | flops 8000000000 | tf_op jit(solution)/shard_map/pallas_call | solution.py:334
  14.8 0.0 collective-permute-done.packed
  14.9 5.2 %shard_map.103 = (bf16[640,256]{1,0:T(8,128)(2,1)S(1)}, bf16[512,256]{1,0:T(8,128)(2,1)S(1)}, bf16[512,256]{1,0:T(8,128)(2,1)S(1)}, bf16[256,512]{1,0:T(8,128)(2,1)S(1)}) custom-call(bf16[1024,256]{1,0:T(8,128)(2,1)S(1)} %copy-done.8, bf16[1024,256]{1,0:T(8,128)(2,1)S(1)} %copy-done.7, bf16[1024,256]{1,0:T(8,128)(2,1)S(1)} %copy-done.1, ...), custom_call_target="tpu_custom_call" | custom-call | flops 8000000000 | tf_op jit(solution)/shard_map/pallas_call | solution.py:334
  20.0 1.9 %collective-permute-start.1 = (bf16[640,256]{1,0:T(8,128)(2,1)S(1)}, bf16[640,256]{1,0:T(8,128)(2,1)S(1)}, u32[]{:S(2)}, u32[]{:S(2)}) collective-permute-start(bf16[640,256]{1,0:T(8,128)(2,1)S(1)} %get-tuple-element.18), channel_id=1, source_target_pairs={{4,0},{8,4},{12,8},{16,12},{20,16},{24,20},{28,24},{32,28},{36,32}... | collective-permute-start | bytes 983048 | tf_op jit(solution)/shard_map/ppermute | solution.py:391
  21.9 0.0 copy-start.3
  22.0 0.0 copy-start.4
  22.0 0.0 copy-start.5
  22.0 2.9 %shard_map.104.x_in = f32[256,768]{1,0:T(8,128)S(1)} custom-call(bf16[1024,256]{1,0:T(8,128)(2,1)S(1)} %copy-done.8, bf16[1024,256]{1,0:T(8,128)(2,1)S(1)} %copy-done.7, bf16[1024,256]{1,0:T(8,128)(2,1)S(1)} %copy-done.1, bf16[1024,256]{1,0:T(8,128)(2,1)S(1)} %copy-done.2, s32[1,1024]{1,0:T(1,128)S(1)} %bitcast.4, ...), custom_call_target="tpu_custom_call" | custom-call | flops 8000000000 | tf_op jit(solution)/shard_map/pallas_call | solution.py:334
  24.9 0.0 copy-start
  24.9 6.8 %collective-permute-done.1.arrived = bf16[640,256]{1,0:T(8,128)(2,1)S(1)} collective-permute-done((bf16[640,256]{1,0:T(8,128)(2,1)S(1)}, bf16[640,256]{1,0:T(8,128)(2,1)S(1)}, u32[]{:S(2)}, u32[]{:S(2)}) %collective-permute-start.1) | collective-permute-done | bytes 327712 | tf_op jit(solution)/shard_map/ppermute | solution.py:391
  31.7 0.0 copy-done.3
  31.7 0.0 copy-done.4
  31.7 0.0 copy-done.5
  31.7 0.6 %shard_map.105 = (bf16[128,1024]{1,0:T(8,128)(2,1)S(1)}, bf16[128,1024]{1,0:T(8,128)(2,1)S(1)}) custom-call(f32[256,768]{1,0:T(8,128)S(1)} %shard_map.104.x_in, bf16[640,256]{1,0:T(8,128)(2,1)S(1)} %collective-permute-done.1.arrived, bf16[1024,256]{1,0:T(8,128)(2,1)S(1)} %copy-done.3, bf16[1024,256]{1,0:T(8,128)(2,1)S(1)} %copy-done.4, ...), custom_call_target="tpu_custom_call" | custom-call | flops 400000000 | tf_op jit(solution)/shard_map/pallas_call | solution.py:334
  32.4 1.6 %collective-permute-start.4 = (bf16[128,1024]{1,0:T(8,128)(2,1)S(1)}, bf16[128,1024]{1,0:T(8,128)(2,1)S(1)}, u32[]{:S(2)}, u32[]{:S(2)}) collective-permute-start(bf16[128,1024]{1,0:T(8,128)(2,1)S(1)} %get-tuple-element.20), channel_id=1, source_target_pairs={{0,1},{1,0},{2,3},{3,2},{4,5},{5,4},{6,7},{7,6},{8,9},{9,8},{10,11... | collective-permute-start | bytes 786440 | tf_op jit(solution)/shard_map/ppermute | solution.py:410
  33.9 1.9 %collective-permute-start.2 = (bf16[128,1024]{1,0:T(8,128)(2,1)S(1)}, bf16[128,1024]{1,0:T(8,128)(2,1)S(1)}, u32[]{:S(2)}, u32[]{:S(2)}) collective-permute-start(bf16[128,1024]{1,0:T(8,128)(2,1)S(1)} %get-tuple-element.19), channel_id=1, source_target_pairs={{0,3},{3,0},{1,2},{2,1},{4,7},{7,4},{5,6},{6,5},{8,11},{11,8},{9,1... | collective-permute-start | bytes 786440 | tf_op jit(solution)/shard_map/ppermute | solution.py:410
  35.8 2.3 %collective-permute-done.4 = bf16[128,1024]{1,0:T(8,128)(2,1)S(1)} collective-permute-done((bf16[128,1024]{1,0:T(8,128)(2,1)S(1)}, bf16[128,1024]{1,0:T(8,128)(2,1)S(1)}, u32[]{:S(2)}, u32[]{:S(2)}) %collective-permute-start.4) | collective-permute-done | bytes 262176 | tf_op jit(solution)/shard_map/ppermute | solution.py:410
  38.1 0.1 add_convert_fusion.mine
  38.2 2.8 %collective-permute-start.5 = (bf16[128,1024]{1,0:T(8,128)(2,1)S(1)}, bf16[128,1024]{1,0:T(8,128)(2,1)S(1)}, u32[]{:S(2)}, u32[]{:S(2)}) collective-permute-start(bf16[128,1024]{1,0:T(8,128)(2,1)S(1)} %add_convert_fusion.mine), channel_id=1, source_target_pairs={{0,3},{3,0},{1,2},{2,1},{4,7},{7,4},{5,6},{6,5},{8,11},{11,8},{9,1... | collective-permute-start | bytes 786440 | tf_op jit(solution)/shard_map/ppermute | solution.py:412
  41.0 1.7 %collective-permute-done.2 = bf16[128,1024]{1,0:T(8,128)(2,1)S(1)} collective-permute-done((bf16[128,1024]{1,0:T(8,128)(2,1)S(1)}, bf16[128,1024]{1,0:T(8,128)(2,1)S(1)}, u32[]{:S(2)}, u32[]{:S(2)}) %collective-permute-start.2) | collective-permute-done | bytes 262176 | tf_op jit(solution)/shard_map/ppermute | solution.py:410
  42.7 0.1 add_convert_fusion.1.mine
  42.8 0.5 collective-permute-start.3
  43.2 2.3 %collective-permute-done.5.other = bf16[128,1024]{1,0:T(8,128)(2,1)S(1)} collective-permute-done((bf16[128,1024]{1,0:T(8,128)(2,1)S(1)}, bf16[128,1024]{1,0:T(8,128)(2,1)S(1)}, u32[]{:S(2)}, u32[]{:S(2)}) %collective-permute-start.5) | collective-permute-done | bytes 262176 | tf_op jit(solution)/shard_map/ppermute | solution.py:412
  45.5 0.0 copy-done
  45.5 1.1 %shard_map.106.refs_0_ = bf16[256,1024]{1,0:T(8,128)(2,1)} custom-call(bf16[128,1024]{1,0:T(8,128)(2,1)S(1)} %add_convert_fusion.mine, bf16[128,1024]{1,0:T(8,128)(2,1)S(1)} %collective-permute-done.5.other, bf16[1024,1024]{1,0:T(8,128)(2,1)S(1)} %copy-done), custom_call_target="tpu_custom_call" | custom-call | flops 300000000 | tf_op jit(solution)/shard_map/pallas_call | solution.py:334
  46.7 1.4 %collective-permute-done.3.other = bf16[128,1024]{1,0:T(8,128)(2,1)S(1)} collective-permute-done((bf16[128,1024]{1,0:T(8,128)(2,1)S(1)}, bf16[128,1024]{1,0:T(8,128)(2,1)S(1)}, u32[]{:S(2)}, u32[]{:S(2)}) %collective-permute-start.3) | collective-permute-done | bytes 262176 | tf_op jit(solution)/shard_map/ppermute | solution.py:412
  48.1 1.1 %shard_map.107 = bf16[256,1024]{1,0:T(8,128)(2,1)} custom-call(bf16[128,1024]{1,0:T(8,128)(2,1)S(1)} %add_convert_fusion.1.mine, bf16[128,1024]{1,0:T(8,128)(2,1)S(1)} %collective-permute-done.3.other, bf16[1024,1024]{1,0:T(8,128)(2,1)S(1)} %copy-done, bf16[256,1024]{1,0:T(8,128)(2,1)} %shard_map.106.refs_0_), custom_call_target="tpu_custom_call", output_to_operand_aliasing={{}: (3, {})} | custom-call | flops 300000000 | tf_op jit(solution)/shard_map/pallas_call | solution.py:334
Async XLA Ops:
  1.8 9.1 %copy-start.1 = (bf16[1024,256]{1,0:T(8,128)(2,1)S(1)}, bf16[1024,256]{1,0:T(8,128)(2,1)}, u32[]{:S(2)}) copy-start(bf16[1024,256]{1,0:T(8,128)(2,1)} %keys.7) | copy-start | bytes 1572868
  1.9 9.1 %copy-start.2 = (bf16[1024,256]{1,0:T(8,128)(2,1)S(1)}, bf16[1024,256]{1,0:T(8,128)(2,1)}, u32[]{:S(2)}) copy-start(bf16[1024,256]{1,0:T(8,128)(2,1)} %values.7) | copy-start | bytes 1572868
  1.9 9.1 %copy-start.6 = (s32[1024]{0:T(1024)S(1)}, s32[1024]{0:T(1024)}, u32[]{:S(2)}) copy-start(s32[1024]{0:T(1024)} %param.18) | copy-start | bytes 12292
  1.9 9.1 %copy-start.7 = (bf16[1024,256]{1,0:T(8,128)(2,1)S(1)}, bf16[1024,256]{1,0:T(8,128)(2,1)}, u32[]{:S(2)}) copy-start(bf16[1024,256]{1,0:T(8,128)(2,1)} %queries.5) | copy-start | bytes 1572868
  1.9 12.9 %collective-permute-start = (bf16[1040,256]{1,0:T(8,128)(2,1)}, bf16[1040,256]{1,0:T(8,128)(2,1)S(1)}, u32[]{:S(2)}, u32[]{:S(2)}) collective-permute-start(bf16[1040,256]{1,0:T(8,128)(2,1)} %shard_map.101), channel_id=1, source_target_pairs={{0,4},{4,8},{8,12},{12,16},{16,20},{20,24},{24,28},{28,32},{32,36}... | collective-permute-start | bytes 1597448 | tf_op jit(solution)/shard_map/ppermute | solution.py:368
  11.0 1.0 %copy-start.8 = (bf16[1024,256]{1,0:T(8,128)(2,1)S(1)}, bf16[1024,256]{1,0:T(8,128)(2,1)}, u32[]{:S(2)}) copy-start(bf16[1024,256]{1,0:T(8,128)(2,1)} %shard_map.100.grads) | copy-start | bytes 1572868
  20.0 11.7 %collective-permute-start.1 = (bf16[640,256]{1,0:T(8,128)(2,1)S(1)}, bf16[640,256]{1,0:T(8,128)(2,1)S(1)}, u32[]{:S(2)}, u32[]{:S(2)}) collective-permute-start(bf16[640,256]{1,0:T(8,128)(2,1)S(1)} %get-tuple-element.18), channel_id=1, source_target_pairs={{4,0},{8,4},{12,8},{16,12},{20,16},{24,20},{28,24},{32,28},{36,32}... | collective-permute-start | bytes 983048 | tf_op jit(solution)/shard_map/ppermute | solution.py:391
  21.9 9.8 %copy-start.3 = (bf16[1024,256]{1,0:T(8,128)(2,1)S(1)}, bf16[1024,256]{1,0:T(8,128)(2,1)}, u32[]{:S(2)}) copy-start(bf16[1024,256]{1,0:T(8,128)(2,1)} %w_query.1) | copy-start | bytes 1572868
  22.0 9.8 %copy-start.4 = (bf16[1024,256]{1,0:T(8,128)(2,1)S(1)}, bf16[1024,256]{1,0:T(8,128)(2,1)}, u32[]{:S(2)}) copy-start(bf16[1024,256]{1,0:T(8,128)(2,1)} %w_key.1) | copy-start | bytes 1572868
  22.0 9.8 %copy-start.5 = (bf16[1024,256]{1,0:T(8,128)(2,1)S(1)}, bf16[1024,256]{1,0:T(8,128)(2,1)}, u32[]{:S(2)}) copy-start(bf16[1024,256]{1,0:T(8,128)(2,1)} %w_value.1) | copy-start | bytes 1572868
  24.9 20.6 %copy-start = (bf16[1024,1024]{1,0:T(8,128)(2,1)S(1)}, bf16[1024,1024]{1,0:T(8,128)(2,1)}, u32[]{:S(2)}) copy-start(bf16[1024,1024]{1,0:T(8,128)(2,1)} %unpatch.3) | copy-start | bytes 6291460
  32.4 5.8 %collective-permute-start.4 = (bf16[128,1024]{1,0:T(8,128)(2,1)S(1)}, bf16[128,1024]{1,0:T(8,128)(2,1)S(1)}, u32[]{:S(2)}, u32[]{:S(2)}) collective-permute-start(bf16[128,1024]{1,0:T(8,128)(2,1)S(1)} %get-tuple-element.20), channel_id=1, source_target_pairs={{0,1},{1,0},{2,3},{3,2},{4,5},{5,4},{6,7},{7,6},{8,9},{9,8},{10,11... | collective-permute-start | bytes 786440 | tf_op jit(solution)/shard_map/ppermute | solution.py:410
  33.9 8.8 %collective-permute-start.2 = (bf16[128,1024]{1,0:T(8,128)(2,1)S(1)}, bf16[128,1024]{1,0:T(8,128)(2,1)S(1)}, u32[]{:S(2)}, u32[]{:S(2)}) collective-permute-start(bf16[128,1024]{1,0:T(8,128)(2,1)S(1)} %get-tuple-element.19), channel_id=1, source_target_pairs={{0,3},{3,0},{1,2},{2,1},{4,7},{7,4},{5,6},{6,5},{8,11},{11,8},{9,1... | collective-permute-start | bytes 786440 | tf_op jit(solution)/shard_map/ppermute | solution.py:410
  38.2 7.3 %collective-permute-start.5 = (bf16[128,1024]{1,0:T(8,128)(2,1)S(1)}, bf16[128,1024]{1,0:T(8,128)(2,1)S(1)}, u32[]{:S(2)}, u32[]{:S(2)}) collective-permute-start(bf16[128,1024]{1,0:T(8,128)(2,1)S(1)} %add_convert_fusion.mine), channel_id=1, source_target_pairs={{0,3},{3,0},{1,2},{2,1},{4,7},{7,4},{5,6},{6,5},{8,11},{11,8},{9,1... | collective-permute-start | bytes 786440 | tf_op jit(solution)/shard_map/ppermute | solution.py:412
  42.8 5.3 %collective-permute-start.3 = (bf16[128,1024]{1,0:T(8,128)(2,1)S(1)}, bf16[128,1024]{1,0:T(8,128)(2,1)S(1)}, u32[]{:S(2)}, u32[]{:S(2)}) collective-permute-start(bf16[128,1024]{1,0:T(8,128)(2,1)S(1)} %add_convert_fusion.1.mine), channel_id=1, source_target_pairs={{0,1},{1,0},{2,3},{3,2},{4,5},{5,4},{6,7},{7,6},{8,9},{9,8},{10,11... | collective-permute-start | bytes 786440 | tf_op jit(solution)/shard_map/ppermute | solution.py:412

commit v5 on v4

--- a/solution.py
+++ b/solution.py
@@ -44,12 +44,13 @@
 
 
 class Unit:
-    def __init__(self, keys, values, keys_t, query, grad, far_bias, mid_bias):
+    def __init__(self, keys, values, keys_t, query, grad, far_bias, mid_bias, d_key, d_value, known):
         self.keys, self.values, self.keys_t = keys, values, keys_t
         self.query, self.grad = query, grad
         self.far_bias, self.mid_bias = far_bias, mid_bias
-        self.s, self.dp = [None] * 3, [None] * 3
-        self.d_key, self.d_value = [None] * 3, [None] * 3
+        self.known = known
+        self.s, self.dp = [known.get(t, (None, None))[0] for t in range(3)], [known.get(t, (None, None))[1] for t in range(3)]
+        self.d_key, self.d_value = d_key, d_value
         self.strips, self.low = {}, {}
         self.peak = self.total = self.dot = None
 
@@ -57,12 +58,13 @@
         def step(into, t, a, b):
             into[t] = mm_t(a, b)
 
-        steps = [functools.partial(step, self.s, t, self.keys[t], self.query) for t in (0, 2, 1)]
-        return steps + [functools.partial(step, self.dp, t, self.values[t], self.grad) for t in (0, 2, 1)]
+        tiles = [t for t in (0, 2, 1) if t not in self.known]
+        steps = [functools.partial(step, self.s, t, self.keys[t], self.query) for t in tiles]
+        return steps + [functools.partial(step, self.dp, t, self.values[t], self.grad) for t in tiles]
 
     def back_steps(self):
         def step(into, t, a, b):
-            into[t] = mm(a[t], b)
+            into[t] = joined(into[t], mm(a[t], b))
 
         def query_step():
             self.d_query_t = mm(self.keys_t, jnp.concatenate(self.ds, 0))
@@ -155,11 +157,12 @@
 
 def attend(tiles):
     units = []
-    for query, grad, keys, values, far_bias, mid_bias in tiles:
+    for query, grad, keys, values, far_bias, mid_bias, known in tiles:
         keys_t = jnp.concatenate([k.T for k in keys], 1)
+        d_key, d_value = [None] * 3, [None] * 3
         q_heads = head_parts(query * jnp.asarray(HS**-0.5, BF16))
         for h, (q, g) in enumerate(zip(q_heads, head_parts(grad))):
-            units.append(Unit(keys, values, keys_t[h * HS : (h + 1) * HS], q, g, far_bias, mid_bias))
+            units.append(Unit(keys, values, keys_t[h * HS : (h + 1) * HS], q, g, far_bias, mid_bias, d_key, d_value, known(h)))
     for n in range(len(units) + 2):
         matmuls = units[n - 2].back_steps() if n >= 2 else []
         matmuls += units[n].score_steps() if n < len(units) else []
@@ -177,10 +180,13 @@
     for first in range(0, len(units), heads):
         own = units[first : first + heads]
         d_query_t = jnp.concatenate([unit.d_query_t for unit in own], 0) * HS**-0.5
-        d_key = [sum(unit.d_key[t] for unit in own) for t in range(3)]
-        d_value = [sum(unit.d_value[t] for unit in own) for t in range(3)]
+        d_key, d_value = own[0].d_key, own[0].d_value
         out.append((d_query_t.astype(BF16), d_key, d_value))
     return out
+
+
+def none_known(head):
+    return {}
 
 
 def tiles_of(ref, first, count=3):
@@ -233,10 +239,18 @@
         grads[rows, :] = mm_t(d_output[rows, :], w_out[...]).astype(BF16)
 
 
-def near_kernel(grads, queries, keys, values, index, near_out, x_out):
+OWN_TILES = ((0, 2, 0), (1, 1, 0), (1, 2, 1))
+
+
+def held_rows(n, head):
+    first = (n * 4 + head) * TILE
+    return slice(first, first + TILE)
+
+
+def near_kernel(grads, queries, keys, values, index, near_out, x_out, s_out, dp_out):
     rows = slice(2 * TILE, 3 * TILE)
     d_query_t, d_key, d_value = attend(
-        [(queries[rows, :], grads[rows, :], tiles_of(keys, 0), tiles_of(values, 0), None, None)]
+        [(queries[rows, :], grads[rows, :], tiles_of(keys, 0), tiles_of(values, 0), None, None, none_known)]
     )[0]
     slots = index[...] - lax.axis_index("seq") * PATCH_DEV
     d_key, d_value = whole_low(d_key), whole_low(d_value)
@@ -247,10 +261,17 @@
     x_out[:, :TILE] = mm_t(chosen[:, 2 * TILE :], d_query_t)
     x_out[:, TILE : 2 * TILE] = mm(chosen, d_key)
     x_out[:, 2 * TILE :] = mm(chosen, d_value)
+    scale = jnp.asarray(HS**-0.5, BF16)
+    for n, (tile, _, key_tile) in enumerate(OWN_TILES):
+        own, there = slice(tile * TILE, (tile + 1) * TILE), slice(key_tile * TILE, (key_tile + 1) * TILE)
+        q_heads, g_heads = head_parts(queries[own, :] * scale), head_parts(grads[own, :])
+        for h, (q, g) in enumerate(zip(q_heads, g_heads)):
+            s_out[held_rows(n, h), :] = mm_t(keys[there, :], q)
+            dp_out[held_rows(n, h), :] = mm_t(values[there, :], g)
 
 
 def far_kernel(
-    grads, queries, keys, values, packed, index, near,
+    grads, queries, keys, values, packed, index, near, s_in, dp_in,
     sent_out, k_out, v_out, q_out,
 ):
     shard = lax.axis_index("seq")
@@ -259,10 +280,26 @@
     all_keys = tiles_of(packed, 0, 2) + tiles_of(keys, 0, 2)
     all_values = tiles_of(packed, 2, 2) + tiles_of(values, 0, 2)
     tiles = []
+
+    def known(tile, head):
+        return {
+            t: (s_in.at[held_rows(n, head), :], dp_in.at[held_rows(n, head), :])
+            for n, (owner, t, _) in enumerate(OWN_TILES)
+            if owner == tile
+        }
+
     for n in range(2):
         rows = slice(n * TILE, (n + 1) * TILE)
         tiles.append(
-            (queries[rows, :], grads[rows, :], all_keys[n : n + 3], all_values[n : n + 3], bias, None if n else bias)
+            (
+                queries[rows, :],
+                grads[rows, :],
+                all_keys[n : n + 3],
+                all_values[n : n + 3],
+                bias,
+                None if n else bias,
+                functools.partial(known, n),
+            )
         )
     (q_first, *first), (q_second, *second) = attend(tiles)
     q_out[:, :TILE], q_out[:, TILE:] = q_first, q_second
@@ -285,7 +322,7 @@
 def last_kernel(grads, queries, keys, values, index, k_in, v_in, q_in, x_in, x_out):
     rows = slice(3 * TILE, 4 * TILE)
     d_query_t, d_key, d_value = attend(
-        [(queries[rows, :], grads[rows, :], tiles_of(keys, 1), tiles_of(values, 1), None, None)]
+        [(queries[rows, :], grads[rows, :], tiles_of(keys, 1), tiles_of(values, 1), None, None, none_known)]
     )[0]
     chosen = one_hot(index[...] - lax.axis_index("seq") * PATCH_DEV, 0, PATCH_DEV)
     first, later = chosen[:, :WINDOW], chosen[:, TILE:]
@@ -372,20 +409,20 @@
         (d_output, w_out),
         [pltpu.VMEM((1024, 1024), BF16), pltpu.VMEM((256, 1024), BF16), pltpu.SemaphoreType.DMA((3,))],
         flops=8 * 10**9,
-        vmem=58,
+        vmem=52,
         whole=(0, 1),
     )[0]
     own = (grads, queries, byte_keys, byte_values)
-    near, x_near = call(
+    near, x_near, s_own, dp_own = call(
         near_kernel,
-        [((REACH, 512), F32), ((PATCH_DEV, 768), F32)],
+        [((REACH, 512), F32), ((PATCH_DEV, 768), F32), ((3072, TILE), F32), ((3072, TILE), F32)],
         (*own, index),
         flops=8 * 10**9,
     )
     sent, k_part, v_part, q_part = call(
         far_kernel,
         [((2 * PATCH_DEV + REACH, 256), BF16), ((WINDOW, 256), BF16), ((WINDOW, 256), BF16), ((256, WINDOW), BF16)],
-        (*own, packed, index, near),
+        (*own, packed, index, near, s_own, dp_own),
         flops=8 * 10**9,
     )
     arrived = lax.ppermute(sent, "seq", back)

time: 49.6 us -> 48.7 us (0.982)
  Pallas kernels: 19.3 us -> 18.4 us
    pallas_call x8, Pallas kernels: 19.3 us -> 18.4 us  [call(): pl.pallas_call(kernel, out_shape=[jax.ShapeDtypeStruct(*shape) for shape...]
  transfers between devices with their start and end apart: 6 -> 6, of which waited for: 5 -> 5; matrix products, arithmetic and copies ran while one was open for 0% -> 0% of each run, Pallas kernels for 21% -> 22%
where the time goes in v5:
time: 48.7 us; the launch traced here: 48.5 us
  Pallas kernels  18.4 us (38%)
  waiting for transfers between devices  14.6 us (30%)
  starting transfers between devices  14 us (29%)
  local copies, waits for them, and re-layouts  1.08 us (2%)
    pallas_call x8, Pallas kernels, call(): pl.pallas_call(kernel, out_shape=[jax.ShapeDtypeStruct(*shape) for shape...  18.4 us
    ppermute x1, waiting for transfers between devices, on_device(): arrived = lax.ppermute(sent, 'seq', back)  6.83 us
    ppermute x1, starting transfers between devices, on_device(): packed = lax.ppermute(packed, 'seq', onward)  5.36 us
    ppermute x2, waiting for transfers between devices, on_device(): a_in, b_in = (lax.ppermute(a, 'mp', across), lax.ppermute(b, 'mp', around))  4.01 us
    ppermute x2, waiting for transfers between devices, on_device(): a_in, b_in = (lax.ppermute(a, 'mp', around), lax.ppermute(b, 'mp', across))  3.74 us
    ppermute x2, starting transfers between devices, on_device(): a_in, b_in = (lax.ppermute(a, 'mp', across), lax.ppermute(b, 'mp', around))  3.47 us
    ppermute x2, starting transfers between devices, on_device(): a_in, b_in = (lax.ppermute(a, 'mp', around), lax.ppermute(b, 'mp', across))  3.23 us
    ppermute x1, starting transfers between devices, on_device(): arrived = lax.ppermute(sent, 'seq', back)  1.92 us
  transfers between devices with their start and end apart: 6, of which 5 were waited for; matrix products, arithmetic and copies ran while one was open for 0% of the time, Pallas kernels for 22%

profile of v5, /device:TPU:103, one launch (start us, length us, event | category | flops | bytes accessed | tf_op | source)
XLA Modules:
  0.0 48.5 jit_solution(4226847488905605265)
XLA Ops:
  0.0 1.8 %shard_map.101 = bf16[1040,256]{1,0:T(8,128)(2,1)} custom-call(bf16[1024,256]{1,0:T(8,128)(2,1)} %keys.7, bf16[1024,256]{1,0:T(8,128)(2,1)} %values.7, s32[1,1024]{1,0:T(1,128)} %bitcast.1), custom_call_target="tpu_custom_call" | custom-call | flops 1000000 | tf_op jit(solution)/shard_map/pallas_call | solution.py:371
  1.8 0.0 copy-start.1
  1.9 0.0 copy-start.2
  1.9 0.0 copy-start.6
  1.9 5.4 %collective-permute-start = (bf16[1040,256]{1,0:T(8,128)(2,1)}, bf16[1040,256]{1,0:T(8,128)(2,1)S(1)}, u32[]{:S(2)}, u32[]{:S(2)}) collective-permute-start(bf16[1040,256]{1,0:T(8,128)(2,1)} %shard_map.101), channel_id=1, source_target_pairs={{0,4},{4,8},{8,12},{12,16},{16,20},{20,24},{24,28},{28,32},{32,36}... | collective-permute-start | bytes 1597448 | tf_op jit(solution)/shard_map/ppermute | solution.py:405
  7.3 0.0 copy-start.7
  7.3 1.0 %copy-done.7 = bf16[256,1024]{1,0:T(8,128)(2,1)S(1)} copy-done((bf16[256,1024]{1,0:T(8,128)(2,1)S(1)}, bf16[256,1024]{1,0:T(8,128)(2,1)}, u32[]{:S(2)}) %copy-start.7) | copy-done | bytes 524312
  8.3 0.0 copy-start.8
  8.3 2.8 %shard_map.100.grads = bf16[1024,256]{1,0:T(8,128)(2,1)S(1)} custom-call(bf16[1024,1024]{1,0:T(8,128)(2,1)} %d_output_hbm.1, bf16[256,1024]{1,0:T(8,128)(2,1)S(1)} %copy-done.7), custom_call_target="tpu_custom_call" | custom-call | flops 8000000000 | tf_op jit(solution)/shard_map/pallas_call | solution.py:371
  11.1 0.0 copy-done.1
  11.1 0.0 copy-done.2
  11.1 0.0 copy-done.6
  11.1 0.0 copy-done.8
  11.1 3.6 %shard_map.102 = (f32[128,512]{1,0:T(8,128)S(1)}, f32[256,768]{1,0:T(8,128)S(1)}, f32[3072,256]{1,0:T(8,128)S(1)}, f32[3072,256]{1,0:T(8,128)S(1)}) custom-call(bf16[1024,256]{1,0:T(8,128)(2,1)S(1)} %shard_map.100.grads, bf16[1024,256]{1,0:T(8,128)(2,1)S(1)} %copy-done.8, bf16[1024,256]{1,0:T(8,128)(2,1)S(1)} %copy-done.1, bf16[1024,256]{1,0:T(8,128)(2,1)S(1)} %copy-done.2, ...), custom_call_target="tpu_custom_call" | custom-call | flops 8000000000 | tf_op jit(solution)/shard_map/pallas_call | solution.py:371
  14.8 0.0 collective-permute-done.packed
  14.8 4.3 %shard_map.103 = (bf16[640,256]{1,0:T(8,128)(2,1)S(1)}, bf16[512,256]{1,0:T(8,128)(2,1)S(1)}, bf16[512,256]{1,0:T(8,128)(2,1)S(1)}, bf16[256,512]{1,0:T(8,128)(2,1)S(1)}) custom-call(bf16[1024,256]{1,0:T(8,128)(2,1)S(1)} %shard_map.100.grads, bf16[1024,256]{1,0:T(8,128)(2,1)S(1)} %copy-done.8, bf16[1024,256]{1,0:T(8,128)(2,1)S(1)} %copy-done.1, ...), custom_call_target="tpu_custom_call" | custom-call | flops 8000000000 | tf_op jit(solution)/shard_map/pallas_call | solution.py:371
  19.1 1.9 %collective-permute-start.1 = (bf16[640,256]{1,0:T(8,128)(2,1)S(1)}, bf16[640,256]{1,0:T(8,128)(2,1)S(1)}, u32[]{:S(2)}, u32[]{:S(2)}) collective-permute-start(bf16[640,256]{1,0:T(8,128)(2,1)S(1)} %get-tuple-element.22), channel_id=1, source_target_pairs={{4,0},{8,4},{12,8},{16,12},{20,16},{24,20},{28,24},{32,28},{36,32}... | collective-permute-start | bytes 983048 | tf_op jit(solution)/shard_map/ppermute | solution.py:428
  21.0 0.0 copy-start.3
  21.0 0.0 copy-start.4
  21.0 0.0 copy-start.5
  21.1 2.9 %shard_map.104.x_in = f32[256,768]{1,0:T(8,128)S(1)} custom-call(bf16[1024,256]{1,0:T(8,128)(2,1)S(1)} %shard_map.100.grads, bf16[1024,256]{1,0:T(8,128)(2,1)S(1)} %copy-done.8, bf16[1024,256]{1,0:T(8,128)(2,1)S(1)} %copy-done.1, bf16[1024,256]{1,0:T(8,128)(2,1)S(1)} %copy-done.2, s32[1,1024]{1,0:T(1,128)S(1)} %bitcast.4, ...), custom_call_target="tpu_custom_call" | custom-call | flops 8000000000 | tf_op jit(solution)/shard_map/pallas_call | solution.py:371
  24.0 0.0 copy-start
  24.0 6.8 %collective-permute-done.1.arrived = bf16[640,256]{1,0:T(8,128)(2,1)S(1)} collective-permute-done((bf16[640,256]{1,0:T(8,128)(2,1)S(1)}, bf16[640,256]{1,0:T(8,128)(2,1)S(1)}, u32[]{:S(2)}, u32[]{:S(2)}) %collective-permute-start.1) | collective-permute-done | bytes 327712 | tf_op jit(solution)/shard_map/ppermute | solution.py:428
  30.8 0.0 copy-done.3
  30.8 0.0 copy-done.4
  30.8 0.0 copy-done.5
  30.8 0.6 %shard_map.105 = (bf16[128,1024]{1,0:T(8,128)(2,1)S(1)}, bf16[128,1024]{1,0:T(8,128)(2,1)S(1)}) custom-call(f32[256,768]{1,0:T(8,128)S(1)} %shard_map.104.x_in, bf16[640,256]{1,0:T(8,128)(2,1)S(1)} %collective-permute-done.1.arrived, bf16[1024,256]{1,0:T(8,128)(2,1)S(1)} %copy-done.3, bf16[1024,256]{1,0:T(8,128)(2,1)S(1)} %copy-done.4, ...), custom_call_target="tpu_custom_call" | custom-call | flops 400000000 | tf_op jit(solution)/shard_map/pallas_call | solution.py:371
  31.4 1.6 %collective-permute-start.4 = (bf16[128,1024]{1,0:T(8,128)(2,1)S(1)}, bf16[128,1024]{1,0:T(8,128)(2,1)S(1)}, u32[]{:S(2)}, u32[]{:S(2)}) collective-permute-start(bf16[128,1024]{1,0:T(8,128)(2,1)S(1)} %get-tuple-element.24), channel_id=1, source_target_pairs={{0,1},{1,0},{2,3},{3,2},{4,5},{5,4},{6,7},{7,6},{8,9},{9,8},{10,11... | collective-permute-start | bytes 786440 | tf_op jit(solution)/shard_map/ppermute | solution.py:447
  33.0 1.9 %collective-permute-start.2 = (bf16[128,1024]{1,0:T(8,128)(2,1)S(1)}, bf16[128,1024]{1,0:T(8,128)(2,1)S(1)}, u32[]{:S(2)}, u32[]{:S(2)}) collective-permute-start(bf16[128,1024]{1,0:T(8,128)(2,1)S(1)} %get-tuple-element.23), channel_id=1, source_target_pairs={{0,3},{3,0},{1,2},{2,1},{4,7},{7,4},{5,6},{6,5},{8,11},{11,8},{9,1... | collective-permute-start | bytes 786440 | tf_op jit(solution)/shard_map/ppermute | solution.py:447
  34.9 2.3 %collective-permute-done.4 = bf16[128,1024]{1,0:T(8,128)(2,1)S(1)} collective-permute-done((bf16[128,1024]{1,0:T(8,128)(2,1)S(1)}, bf16[128,1024]{1,0:T(8,128)(2,1)S(1)}, u32[]{:S(2)}, u32[]{:S(2)}) %collective-permute-start.4) | collective-permute-done | bytes 262176 | tf_op jit(solution)/shard_map/ppermute | solution.py:447
  37.2 0.1 add_convert_fusion.mine
  37.3 2.8 %collective-permute-start.5 = (bf16[128,1024]{1,0:T(8,128)(2,1)S(1)}, bf16[128,1024]{1,0:T(8,128)(2,1)S(1)}, u32[]{:S(2)}, u32[]{:S(2)}) collective-permute-start(bf16[128,1024]{1,0:T(8,128)(2,1)S(1)} %add_convert_fusion.mine), channel_id=1, source_target_pairs={{0,3},{3,0},{1,2},{2,1},{4,7},{7,4},{5,6},{6,5},{8,11},{11,8},{9,1... | collective-permute-start | bytes 786440 | tf_op jit(solution)/shard_map/ppermute | solution.py:449
  40.1 1.7 %collective-permute-done.2 = bf16[128,1024]{1,0:T(8,128)(2,1)S(1)} collective-permute-done((bf16[128,1024]{1,0:T(8,128)(2,1)S(1)}, bf16[128,1024]{1,0:T(8,128)(2,1)S(1)}, u32[]{:S(2)}, u32[]{:S(2)}) %collective-permute-start.2) | collective-permute-done | bytes 262176 | tf_op jit(solution)/shard_map/ppermute | solution.py:447
  41.8 0.1 add_convert_fusion.1.mine
  41.9 0.4 collective-permute-start.3
  42.3 2.3 %collective-permute-done.5.other = bf16[128,1024]{1,0:T(8,128)(2,1)S(1)} collective-permute-done((bf16[128,1024]{1,0:T(8,128)(2,1)S(1)}, bf16[128,1024]{1,0:T(8,128)(2,1)S(1)}, u32[]{:S(2)}, u32[]{:S(2)}) %collective-permute-start.5) | collective-permute-done | bytes 262176 | tf_op jit(solution)/shard_map/ppermute | solution.py:449
  44.6 0.0 copy-done
  44.6 1.1 %shard_map.106.refs_0_ = bf16[256,1024]{1,0:T(8,128)(2,1)} custom-call(bf16[128,1024]{1,0:T(8,128)(2,1)S(1)} %add_convert_fusion.mine, bf16[128,1024]{1,0:T(8,128)(2,1)S(1)} %collective-permute-done.5.other, bf16[1024,1024]{1,0:T(8,128)(2,1)S(1)} %copy-done), custom_call_target="tpu_custom_call" | custom-call | flops 300000000 | tf_op jit(solution)/shard_map/pallas_call | solution.py:371
  45.8 1.4 %collective-permute-done.3.other = bf16[128,1024]{1,0:T(8,128)(2,1)S(1)} collective-permute-done((bf16[128,1024]{1,0:T(8,128)(2,1)S(1)}, bf16[128,1024]{1,0:T(8,128)(2,1)S(1)}, u32[]{:S(2)}, u32[]{:S(2)}) %collective-permute-start.3) | collective-permute-done | bytes 262176 | tf_op jit(solution)/shard_map/ppermute | solution.py:449
  47.2 1.1 %shard_map.107 = bf16[256,1024]{1,0:T(8,128)(2,1)} custom-call(bf16[128,1024]{1,0:T(8,128)(2,1)S(1)} %add_convert_fusion.1.mine, bf16[128,1024]{1,0:T(8,128)(2,1)S(1)} %collective-permute-done.3.other, bf16[1024,1024]{1,0:T(8,128)(2,1)S(1)} %copy-done, bf16[256,1024]{1,0:T(8,128)(2,1)} %shard_map.106.refs_0_), custom_call_target="tpu_custom_call", output_to_operand_aliasing={{}: (3, {})} | custom-call | flops 300000000 | tf_op jit(solution)/shard_map/pallas_call | solution.py:371
Async XLA Ops:
  1.8 9.3 %copy-start.1 = (bf16[1024,256]{1,0:T(8,128)(2,1)S(1)}, bf16[1024,256]{1,0:T(8,128)(2,1)}, u32[]{:S(2)}) copy-start(bf16[1024,256]{1,0:T(8,128)(2,1)} %keys.7) | copy-start | bytes 1572868
  1.9 9.2 %copy-start.2 = (bf16[1024,256]{1,0:T(8,128)(2,1)S(1)}, bf16[1024,256]{1,0:T(8,128)(2,1)}, u32[]{:S(2)}) copy-start(bf16[1024,256]{1,0:T(8,128)(2,1)} %values.7) | copy-start | bytes 1572868
  1.9 9.2 %copy-start.6 = (s32[1024]{0:T(1024)S(1)}, s32[1024]{0:T(1024)}, u32[]{:S(2)}) copy-start(s32[1024]{0:T(1024)} %param.18) | copy-start | bytes 12292
  1.9 12.9 %collective-permute-start = (bf16[1040,256]{1,0:T(8,128)(2,1)}, bf16[1040,256]{1,0:T(8,128)(2,1)S(1)}, u32[]{:S(2)}, u32[]{:S(2)}) collective-permute-start(bf16[1040,256]{1,0:T(8,128)(2,1)} %shard_map.101), channel_id=1, source_target_pairs={{0,4},{4,8},{8,12},{12,16},{16,20},{20,24},{24,28},{28,32},{32,36}... | collective-permute-start | bytes 1597448 | tf_op jit(solution)/shard_map/ppermute | solution.py:405
  7.3 1.0 %copy-start.7 = (bf16[256,1024]{1,0:T(8,128)(2,1)S(1)}, bf16[256,1024]{1,0:T(8,128)(2,1)}, u32[]{:S(2)}) copy-start(bf16[256,1024]{1,0:T(8,128)(2,1)} %w_out_hbm.1) | copy-start | bytes 1572868
  8.3 2.8 %copy-start.8 = (bf16[1024,256]{1,0:T(8,128)(2,1)S(1)}, bf16[1024,256]{1,0:T(8,128)(2,1)}, u32[]{:S(2)}) copy-start(bf16[1024,256]{1,0:T(8,128)(2,1)} %queries.5) | copy-start | bytes 1572868
  19.1 11.7 %collective-permute-start.1 = (bf16[640,256]{1,0:T(8,128)(2,1)S(1)}, bf16[640,256]{1,0:T(8,128)(2,1)S(1)}, u32[]{:S(2)}, u32[]{:S(2)}) collective-permute-start(bf16[640,256]{1,0:T(8,128)(2,1)S(1)} %get-tuple-element.22), channel_id=1, source_target_pairs={{4,0},{8,4},{12,8},{16,12},{20,16},{24,20},{28,24},{32,28},{36,32}... | collective-permute-start | bytes 983048 | tf_op jit(solution)/shard_map/ppermute | solution.py:428
  21.0 9.8 %copy-start.3 = (bf16[1024,256]{1,0:T(8,128)(2,1)S(1)}, bf16[1024,256]{1,0:T(8,128)(2,1)}, u32[]{:S(2)}) copy-start(bf16[1024,256]{1,0:T(8,128)(2,1)} %w_query.1) | copy-start | bytes 1572868
  21.0 9.8 %copy-start.4 = (bf16[1024,256]{1,0:T(8,128)(2,1)S(1)}, bf16[1024,256]{1,0:T(8,128)(2,1)}, u32[]{:S(2)}) copy-start(bf16[1024,256]{1,0:T(8,128)(2,1)} %w_key.1) | copy-start | bytes 1572868
  21.0 9.8 %copy-start.5 = (bf16[1024,256]{1,0:T(8,128)(2,1)S(1)}, bf16[1024,256]{1,0:T(8,128)(2,1)}, u32[]{:S(2)}) copy-start(bf16[1024,256]{1,0:T(8,128)(2,1)} %w_value.1) | copy-start | bytes 1572868
  24.0 20.7 %copy-start = (bf16[1024,1024]{1,0:T(8,128)(2,1)S(1)}, bf16[1024,1024]{1,0:T(8,128)(2,1)}, u32[]{:S(2)}) copy-start(bf16[1024,1024]{1,0:T(8,128)(2,1)} %unpatch.3) | copy-start | bytes 6291460
  31.4 5.8 %collective-permute-start.4 = (bf16[128,1024]{1,0:T(8,128)(2,1)S(1)}, bf16[128,1024]{1,0:T(8,128)(2,1)S(1)}, u32[]{:S(2)}, u32[]{:S(2)}) collective-permute-start(bf16[128,1024]{1,0:T(8,128)(2,1)S(1)} %get-tuple-element.24), channel_id=1, source_target_pairs={{0,1},{1,0},{2,3},{3,2},{4,5},{5,4},{6,7},{7,6},{8,9},{9,8},{10,11... | collective-permute-start | bytes 786440 | tf_op jit(solution)/shard_map/ppermute | solution.py:447
  33.0 8.8 %collective-permute-start.2 = (bf16[128,1024]{1,0:T(8,128)(2,1)S(1)}, bf16[128,1024]{1,0:T(8,128)(2,1)S(1)}, u32[]{:S(2)}, u32[]{:S(2)}) collective-permute-start(bf16[128,1024]{1,0:T(8,128)(2,1)S(1)} %get-tuple-element.23), channel_id=1, source_target_pairs={{0,3},{3,0},{1,2},{2,1},{4,7},{7,4},{5,6},{6,5},{8,11},{11,8},{9,1... | collective-permute-start | bytes 786440 | tf_op jit(solution)/shard_map/ppermute | solution.py:447
  37.3 7.3 %collective-permute-start.5 = (bf16[128,1024]{1,0:T(8,128)(2,1)S(1)}, bf16[128,1024]{1,0:T(8,128)(2,1)S(1)}, u32[]{:S(2)}, u32[]{:S(2)}) collective-permute-start(bf16[128,1024]{1,0:T(8,128)(2,1)S(1)} %add_convert_fusion.mine), channel_id=1, source_target_pairs={{0,3},{3,0},{1,2},{2,1},{4,7},{7,4},{5,6},{6,5},{8,11},{11,8},{9,1... | collective-permute-start | bytes 786440 | tf_op jit(solution)/shard_map/ppermute | solution.py:449
  41.9 5.3 %collective-permute-start.3 = (bf16[128,1024]{1,0:T(8,128)(2,1)S(1)}, bf16[128,1024]{1,0:T(8,128)(2,1)S(1)}, u32[]{:S(2)}, u32[]{:S(2)}) collective-permute-start(bf16[128,1024]{1,0:T(8,128)(2,1)S(1)} %add_convert_fusion.1.mine), channel_id=1, source_target_pairs={{0,1},{1,0},{2,3},{3,2},{4,5},{5,4},{6,7},{7,6},{8,9},{9,8},{10,11... | collective-permute-start | bytes 786440 | tf_op jit(solution)/shard_map/ppermute | solution.py:449

commit v6 on v5

--- a/solution.py
+++ b/solution.py
@@ -375,7 +375,7 @@
         out_specs=[pl.BlockSpec(memory_space=out_space)] * len(shapes),
         input_output_aliases=aliases,
         scratch_shapes=list(scratch),
-        compiler_params=pltpu.CompilerParams(vmem_limit_bytes=vmem * 1024 * 1024),
+        compiler_params=pltpu.CompilerParams(vmem_limit_bytes=int(vmem * 1024 * 1024)),
         cost_estimate=pl.CostEstimate(flops=flops, bytes_accessed=0, transcendentals=0),
     )(*args)
 
@@ -409,7 +409,7 @@
         (d_output, w_out),
         [pltpu.VMEM((1024, 1024), BF16), pltpu.VMEM((256, 1024), BF16), pltpu.SemaphoreType.DMA((3,))],
         flops=8 * 10**9,
-        vmem=52,
+        vmem=53.2,
         whole=(0, 1),
     )[0]
     own = (grads, queries, byte_keys, byte_values)

time: 48.7 us -> 48.3 us (level)
  local copies, waits for them, and re-layouts: 1.08 us -> 0.05 us
  waiting for transfers between devices: 14.6 us -> 15.2 us
    unnamed x18 -> x16, local copies, waits for them, and re-layouts: 1.08 us -> 0.05 us
    ppermute x1, waiting for transfers between devices: 6.83 us -> 7.39 us  [on_device(): arrived = lax.ppermute(sent, 'seq', back)]
where the time goes in v6:
time: 48.3 us; the launch traced here: 48.1 us
  Pallas kernels  18.4 us (38%)
  waiting for transfers between devices  15.2 us (31%)
  starting transfers between devices  14 us (29%)
    pallas_call x8, Pallas kernels, call(): pl.pallas_call(kernel, out_shape=[jax.ShapeDtypeStruct(*shape) for shape...  18.4 us
    ppermute x1, waiting for transfers between devices, on_device(): arrived = lax.ppermute(sent, 'seq', back)  7.39 us
    ppermute x1, starting transfers between devices, on_device(): packed = lax.ppermute(packed, 'seq', onward)  5.36 us
    ppermute x2, waiting for transfers between devices, on_device(): a_in, b_in = (lax.ppermute(a, 'mp', across), lax.ppermute(b, 'mp', around))  4.02 us
    ppermute x2, waiting for transfers between devices, on_device(): a_in, b_in = (lax.ppermute(a, 'mp', around), lax.ppermute(b, 'mp', across))  3.75 us
    ppermute x2, starting transfers between devices, on_device(): a_in, b_in = (lax.ppermute(a, 'mp', across), lax.ppermute(b, 'mp', around))  3.46 us
    ppermute x2, starting transfers between devices, on_device(): a_in, b_in = (lax.ppermute(a, 'mp', around), lax.ppermute(b, 'mp', across))  3.22 us
    ppermute x1, starting transfers between devices, on_device(): arrived = lax.ppermute(sent, 'seq', back)  1.92 us
  transfers between devices with their start and end apart: 6, of which 5 were waited for; matrix products, arithmetic and copies ran while one was open for 0% of the time, Pallas kernels for 22%

profile of v6, /device:TPU:103, one launch (start us, length us, event | category | flops | bytes accessed | tf_op | source)
XLA Modules:
  0.0 48.1 jit_solution(2320127930729921922)
XLA Ops:
  0.0 1.8 %shard_map.101 = bf16[1040,256]{1,0:T(8,128)(2,1)} custom-call(bf16[1024,256]{1,0:T(8,128)(2,1)} %keys.7, bf16[1024,256]{1,0:T(8,128)(2,1)} %values.7, s32[1,1024]{1,0:T(1,128)} %bitcast.1), custom_call_target="tpu_custom_call" | custom-call | flops 1000000 | tf_op jit(solution)/shard_map/pallas_call | solution.py:371
  1.9 0.0 copy-start.1
  1.9 0.0 copy-start.2
  1.9 0.0 copy-start.6
  1.9 0.0 copy-start.7
  1.9 5.4 %collective-permute-start = (bf16[1040,256]{1,0:T(8,128)(2,1)}, bf16[1040,256]{1,0:T(8,128)(2,1)S(1)}, u32[]{:S(2)}, u32[]{:S(2)}) collective-permute-start(bf16[1040,256]{1,0:T(8,128)(2,1)} %shard_map.101), channel_id=1, source_target_pairs={{0,4},{4,8},{8,12},{12,16},{16,20},{20,24},{24,28},{28,32},{32,36}... | collective-permute-start | bytes 1597448 | tf_op jit(solution)/shard_map/ppermute | solution.py:405
  7.3 2.9 %shard_map.100.grads = bf16[1024,256]{1,0:T(8,128)(2,1)S(1)} custom-call(bf16[1024,1024]{1,0:T(8,128)(2,1)} %d_output_hbm.1, bf16[256,1024]{1,0:T(8,128)(2,1)} %w_out_hbm.1), custom_call_target="tpu_custom_call" | custom-call | flops 8000000000 | tf_op jit(solution)/shard_map/pallas_call | solution.py:371
  10.1 0.0 copy-done.1
  10.2 0.0 copy-done.2
  10.2 0.0 copy-done.6
  10.2 0.0 copy-done.7
  10.2 3.6 %shard_map.102 = (f32[128,512]{1,0:T(8,128)S(1)}, f32[256,768]{1,0:T(8,128)S(1)}, f32[3072,256]{1,0:T(8,128)S(1)}, f32[3072,256]{1,0:T(8,128)S(1)}) custom-call(bf16[1024,256]{1,0:T(8,128)(2,1)S(1)} %shard_map.100.grads, bf16[1024,256]{1,0:T(8,128)(2,1)S(1)} %copy-done.7, bf16[1024,256]{1,0:T(8,128)(2,1)S(1)} %copy-done.1, bf16[1024,256]{1,0:T(8,128)(2,1)S(1)} %copy-done.2, ...), custom_call_target="tpu_custom_call" | custom-call | flops 8000000000 | tf_op jit(solution)/shard_map/pallas_call | solution.py:371
  13.8 0.0 collective-permute-done.packed
  13.9 4.3 %shard_map.103 = (bf16[640,256]{1,0:T(8,128)(2,1)S(1)}, bf16[512,256]{1,0:T(8,128)(2,1)S(1)}, bf16[512,256]{1,0:T(8,128)(2,1)S(1)}, bf16[256,512]{1,0:T(8,128)(2,1)S(1)}) custom-call(bf16[1024,256]{1,0:T(8,128)(2,1)S(1)} %shard_map.100.grads, bf16[1024,256]{1,0:T(8,128)(2,1)S(1)} %copy-done.7, bf16[1024,256]{1,0:T(8,128)(2,1)S(1)} %copy-done.1, ...), custom_call_target="tpu_custom_call" | custom-call | flops 8000000000 | tf_op jit(solution)/shard_map/pallas_call | solution.py:371
  18.1 1.9 %collective-permute-start.1 = (bf16[640,256]{1,0:T(8,128)(2,1)S(1)}, bf16[640,256]{1,0:T(8,128)(2,1)S(1)}, u32[]{:S(2)}, u32[]{:S(2)}) collective-permute-start(bf16[640,256]{1,0:T(8,128)(2,1)S(1)} %get-tuple-element.22), channel_id=1, source_target_pairs={{4,0},{8,4},{12,8},{16,12},{20,16},{24,20},{28,24},{32,28},{36,32}... | collective-permute-start | bytes 983048 | tf_op jit(solution)/shard_map/ppermute | solution.py:428
  20.1 0.0 copy-start.3
  20.1 0.0 copy-start.4
  20.1 0.0 copy-start.5
  20.1 2.9 %shard_map.104.x_in = f32[256,768]{1,0:T(8,128)S(1)} custom-call(bf16[1024,256]{1,0:T(8,128)(2,1)S(1)} %shard_map.100.grads, bf16[1024,256]{1,0:T(8,128)(2,1)S(1)} %copy-done.7, bf16[1024,256]{1,0:T(8,128)(2,1)S(1)} %copy-done.1, bf16[1024,256]{1,0:T(8,128)(2,1)S(1)} %copy-done.2, s32[1,1024]{1,0:T(1,128)S(1)} %bitcast.4, ...), custom_call_target="tpu_custom_call" | custom-call | flops 8000000000 | tf_op jit(solution)/shard_map/pallas_call | solution.py:371
  23.0 0.0 copy-start
  23.0 7.4 %collective-permute-done.1.arrived = bf16[640,256]{1,0:T(8,128)(2,1)S(1)} collective-permute-done((bf16[640,256]{1,0:T(8,128)(2,1)S(1)}, bf16[640,256]{1,0:T(8,128)(2,1)S(1)}, u32[]{:S(2)}, u32[]{:S(2)}) %collective-permute-start.1) | collective-permute-done | bytes 327712 | tf_op jit(solution)/shard_map/ppermute | solution.py:428
  30.4 0.0 copy-done.3
  30.4 0.0 copy-done.4
  30.4 0.0 copy-done.5
  30.4 0.6 %shard_map.105 = (bf16[128,1024]{1,0:T(8,128)(2,1)S(1)}, bf16[128,1024]{1,0:T(8,128)(2,1)S(1)}) custom-call(f32[256,768]{1,0:T(8,128)S(1)} %shard_map.104.x_in, bf16[640,256]{1,0:T(8,128)(2,1)S(1)} %collective-permute-done.1.arrived, bf16[1024,256]{1,0:T(8,128)(2,1)S(1)} %copy-done.3, bf16[1024,256]{1,0:T(8,128)(2,1)S(1)} %copy-done.4, ...), custom_call_target="tpu_custom_call" | custom-call | flops 400000000 | tf_op jit(solution)/shard_map/pallas_call | solution.py:371
  31.1 1.6 %collective-permute-start.4 = (bf16[128,1024]{1,0:T(8,128)(2,1)S(1)}, bf16[128,1024]{1,0:T(8,128)(2,1)S(1)}, u32[]{:S(2)}, u32[]{:S(2)}) collective-permute-start(bf16[128,1024]{1,0:T(8,128)(2,1)S(1)} %get-tuple-element.24), channel_id=1, source_target_pairs={{0,1},{1,0},{2,3},{3,2},{4,5},{5,4},{6,7},{7,6},{8,9},{9,8},{10,11... | collective-permute-start | bytes 786440 | tf_op jit(solution)/shard_map/ppermute | solution.py:447
  32.6 1.9 %collective-permute-start.2 = (bf16[128,1024]{1,0:T(8,128)(2,1)S(1)}, bf16[128,1024]{1,0:T(8,128)(2,1)S(1)}, u32[]{:S(2)}, u32[]{:S(2)}) collective-permute-start(bf16[128,1024]{1,0:T(8,128)(2,1)S(1)} %get-tuple-element.23), channel_id=1, source_target_pairs={{0,3},{3,0},{1,2},{2,1},{4,7},{7,4},{5,6},{6,5},{8,11},{11,8},{9,1... | collective-permute-start | bytes 786440 | tf_op jit(solution)/shard_map/ppermute | solution.py:447
  34.5 2.3 %collective-permute-done.4 = bf16[128,1024]{1,0:T(8,128)(2,1)S(1)} collective-permute-done((bf16[128,1024]{1,0:T(8,128)(2,1)S(1)}, bf16[128,1024]{1,0:T(8,128)(2,1)S(1)}, u32[]{:S(2)}, u32[]{:S(2)}) %collective-permute-start.4) | collective-permute-done | bytes 262176 | tf_op jit(solution)/shard_map/ppermute | solution.py:447
  36.8 0.1 add_convert_fusion.mine
  36.9 2.8 %collective-permute-start.5 = (bf16[128,1024]{1,0:T(8,128)(2,1)S(1)}, bf16[128,1024]{1,0:T(8,128)(2,1)S(1)}, u32[]{:S(2)}, u32[]{:S(2)}) collective-permute-start(bf16[128,1024]{1,0:T(8,128)(2,1)S(1)} %add_convert_fusion.mine), channel_id=1, source_target_pairs={{0,3},{3,0},{1,2},{2,1},{4,7},{7,4},{5,6},{6,5},{8,11},{11,8},{9,1... | collective-permute-start | bytes 786440 | tf_op jit(solution)/shard_map/ppermute | solution.py:449
  39.7 1.7 %collective-permute-done.2 = bf16[128,1024]{1,0:T(8,128)(2,1)S(1)} collective-permute-done((bf16[128,1024]{1,0:T(8,128)(2,1)S(1)}, bf16[128,1024]{1,0:T(8,128)(2,1)S(1)}, u32[]{:S(2)}, u32[]{:S(2)}) %collective-permute-start.2) | collective-permute-done | bytes 262176 | tf_op jit(solution)/shard_map/ppermute | solution.py:447
  41.4 0.1 add_convert_fusion.1.mine
  41.5 0.4 collective-permute-start.3
  41.9 2.3 %collective-permute-done.5.other = bf16[128,1024]{1,0:T(8,128)(2,1)S(1)} collective-permute-done((bf16[128,1024]{1,0:T(8,128)(2,1)S(1)}, bf16[128,1024]{1,0:T(8,128)(2,1)S(1)}, u32[]{:S(2)}, u32[]{:S(2)}) %collective-permute-start.5) | collective-permute-done | bytes 262176 | tf_op jit(solution)/shard_map/ppermute | solution.py:449
  44.2 0.0 copy-done
  44.2 1.1 %shard_map.106.refs_0_ = bf16[256,1024]{1,0:T(8,128)(2,1)} custom-call(bf16[128,1024]{1,0:T(8,128)(2,1)S(1)} %add_convert_fusion.mine, bf16[128,1024]{1,0:T(8,128)(2,1)S(1)} %collective-permute-done.5.other, bf16[1024,1024]{1,0:T(8,128)(2,1)S(1)} %copy-done), custom_call_target="tpu_custom_call" | custom-call | flops 300000000 | tf_op jit(solution)/shard_map/pallas_call | solution.py:371
  45.4 1.4 %collective-permute-done.3.other = bf16[128,1024]{1,0:T(8,128)(2,1)S(1)} collective-permute-done((bf16[128,1024]{1,0:T(8,128)(2,1)S(1)}, bf16[128,1024]{1,0:T(8,128)(2,1)S(1)}, u32[]{:S(2)}, u32[]{:S(2)}) %collective-permute-start.3) | collective-permute-done | bytes 262176 | tf_op jit(solution)/shard_map/ppermute | solution.py:449
  46.8 1.1 %shard_map.107 = bf16[256,1024]{1,0:T(8,128)(2,1)} custom-call(bf16[128,1024]{1,0:T(8,128)(2,1)S(1)} %add_convert_fusion.1.mine, bf16[128,1024]{1,0:T(8,128)(2,1)S(1)} %collective-permute-done.3.other, bf16[1024,1024]{1,0:T(8,128)(2,1)S(1)} %copy-done, bf16[256,1024]{1,0:T(8,128)(2,1)} %shard_map.106.refs_0_), custom_call_target="tpu_custom_call", output_to_operand_aliasing={{}: (3, {})} | custom-call | flops 300000000 | tf_op jit(solution)/shard_map/pallas_call | solution.py:371
Async XLA Ops:
  1.9 8.3 %copy-start.1 = (bf16[1024,256]{1,0:T(8,128)(2,1)S(1)}, bf16[1024,256]{1,0:T(8,128)(2,1)}, u32[]{:S(2)}) copy-start(bf16[1024,256]{1,0:T(8,128)(2,1)} %keys.7) | copy-start | bytes 1572868
  1.9 8.3 %copy-start.2 = (bf16[1024,256]{1,0:T(8,128)(2,1)S(1)}, bf16[1024,256]{1,0:T(8,128)(2,1)}, u32[]{:S(2)}) copy-start(bf16[1024,256]{1,0:T(8,128)(2,1)} %values.7) | copy-start | bytes 1572868
  1.9 8.3 %copy-start.6 = (s32[1024]{0:T(1024)S(1)}, s32[1024]{0:T(1024)}, u32[]{:S(2)}) copy-start(s32[1024]{0:T(1024)} %param.18) | copy-start | bytes 12292
  1.9 8.3 %copy-start.7 = (bf16[1024,256]{1,0:T(8,128)(2,1)S(1)}, bf16[1024,256]{1,0:T(8,128)(2,1)}, u32[]{:S(2)}) copy-start(bf16[1024,256]{1,0:T(8,128)(2,1)} %queries.5) | copy-start | bytes 1572868
  1.9 11.9 %collective-permute-start = (bf16[1040,256]{1,0:T(8,128)(2,1)}, bf16[1040,256]{1,0:T(8,128)(2,1)S(1)}, u32[]{:S(2)}, u32[]{:S(2)}) collective-permute-start(bf16[1040,256]{1,0:T(8,128)(2,1)} %shard_map.101), channel_id=1, source_target_pairs={{0,4},{4,8},{8,12},{12,16},{16,20},{20,24},{24,28},{28,32},{32,36}... | collective-permute-start | bytes 1597448 | tf_op jit(solution)/shard_map/ppermute | solution.py:405
  18.1 12.3 %collective-permute-start.1 = (bf16[640,256]{1,0:T(8,128)(2,1)S(1)}, bf16[640,256]{1,0:T(8,128)(2,1)S(1)}, u32[]{:S(2)}, u32[]{:S(2)}) collective-permute-start(bf16[640,256]{1,0:T(8,128)(2,1)S(1)} %get-tuple-element.22), channel_id=1, source_target_pairs={{4,0},{8,4},{12,8},{16,12},{20,16},{24,20},{28,24},{32,28},{36,32}... | collective-permute-start | bytes 983048 | tf_op jit(solution)/shard_map/ppermute | solution.py:428
  20.1 10.4 %copy-start.3 = (bf16[1024,256]{1,0:T(8,128)(2,1)S(1)}, bf16[1024,256]{1,0:T(8,128)(2,1)}, u32[]{:S(2)}) copy-start(bf16[1024,256]{1,0:T(8,128)(2,1)} %w_query.1) | copy-start | bytes 1572868
  20.1 10.3 %copy-start.4 = (bf16[1024,256]{1,0:T(8,128)(2,1)S(1)}, bf16[1024,256]{1,0:T(8,128)(2,1)}, u32[]{:S(2)}) copy-start(bf16[1024,256]{1,0:T(8,128)(2,1)} %w_key.1) | copy-start | bytes 1572868
  20.1 10.3 %copy-start.5 = (bf16[1024,256]{1,0:T(8,128)(2,1)S(1)}, bf16[1024,256]{1,0:T(8,128)(2,1)}, u32[]{:S(2)}) copy-start(bf16[1024,256]{1,0:T(8,128)(2,1)} %w_value.1) | copy-start | bytes 1572868
  23.0 21.2 %copy-start = (bf16[1024,1024]{1,0:T(8,128)(2,1)S(1)}, bf16[1024,1024]{1,0:T(8,128)(2,1)}, u32[]{:S(2)}) copy-start(bf16[1024,1024]{1,0:T(8,128)(2,1)} %unpatch.3) | copy-start | bytes 6291460
  31.1 5.8 %collective-permute-start.4 = (bf16[128,1024]{1,0:T(8,128)(2,1)S(1)}, bf16[128,1024]{1,0:T(8,128)(2,1)S(1)}, u32[]{:S(2)}, u32[]{:S(2)}) collective-permute-start(bf16[128,1024]{1,0:T(8,128)(2,1)S(1)} %get-tuple-element.24), channel_id=1, source_target_pairs={{0,1},{1,0},{2,3},{3,2},{4,5},{5,4},{6,7},{7,6},{8,9},{9,8},{10,11... | collective-permute-start | bytes 786440 | tf_op jit(solution)/shard_map/ppermute | solution.py:447
  32.6 8.8 %collective-permute-start.2 = (bf16[128,1024]{1,0:T(8,128)(2,1)S(1)}, bf16[128,1024]{1,0:T(8,128)(2,1)S(1)}, u32[]{:S(2)}, u32[]{:S(2)}) collective-permute-start(bf16[128,1024]{1,0:T(8,128)(2,1)S(1)} %get-tuple-element.23), channel_id=1, source_target_pairs={{0,3},{3,0},{1,2},{2,1},{4,7},{7,4},{5,6},{6,5},{8,11},{11,8},{9,1... | collective-permute-start | bytes 786440 | tf_op jit(solution)/shard_map/ppermute | solution.py:447
  36.9 7.3 %collective-permute-start.5 = (bf16[128,1024]{1,0:T(8,128)(2,1)S(1)}, bf16[128,1024]{1,0:T(8,128)(2,1)S(1)}, u32[]{:S(2)}, u32[]{:S(2)}) collective-permute-start(bf16[128,1024]{1,0:T(8,128)(2,1)S(1)} %add_convert_fusion.mine), channel_id=1, source_target_pairs={{0,3},{3,0},{1,2},{2,1},{4,7},{7,4},{5,6},{6,5},{8,11},{11,8},{9,1... | collective-permute-start | bytes 786440 | tf_op jit(solution)/shard_map/ppermute | solution.py:449
  41.5 5.3 %collective-permute-start.3 = (bf16[128,1024]{1,0:T(8,128)(2,1)S(1)}, bf16[128,1024]{1,0:T(8,128)(2,1)S(1)}, u32[]{:S(2)}, u32[]{:S(2)}) collective-permute-start(bf16[128,1024]{1,0:T(8,128)(2,1)S(1)} %add_convert_fusion.1.mine), channel_id=1, source_target_pairs={{0,1},{1,0},{2,3},{3,2},{4,5},{5,4},{6,7},{7,6},{8,9},{9,8},{10,11... | collective-permute-start | bytes 786440 | tf_op jit(solution)/shard_map/ppermute | solution.py:449

commit v7 on v6

--- a/solution.py
+++ b/solution.py
@@ -199,13 +199,11 @@
 
 def pack_kernel(keys, values, index_hbm, packed, index, held, sems, out_sems):
     arriving, leaving = [], []
-    for n in range(4):
-        source = (keys, values)[n // 2]
-        first = WINDOW + n % 2 * TILE
-        rows = slice(n * TILE, (n + 1) * TILE)
-        arriving.append(pltpu.make_async_copy(source.at[first : first + TILE, :], held.at[rows, :], sems.at[n]))
+    for n, source in enumerate((keys, values)):
+        rows = slice(n * WINDOW, (n + 1) * WINDOW)
+        arriving.append(pltpu.make_async_copy(source.at[WINDOW:, :], held.at[rows, :], sems.at[n]))
         leaving.append(pltpu.make_async_copy(held.at[rows, :], packed.at[rows, :], out_sems.at[n]))
-    places = pltpu.make_async_copy(index_hbm, index, sems.at[4])
+    places = pltpu.make_async_copy(index_hbm, index, sems.at[2])
     for copy in (places, *arriving):
         copy.start()
     places.wait()
@@ -214,7 +212,7 @@
     both = jnp.where(row == 0, slots[:, :TILE], slots[:, TILE:])
     held[2 * WINDOW :, :] = both.astype(BF16)
     slots_leaving = pltpu.make_async_copy(
-        held.at[2 * WINDOW :, :], packed.at[2 * WINDOW :, :], out_sems.at[4]
+        held.at[2 * WINDOW :, :], packed.at[2 * WINDOW :, :], out_sems.at[2]
     )
     slots_leaving.start()
     for copy, onward in zip(arriving, leaving):
@@ -394,8 +392,8 @@
         [
             pltpu.VMEM((1, 1024), jnp.int32),
             pltpu.VMEM((2 * WINDOW + 16, 256), BF16),
-            pltpu.SemaphoreType.DMA((5,)),
-            pltpu.SemaphoreType.DMA((5,)),
+            pltpu.SemaphoreType.DMA((3,)),
+            pltpu.SemaphoreType.DMA((3,)),
         ],
         flops=10**6,
         vmem=60,

time: 48.3 us -> 48.3 us (level)
  no operation moved by 1% of the time
where the time goes in v7:
time: 48.3 us; the launch traced here: 48.1 us
  Pallas kernels  18.4 us (38%)
  waiting for transfers between devices  15.1 us (31%)
  starting transfers between devices  14 us (29%)
    pallas_call x8, Pallas kernels, call(): pl.pallas_call(kernel, out_shape=[jax.ShapeDtypeStruct(*shape) for shape...  18.4 us
    ppermute x1, waiting for transfers between devices, on_device(): arrived = lax.ppermute(sent, 'seq', back)  7.39 us
    ppermute x1, starting transfers between devices, on_device(): packed = lax.ppermute(packed, 'seq', onward)  5.36 us
    ppermute x2, waiting for transfers between devices, on_device(): a_in, b_in = (lax.ppermute(a, 'mp', across), lax.ppermute(b, 'mp', around))  3.99 us
    ppermute x2, waiting for transfers between devices, on_device(): a_in, b_in = (lax.ppermute(a, 'mp', around), lax.ppermute(b, 'mp', across))  3.72 us
    ppermute x2, starting transfers between devices, on_device(): a_in, b_in = (lax.ppermute(a, 'mp', across), lax.ppermute(b, 'mp', around))  3.48 us
    ppermute x2, starting transfers between devices, on_device(): a_in, b_in = (lax.ppermute(a, 'mp', around), lax.ppermute(b, 'mp', across))  3.28 us
    ppermute x1, starting transfers between devices, on_device(): arrived = lax.ppermute(sent, 'seq', back)  1.92 us
  transfers between devices with their start and end apart: 6, of which 5 were waited for; matrix products, arithmetic and copies ran while one was open for 0% of the time, Pallas kernels for 22%

profile of v7, /device:TPU:103, one launch (start us, length us, event | category | flops | bytes accessed | tf_op | source)
XLA Modules:
  0.0 48.1 jit_solution(3030350911290969989)
XLA Ops:
  0.0 1.8 %shard_map.101 = bf16[1040,256]{1,0:T(8,128)(2,1)} custom-call(bf16[1024,256]{1,0:T(8,128)(2,1)} %keys.7, bf16[1024,256]{1,0:T(8,128)(2,1)} %values.7, s32[1,1024]{1,0:T(1,128)} %bitcast.1), custom_call_target="tpu_custom_call" | custom-call | flops 1000000 | tf_op jit(solution)/shard_map/pallas_call | solution.py:369
  1.8 0.0 copy-start.1
  1.8 0.0 copy-start.2
  1.8 0.0 copy-start.6
  1.9 0.0 copy-start.7
  1.9 5.4 %collective-permute-start = (bf16[1040,256]{1,0:T(8,128)(2,1)}, bf16[1040,256]{1,0:T(8,128)(2,1)S(1)}, u32[]{:S(2)}, u32[]{:S(2)}) collective-permute-start(bf16[1040,256]{1,0:T(8,128)(2,1)} %shard_map.101), channel_id=1, source_target_pairs={{0,4},{4,8},{8,12},{12,16},{16,20},{20,24},{24,28},{28,32},{32,36}... | collective-permute-start | bytes 1597448 | tf_op jit(solution)/shard_map/ppermute | solution.py:403
  7.2 2.9 %shard_map.100.grads = bf16[1024,256]{1,0:T(8,128)(2,1)S(1)} custom-call(bf16[1024,1024]{1,0:T(8,128)(2,1)} %d_output_hbm.1, bf16[256,1024]{1,0:T(8,128)(2,1)} %w_out_hbm.1), custom_call_target="tpu_custom_call" | custom-call | flops 8000000000 | tf_op jit(solution)/shard_map/pallas_call | solution.py:369
  10.1 0.0 copy-done.1
  10.1 0.0 copy-done.2
  10.1 0.0 copy-done.6
  10.1 0.0 copy-done.7
  10.2 3.6 %shard_map.102 = (f32[128,512]{1,0:T(8,128)S(1)}, f32[256,768]{1,0:T(8,128)S(1)}, f32[3072,256]{1,0:T(8,128)S(1)}, f32[3072,256]{1,0:T(8,128)S(1)}) custom-call(bf16[1024,256]{1,0:T(8,128)(2,1)S(1)} %shard_map.100.grads, bf16[1024,256]{1,0:T(8,128)(2,1)S(1)} %copy-done.7, bf16[1024,256]{1,0:T(8,128)(2,1)S(1)} %copy-done.1, bf16[1024,256]{1,0:T(8,128)(2,1)S(1)} %copy-done.2, ...), custom_call_target="tpu_custom_call" | custom-call | flops 8000000000 | tf_op jit(solution)/shard_map/pallas_call | solution.py:369
  13.8 0.0 collective-permute-done.packed
  13.8 4.3 %shard_map.103 = (bf16[640,256]{1,0:T(8,128)(2,1)S(1)}, bf16[512,256]{1,0:T(8,128)(2,1)S(1)}, bf16[512,256]{1,0:T(8,128)(2,1)S(1)}, bf16[256,512]{1,0:T(8,128)(2,1)S(1)}) custom-call(bf16[1024,256]{1,0:T(8,128)(2,1)S(1)} %shard_map.100.grads, bf16[1024,256]{1,0:T(8,128)(2,1)S(1)} %copy-done.7, bf16[1024,256]{1,0:T(8,128)(2,1)S(1)} %copy-done.1, ...), custom_call_target="tpu_custom_call" | custom-call | flops 8000000000 | tf_op jit(solution)/shard_map/pallas_call | solution.py:369
  18.1 1.9 %collective-permute-start.1 = (bf16[640,256]{1,0:T(8,128)(2,1)S(1)}, bf16[640,256]{1,0:T(8,128)(2,1)S(1)}, u32[]{:S(2)}, u32[]{:S(2)}) collective-permute-start(bf16[640,256]{1,0:T(8,128)(2,1)S(1)} %get-tuple-element.22), channel_id=1, source_target_pairs={{4,0},{8,4},{12,8},{16,12},{20,16},{24,20},{28,24},{32,28},{36,32}... | collective-permute-start | bytes 983048 | tf_op jit(solution)/shard_map/ppermute | solution.py:426
  20.0 0.0 copy-start.3
  20.0 0.0 copy-start.4
  20.1 0.0 copy-start.5
  20.1 2.9 %shard_map.104.x_in = f32[256,768]{1,0:T(8,128)S(1)} custom-call(bf16[1024,256]{1,0:T(8,128)(2,1)S(1)} %shard_map.100.grads, bf16[1024,256]{1,0:T(8,128)(2,1)S(1)} %copy-done.7, bf16[1024,256]{1,0:T(8,128)(2,1)S(1)} %copy-done.1, bf16[1024,256]{1,0:T(8,128)(2,1)S(1)} %copy-done.2, s32[1,1024]{1,0:T(1,128)S(1)} %bitcast.4, ...), custom_call_target="tpu_custom_call" | custom-call | flops 8000000000 | tf_op jit(solution)/shard_map/pallas_call | solution.py:369
  23.0 0.0 copy-start
  23.0 7.4 %collective-permute-done.1.arrived = bf16[640,256]{1,0:T(8,128)(2,1)S(1)} collective-permute-done((bf16[640,256]{1,0:T(8,128)(2,1)S(1)}, bf16[640,256]{1,0:T(8,128)(2,1)S(1)}, u32[]{:S(2)}, u32[]{:S(2)}) %collective-permute-start.1) | collective-permute-done | bytes 327712 | tf_op jit(solution)/shard_map/ppermute | solution.py:426
  30.4 0.0 copy-done.3
  30.4 0.0 copy-done.4
  30.4 0.0 copy-done.5
  30.4 0.6 %shard_map.105 = (bf16[128,1024]{1,0:T(8,128)(2,1)S(1)}, bf16[128,1024]{1,0:T(8,128)(2,1)S(1)}) custom-call(f32[256,768]{1,0:T(8,128)S(1)} %shard_map.104.x_in, bf16[640,256]{1,0:T(8,128)(2,1)S(1)} %collective-permute-done.1.arrived, bf16[1024,256]{1,0:T(8,128)(2,1)S(1)} %copy-done.3, bf16[1024,256]{1,0:T(8,128)(2,1)S(1)} %copy-done.4, ...), custom_call_target="tpu_custom_call" | custom-call | flops 400000000 | tf_op jit(solution)/shard_map/pallas_call | solution.py:369
  31.0 1.6 %collective-permute-start.4 = (bf16[128,1024]{1,0:T(8,128)(2,1)S(1)}, bf16[128,1024]{1,0:T(8,128)(2,1)S(1)}, u32[]{:S(2)}, u32[]{:S(2)}) collective-permute-start(bf16[128,1024]{1,0:T(8,128)(2,1)S(1)} %get-tuple-element.24), channel_id=1, source_target_pairs={{0,1},{1,0},{2,3},{3,2},{4,5},{5,4},{6,7},{7,6},{8,9},{9,8},{10,11... | collective-permute-start | bytes 786440 | tf_op jit(solution)/shard_map/ppermute | solution.py:445
  32.6 1.9 %collective-permute-start.2 = (bf16[128,1024]{1,0:T(8,128)(2,1)S(1)}, bf16[128,1024]{1,0:T(8,128)(2,1)S(1)}, u32[]{:S(2)}, u32[]{:S(2)}) collective-permute-start(bf16[128,1024]{1,0:T(8,128)(2,1)S(1)} %get-tuple-element.23), channel_id=1, source_target_pairs={{0,3},{3,0},{1,2},{2,1},{4,7},{7,4},{5,6},{6,5},{8,11},{11,8},{9,1... | collective-permute-start | bytes 786440 | tf_op jit(solution)/shard_map/ppermute | solution.py:445
  34.5 2.3 %collective-permute-done.4 = bf16[128,1024]{1,0:T(8,128)(2,1)S(1)} collective-permute-done((bf16[128,1024]{1,0:T(8,128)(2,1)S(1)}, bf16[128,1024]{1,0:T(8,128)(2,1)S(1)}, u32[]{:S(2)}, u32[]{:S(2)}) %collective-permute-start.4) | collective-permute-done | bytes 262176 | tf_op jit(solution)/shard_map/ppermute | solution.py:445
  36.8 0.1 add_convert_fusion.mine
  36.9 2.8 %collective-permute-start.5 = (bf16[128,1024]{1,0:T(8,128)(2,1)S(1)}, bf16[128,1024]{1,0:T(8,128)(2,1)S(1)}, u32[]{:S(2)}, u32[]{:S(2)}) collective-permute-start(bf16[128,1024]{1,0:T(8,128)(2,1)S(1)} %add_convert_fusion.mine), channel_id=1, source_target_pairs={{0,3},{3,0},{1,2},{2,1},{4,7},{7,4},{5,6},{6,5},{8,11},{11,8},{9,1... | collective-permute-start | bytes 786440 | tf_op jit(solution)/shard_map/ppermute | solution.py:447
  39.7 1.7 %collective-permute-done.2 = bf16[128,1024]{1,0:T(8,128)(2,1)S(1)} collective-permute-done((bf16[128,1024]{1,0:T(8,128)(2,1)S(1)}, bf16[128,1024]{1,0:T(8,128)(2,1)S(1)}, u32[]{:S(2)}, u32[]{:S(2)}) %collective-permute-start.2) | collective-permute-done | bytes 262176 | tf_op jit(solution)/shard_map/ppermute | solution.py:445
  41.4 0.1 add_convert_fusion.1.mine
  41.5 0.4 collective-permute-start.3
  41.9 2.3 %collective-permute-done.5.other = bf16[128,1024]{1,0:T(8,128)(2,1)S(1)} collective-permute-done((bf16[128,1024]{1,0:T(8,128)(2,1)S(1)}, bf16[128,1024]{1,0:T(8,128)(2,1)S(1)}, u32[]{:S(2)}, u32[]{:S(2)}) %collective-permute-start.5) | collective-permute-done | bytes 262176 | tf_op jit(solution)/shard_map/ppermute | solution.py:447
  44.2 0.0 copy-done
  44.2 1.1 %shard_map.106.refs_0_ = bf16[256,1024]{1,0:T(8,128)(2,1)} custom-call(bf16[128,1024]{1,0:T(8,128)(2,1)S(1)} %add_convert_fusion.mine, bf16[128,1024]{1,0:T(8,128)(2,1)S(1)} %collective-permute-done.5.other, bf16[1024,1024]{1,0:T(8,128)(2,1)S(1)} %copy-done), custom_call_target="tpu_custom_call" | custom-call | flops 300000000 | tf_op jit(solution)/shard_map/pallas_call | solution.py:369
  45.4 1.4 %collective-permute-done.3.other = bf16[128,1024]{1,0:T(8,128)(2,1)S(1)} collective-permute-done((bf16[128,1024]{1,0:T(8,128)(2,1)S(1)}, bf16[128,1024]{1,0:T(8,128)(2,1)S(1)}, u32[]{:S(2)}, u32[]{:S(2)}) %collective-permute-start.3) | collective-permute-done | bytes 262176 | tf_op jit(solution)/shard_map/ppermute | solution.py:447
  46.8 1.1 %shard_map.107 = bf16[256,1024]{1,0:T(8,128)(2,1)} custom-call(bf16[128,1024]{1,0:T(8,128)(2,1)S(1)} %add_convert_fusion.1.mine, bf16[128,1024]{1,0:T(8,128)(2,1)S(1)} %collective-permute-done.3.other, bf16[1024,1024]{1,0:T(8,128)(2,1)S(1)} %copy-done, bf16[256,1024]{1,0:T(8,128)(2,1)} %shard_map.106.refs_0_), custom_call_target="tpu_custom_call", output_to_operand_aliasing={{}: (3, {})} | custom-call | flops 300000000 | tf_op jit(solution)/shard_map/pallas_call | solution.py:369
Async XLA Ops:
  1.8 8.3 %copy-start.1 = (bf16[1024,256]{1,0:T(8,128)(2,1)S(1)}, bf16[1024,256]{1,0:T(8,128)(2,1)}, u32[]{:S(2)}) copy-start(bf16[1024,256]{1,0:T(8,128)(2,1)} %keys.7) | copy-start | bytes 1572868
  1.8 8.3 %copy-start.2 = (bf16[1024,256]{1,0:T(8,128)(2,1)S(1)}, bf16[1024,256]{1,0:T(8,128)(2,1)}, u32[]{:S(2)}) copy-start(bf16[1024,256]{1,0:T(8,128)(2,1)} %values.7) | copy-start | bytes 1572868
  1.8 8.3 %copy-start.6 = (s32[1024]{0:T(1024)S(1)}, s32[1024]{0:T(1024)}, u32[]{:S(2)}) copy-start(s32[1024]{0:T(1024)} %param.18) | copy-start | bytes 12292
  1.9 8.3 %copy-start.7 = (bf16[1024,256]{1,0:T(8,128)(2,1)S(1)}, bf16[1024,256]{1,0:T(8,128)(2,1)}, u32[]{:S(2)}) copy-start(bf16[1024,256]{1,0:T(8,128)(2,1)} %queries.5) | copy-start | bytes 1572868
  1.9 11.9 %collective-permute-start = (bf16[1040,256]{1,0:T(8,128)(2,1)}, bf16[1040,256]{1,0:T(8,128)(2,1)S(1)}, u32[]{:S(2)}, u32[]{:S(2)}) collective-permute-start(bf16[1040,256]{1,0:T(8,128)(2,1)} %shard_map.101), channel_id=1, source_target_pairs={{0,4},{4,8},{8,12},{12,16},{16,20},{20,24},{24,28},{28,32},{32,36}... | collective-permute-start | bytes 1597448 | tf_op jit(solution)/shard_map/ppermute | solution.py:403
  18.1 12.3 %collective-permute-start.1 = (bf16[640,256]{1,0:T(8,128)(2,1)S(1)}, bf16[640,256]{1,0:T(8,128)(2,1)S(1)}, u32[]{:S(2)}, u32[]{:S(2)}) collective-permute-start(bf16[640,256]{1,0:T(8,128)(2,1)S(1)} %get-tuple-element.22), channel_id=1, source_target_pairs={{4,0},{8,4},{12,8},{16,12},{20,16},{24,20},{28,24},{32,28},{36,32}... | collective-permute-start | bytes 983048 | tf_op jit(solution)/shard_map/ppermute | solution.py:426
  20.0 10.4 %copy-start.3 = (bf16[1024,256]{1,0:T(8,128)(2,1)S(1)}, bf16[1024,256]{1,0:T(8,128)(2,1)}, u32[]{:S(2)}) copy-start(bf16[1024,256]{1,0:T(8,128)(2,1)} %w_query.1) | copy-start | bytes 1572868
  20.0 10.3 %copy-start.4 = (bf16[1024,256]{1,0:T(8,128)(2,1)S(1)}, bf16[1024,256]{1,0:T(8,128)(2,1)}, u32[]{:S(2)}) copy-start(bf16[1024,256]{1,0:T(8,128)(2,1)} %w_key.1) | copy-start | bytes 1572868
  20.1 10.3 %copy-start.5 = (bf16[1024,256]{1,0:T(8,128)(2,1)S(1)}, bf16[1024,256]{1,0:T(8,128)(2,1)}, u32[]{:S(2)}) copy-start(bf16[1024,256]{1,0:T(8,128)(2,1)} %w_value.1) | copy-start | bytes 1572868
  23.0 21.2 %copy-start = (bf16[1024,1024]{1,0:T(8,128)(2,1)S(1)}, bf16[1024,1024]{1,0:T(8,128)(2,1)}, u32[]{:S(2)}) copy-start(bf16[1024,1024]{1,0:T(8,128)(2,1)} %unpatch.3) | copy-start | bytes 6291460
  31.0 5.8 %collective-permute-start.4 = (bf16[128,1024]{1,0:T(8,128)(2,1)S(1)}, bf16[128,1024]{1,0:T(8,128)(2,1)S(1)}, u32[]{:S(2)}, u32[]{:S(2)}) collective-permute-start(bf16[128,1024]{1,0:T(8,128)(2,1)S(1)} %get-tuple-element.24), channel_id=1, source_target_pairs={{0,1},{1,0},{2,3},{3,2},{4,5},{5,4},{6,7},{7,6},{8,9},{9,8},{10,11... | collective-permute-start | bytes 786440 | tf_op jit(solution)/shard_map/ppermute | solution.py:445
  32.6 8.8 %collective-permute-start.2 = (bf16[128,1024]{1,0:T(8,128)(2,1)S(1)}, bf16[128,1024]{1,0:T(8,128)(2,1)S(1)}, u32[]{:S(2)}, u32[]{:S(2)}) collective-permute-start(bf16[128,1024]{1,0:T(8,128)(2,1)S(1)} %get-tuple-element.23), channel_id=1, source_target_pairs={{0,3},{3,0},{1,2},{2,1},{4,7},{7,4},{5,6},{6,5},{8,11},{11,8},{9,1... | collective-permute-start | bytes 786440 | tf_op jit(solution)/shard_map/ppermute | solution.py:445
  36.9 7.3 %collective-permute-start.5 = (bf16[128,1024]{1,0:T(8,128)(2,1)S(1)}, bf16[128,1024]{1,0:T(8,128)(2,1)S(1)}, u32[]{:S(2)}, u32[]{:S(2)}) collective-permute-start(bf16[128,1024]{1,0:T(8,128)(2,1)S(1)} %add_convert_fusion.mine), channel_id=1, source_target_pairs={{0,3},{3,0},{1,2},{2,1},{4,7},{7,4},{5,6},{6,5},{8,11},{11,8},{9,1... | collective-permute-start | bytes 786440 | tf_op jit(solution)/shard_map/ppermute | solution.py:447
  41.5 5.3 %collective-permute-start.3 = (bf16[128,1024]{1,0:T(8,128)(2,1)S(1)}, bf16[128,1024]{1,0:T(8,128)(2,1)S(1)}, u32[]{:S(2)}, u32[]{:S(2)}) collective-permute-start(bf16[128,1024]{1,0:T(8,128)(2,1)S(1)} %add_convert_fusion.1.mine), channel_id=1, source_target_pairs={{0,1},{1,0},{2,3},{3,2},{4,5},{5,4},{6,7},{7,6},{8,9},{9,8},{10,11... | collective-permute-start | bytes 786440 | tf_op jit(solution)/shard_map/ppermute | solution.py:447
